TPU v7x, 32 devices: a whole 2x2x4 slice. The times are simulated.
32 devices in a mesh: fsdp: 8 (over z, y), seq: 4 (over x, core).
Axes of the slice: x: 2, y: 2, z: 4, core: 2. Of those that a mesh axis runs over, the one named last changes fastest.
Arguments:
- tokens: bfloat16 [16384, 1152], P(('fsdp', 'seq')), may hold values from -6 to 6
- cotangent: bfloat16 [16384, 1152], P(('fsdp', 'seq')), may hold values from -6 to 6
- positions: int32 [16384], P('fsdp'), may hold values from 0 to 1535, as said below
- segment: int32 [16384], P('fsdp'), may hold values from 0 to 2, as said below
- query_weight: float32 [1152, 1024], P('fsdp'), may hold values from -0.1875 to 0.1875
- key_weight: float32 [1152, 256], P('fsdp'), may hold values from -0.1875 to 0.1875
- value_weight: float32 [1152, 256], P('fsdp'), may hold values from -0.1875 to 0.1875
- out_weight: float32 [1024, 1152], P('fsdp'), may hold values from -0.1875 to 0.1875
- gate_weight: float32 [1152, 6912], P('fsdp'), may hold values from -0.1875 to 0.1875
- up_weight: float32 [1152, 6912], P('fsdp'), may hold values from -0.1875 to 0.1875
- down_weight: float32 [6912, 1152], P('fsdp'), may hold values from -0.078125 to 0.078125
- gain_input: float32 [1152], P('fsdp'), may hold values from 0.25 to 1.75
- gain_query: float32 [256], P('fsdp'), may hold values from 0.25 to 1.75
- gain_key: float32 [256], P('fsdp'), may hold values from 0.25 to 1.75
- gain_mixed: float32 [1152], P('fsdp'), may hold values from 0.25 to 1.75
- gain_feed: float32 [1152], P('fsdp'), may hold values from 0.25 to 1.75
- gain_final: float32 [1152], P('fsdp'), may hold values from 0.25 to 1.75
Outputs:
- output: bfloat16 [16384, 1152], P(('fsdp', 'seq'))
- grad_tokens: float32 [16384, 1152], P(('fsdp', 'seq'))
- grad_query: float32 [1152, 1024], P('fsdp')
- grad_key: float32 [1152, 256], P('fsdp')
- grad_value: float32 [1152, 256], P('fsdp')
- grad_out: float32 [1024, 1152], P('fsdp')
- grad_gate: float32 [1152, 6912], P('fsdp')
- grad_up: float32 [1152, 6912], P('fsdp')
- grad_down: float32 [6912, 1152], P('fsdp')
- grad_gain_input: float32 [1152], P('fsdp')
- grad_gain_query: float32 [256], P('fsdp')
- grad_gain_key: float32 [256], P('fsdp')
- grad_gain_mixed: float32 [1152], P('fsdp')
- grad_gain_feed: float32 [1152], P('fsdp')
- grad_gain_final: float32 [1152], P('fsdp')
Inputs may be any that keep to these rules, and one draw needn't show every extreme that they name: `segment`: in each group of 2048 consecutive entries, 1024 are 0 and 512 are c for each c from 1 to 2; each block of 512 entries holds the same number of each value. In each group, the tokens of segment 0 carry the positions 0 to 1023 once each, and the tokens of each continuation the positions 1024 to 1535 once each.
All inputs are finite; a program needn't handle non-finite values.
Results may differ from a plain program's by a relative error of at most 0.018.
The roundings to bfloat16 on the way count: a program that leaves them out, or rounds other values in their place, can miss the bound.
Values may be sent and summed in bfloat16 or wider, within the bound.
No kernel may reach another device: no remote copies, remote signals or barrier semaphores. Data moves between devices by JAX's collectives and lax.ppermute only.
A program may use at most 320 MiB of HBM per device.

v0:
```python
from functools import partial

import jax
import jax.numpy as jnp
from jax import lax
from jax.sharding import PartitionSpec as P

epsilon = 1e-06


def rms_scale(values, gain):
    return values * lax.rsqrt(jnp.mean(values * values, axis=-1, keepdims=True) + epsilon) * gain


def rotate(values, cosine, sine):
    half_width = values.shape[-1] // 2
    first_half = values[..., :half_width]
    second_half = values[..., half_width:]
    return jnp.concatenate(
        [first_half * cosine - second_half * sine, second_half * cosine + first_half * sine],
        axis=-1,
    )


def rope_tables(places, width):
    half_width = width // 2
    inverse = 1.0 / 1000000.0 ** (jnp.arange(half_width, dtype=jnp.float32) * 2.0 / width)
    angles = places.astype(jnp.float32)[:, None] * inverse[None, :]
    return (jnp.cos(angles), jnp.sin(angles))


def allowed_pairs(query_pos, query_seg, key_pos, key_seg):
    causal = key_pos[None, :] <= query_pos[:, None]
    related = (key_seg[None, :] == query_seg[:, None]) | (key_seg[None, :] == 0)
    return causal & related


def mult(left, right):
    return jnp.dot(left, right, preferred_element_type=jnp.float32)


def inner_rows(left, right):
    return lax.dot_general(
        left, right, (((0,), (0,)), ((), ())), preferred_element_type=jnp.float32
    )


def outer_cols(left, right):
    return lax.dot_general(
        left, right, (((1,), (1,)), ((), ())), preferred_element_type=jnp.float32
    )


def to_half(values):
    return values.astype(jnp.bfloat16)


def gated(gate_in, up_in):
    return jax.nn.gelu(gate_in, approximate=True) * up_in


def head_norms(query_raw, key_raw, gain_q, gain_k, cosine, sine):
    tok_rows = query_raw.shape[0]
    head_width = key_raw.shape[1]
    query_heads = rms_scale(query_raw.reshape(tok_rows, -1, head_width), gain_q)
    query_turned = rotate(query_heads, cosine[:, None, :], sine[:, None, :]).reshape(tok_rows, -1)
    key_turned = rotate(rms_scale(key_raw, gain_k), cosine, sine)
    return (query_turned, key_turned)


def body(
    tokens,
    cotangent,
    positions,
    segment,
    query_weight,
    key_weight,
    value_weight,
    out_weight,
    gate_weight,
    up_weight,
    down_weight,
    gain_input,
    gain_query,
    gain_key,
    gain_mixed,
    gain_feed,
    gain_final,
):
    attn_parts = (
        lax.all_gather(to_half(query_weight), "fsdp", axis=0, tiled=True),
        lax.all_gather(to_half(key_weight), "fsdp", axis=0, tiled=True),
        lax.all_gather(to_half(value_weight), "fsdp", axis=0, tiled=True),
        lax.all_gather(to_half(out_weight), "fsdp", axis=0, tiled=True),
        lax.all_gather(to_half(gain_input), "fsdp", axis=0, tiled=True),
        lax.all_gather(to_half(gain_query), "fsdp", axis=0, tiled=True),
        lax.all_gather(to_half(gain_key), "fsdp", axis=0, tiled=True),
        lax.all_gather(to_half(gain_mixed), "fsdp", axis=0, tiled=True),
    )
    feed_parts = (
        lax.all_gather(to_half(gate_weight), "fsdp", axis=0, tiled=True),
        lax.all_gather(to_half(up_weight), "fsdp", axis=0, tiled=True),
        lax.all_gather(to_half(down_weight), "fsdp", axis=0, tiled=True),
        lax.all_gather(to_half(gain_feed), "fsdp", axis=0, tiled=True),
        lax.all_gather(to_half(gain_final), "fsdp", axis=0, tiled=True),
    )
    w_query, w_key, w_value, w_out = (attn_parts[0], attn_parts[1], attn_parts[2], attn_parts[3])
    g_input = attn_parts[4].astype(jnp.float32)
    g_query = attn_parts[5].astype(jnp.float32)
    g_key = attn_parts[6].astype(jnp.float32)
    g_mixed = attn_parts[7].astype(jnp.float32)
    w_gate, w_up, w_down = (feed_parts[0], feed_parts[1], feed_parts[2])
    g_feed = feed_parts[3].astype(jnp.float32)
    g_final = feed_parts[4].astype(jnp.float32)
    tok_rows = tokens.shape[0]
    group_len = positions.shape[0]
    head_count = lax.axis_size("seq")
    head_width = w_key.shape[1]
    scale_factor = head_width ** (-0.5)
    block_len = min(512, group_len)
    block_count = group_len // block_len
    offset = lax.axis_index("seq") * tok_rows
    own_pos = lax.dynamic_slice_in_dim(positions, offset, tok_rows)
    cosine, sine = rope_tables(own_pos, head_width)
    inputs32 = tokens.astype(jnp.float32)
    normed, input_back = jax.vjp(rms_scale, inputs32, g_input)
    normed16 = to_half(normed)
    query_raw = mult(normed16, w_query)
    key_raw = mult(normed16, w_key)
    value16 = to_half(mult(normed16, w_value))
    (query_turned, key_turned), heads_norm_back = jax.vjp(
        partial(head_norms, cosine=cosine, sine=sine), query_raw, key_raw, g_query, g_key
    )
    query16 = to_half(query_turned)
    key16 = to_half(key_turned)
    query_all = lax.all_to_all(
        query16.reshape(tok_rows, head_count, head_width),
        "seq",
        split_axis=1,
        concat_axis=0,
        tiled=True,
    ).reshape(group_len, head_width)
    key_all, value_all = (
        lax.all_gather(key16, "seq", axis=0, tiled=True),
        lax.all_gather(value16, "seq", axis=0, tiled=True),
    )

    def block_scores(block_index):
        start = block_index * block_len
        query_block = lax.dynamic_slice_in_dim(query_all, start, block_len)
        pos_block = lax.dynamic_slice_in_dim(positions, start, block_len)
        seg_block = lax.dynamic_slice_in_dim(segment, start, block_len)
        scores = scale_factor * outer_cols(query_block, key_all)
        scores = jnp.where(allowed_pairs(pos_block, seg_block, positions, segment), scores, -1e30)
        return (query_block, scores)

    def forward_block(block_index):
        query_block, scores = block_scores(block_index)
        top = jnp.max(scores, axis=1, keepdims=True)
        expd = jnp.exp(scores - top)
        total = jnp.sum(expd, axis=1, keepdims=True)
        weights = expd / total
        attended = to_half(mult(to_half(weights), value_all))
        return (attended, top[:, 0] + jnp.log(total[:, 0]))

    attended, log_totals = lax.map(forward_block, jnp.arange(block_count))
    attended = attended.reshape(group_len, head_width)
    log_totals = log_totals.reshape(group_len)
    heads16 = lax.all_to_all(
        attended.reshape(group_len, 1, head_width), "seq", split_axis=0, concat_axis=1, tiled=True
    ).reshape(tok_rows, head_count * head_width)
    attn = mult(heads16, w_out)
    post_attn, mixed_back = jax.vjp(rms_scale, attn, g_mixed)
    mixed = inputs32 + post_attn
    fed, feed_back = jax.vjp(rms_scale, mixed, g_feed)
    fed16 = to_half(fed)
    gate = mult(fed16, w_gate)
    upper = mult(fed16, w_up)
    act, act_back = jax.vjp(gated, gate, upper)
    act16 = to_half(act)
    ffo = mult(act16, w_down)
    post_feed, final_back = jax.vjp(rms_scale, ffo, g_final)
    output = to_half(mixed + post_feed)
    feed_again = (
        lax.all_gather(to_half(gate_weight), "fsdp", axis=0, tiled=True),
        lax.all_gather(to_half(up_weight), "fsdp", axis=0, tiled=True),
        lax.all_gather(to_half(down_weight), "fsdp", axis=0, tiled=True),
    )
    back_gate, back_up, back_down = (feed_again[0], feed_again[1], feed_again[2])
    grad_out_rows = cotangent.astype(jnp.float32)
    grad_ffo, grad_gain_final = final_back(grad_out_rows)
    grad_ffo16 = to_half(grad_ffo)
    grad_down = inner_rows(act16, grad_ffo16)
    grad_act = outer_cols(grad_ffo16, back_down)
    grad_gate_in, grad_up_in = act_back(grad_act)
    grad_gate16 = to_half(grad_gate_in)
    grad_up16 = to_half(grad_up_in)
    grad_gate = inner_rows(fed16, grad_gate16)
    grad_up = inner_rows(fed16, grad_up16)
    grad_fed = outer_cols(grad_gate16, back_gate) + outer_cols(grad_up16, back_up)
    grad_mixed_part, grad_gain_feed = feed_back(grad_fed)
    grad_mixed = grad_out_rows + grad_mixed_part
    attn_again = (
        lax.all_gather(to_half(query_weight), "fsdp", axis=0, tiled=True),
        lax.all_gather(to_half(key_weight), "fsdp", axis=0, tiled=True),
        lax.all_gather(to_half(value_weight), "fsdp", axis=0, tiled=True),
        lax.all_gather(to_half(out_weight), "fsdp", axis=0, tiled=True),
    )
    back_query, back_key, back_value, back_out = (
        attn_again[0],
        attn_again[1],
        attn_again[2],
        attn_again[3],
    )
    grad_attn, grad_gain_mixed = mixed_back(grad_mixed)
    grad_attn16 = to_half(grad_attn)
    grad_out = inner_rows(heads16, grad_attn16)
    grad_heads16 = to_half(outer_cols(grad_attn16, back_out))
    grad_heads_all = lax.all_to_all(
        grad_heads16.reshape(tok_rows, head_count, head_width),
        "seq",
        split_axis=1,
        concat_axis=0,
        tiled=True,
    ).reshape(group_len, head_width)

    def backward_block(sums, block_index):
        key_sum, value_sum = sums
        start = block_index * block_len
        query_block, scores = block_scores(block_index)
        lse_block = lax.dynamic_slice_in_dim(log_totals, start, block_len)
        weights = jnp.exp(scores - lse_block[:, None])
        weights16 = to_half(weights)
        grad_block = lax.dynamic_slice_in_dim(grad_heads_all, start, block_len)
        grad_weights = outer_cols(grad_block, value_all)
        centre = jnp.sum(weights * grad_weights, axis=1, keepdims=True)
        grad_scores16 = to_half(weights * (grad_weights - centre))
        query_grad = to_half(scale_factor * mult(grad_scores16, key_all))
        key_sum = key_sum + scale_factor * inner_rows(grad_scores16, query_block)
        value_sum = value_sum + inner_rows(weights16, grad_block)
        return ((key_sum, value_sum), query_grad)

    empty = jnp.zeros((group_len, head_width), jnp.float32)
    (key_grad_all, value_grad_all), query_grads = lax.scan(
        backward_block, (empty, empty), jnp.arange(block_count)
    )
    query_grads = query_grads.reshape(group_len, head_width)
    grad_query16 = lax.all_to_all(
        query_grads.reshape(group_len, 1, head_width),
        "seq",
        split_axis=0,
        concat_axis=1,
        tiled=True,
    ).reshape(tok_rows, head_count * head_width)
    key_grad_own, value_grad_own = (
        lax.psum_scatter(key_grad_all, "seq", scatter_dimension=0, tiled=True),
        lax.psum_scatter(value_grad_all, "seq", scatter_dimension=0, tiled=True),
    )
    key_grad16 = to_half(key_grad_own)
    value_grad16 = to_half(value_grad_own)
    grad_query_raw, grad_key_raw, grad_gain_query, grad_gain_key = heads_norm_back(
        (grad_query16.astype(jnp.float32), key_grad16.astype(jnp.float32))
    )
    grad_query_raw16 = to_half(grad_query_raw)
    grad_key_raw16 = to_half(grad_key_raw)
    grad_query = inner_rows(normed16, grad_query_raw16)
    grad_key = inner_rows(normed16, grad_key_raw16)
    grad_value = inner_rows(normed16, value_grad16)
    grad_normed = (
        outer_cols(grad_query_raw16, back_query)
        + outer_cols(grad_key_raw16, back_key)
        + outer_cols(value_grad16, back_value)
    )
    grad_input_part, grad_gain_input = input_back(grad_normed)
    grad_tokens = grad_mixed + grad_input_part
    shares = (
        lax.psum_scatter(grad_query, "fsdp", scatter_dimension=0, tiled=True),
        lax.psum_scatter(grad_key, "fsdp", scatter_dimension=0, tiled=True),
        lax.psum_scatter(grad_value, "fsdp", scatter_dimension=0, tiled=True),
        lax.psum_scatter(grad_out, "fsdp", scatter_dimension=0, tiled=True),
        lax.psum_scatter(grad_gate, "fsdp", scatter_dimension=0, tiled=True),
        lax.psum_scatter(grad_up, "fsdp", scatter_dimension=0, tiled=True),
        lax.psum_scatter(grad_down, "fsdp", scatter_dimension=0, tiled=True),
        lax.psum_scatter(grad_gain_input, "fsdp", scatter_dimension=0, tiled=True),
        lax.psum_scatter(grad_gain_query, "fsdp", scatter_dimension=0, tiled=True),
        lax.psum_scatter(grad_gain_key, "fsdp", scatter_dimension=0, tiled=True),
        lax.psum_scatter(grad_gain_mixed, "fsdp", scatter_dimension=0, tiled=True),
        lax.psum_scatter(grad_gain_feed, "fsdp", scatter_dimension=0, tiled=True),
        lax.psum_scatter(grad_gain_final, "fsdp", scatter_dimension=0, tiled=True),
    )
    totals = lax.psum(
        (
            shares[0],
            shares[1],
            shares[2],
            shares[3],
            shares[4],
            shares[5],
            shares[6],
            shares[7],
            shares[8],
            shares[9],
            shares[10],
            shares[11],
            shares[12],
        ),
        "seq",
    )
    return (
        output,
        grad_tokens,
        totals[0],
        totals[1],
        totals[2],
        totals[3],
        totals[4],
        totals[5],
        totals[6],
        totals[7],
        totals[8],
        totals[9],
        totals[10],
        totals[11],
        totals[12],
    )


def solution(mesh):
    return jax.shard_map(
        body,
        mesh=mesh,
        in_specs=(
            P(("fsdp", "seq"), None),
            P(("fsdp", "seq"), None),
            P("fsdp"),
            P("fsdp"),
            P("fsdp", None),
            P("fsdp", None),
            P("fsdp", None),
            P("fsdp", None),
            P("fsdp", None),
            P("fsdp", None),
            P("fsdp", None),
            P("fsdp"),
            P("fsdp"),
            P("fsdp"),
            P("fsdp"),
            P("fsdp"),
            P("fsdp"),
        ),
        out_specs=(
            P(("fsdp", "seq"), None),
            P(("fsdp", "seq"), None),
            P("fsdp", None),
            P("fsdp", None),
            P("fsdp", None),
            P("fsdp", None),
            P("fsdp", None),
            P("fsdp", None),
            P("fsdp", None),
            P("fsdp"),
            P("fsdp"),
            P("fsdp"),
            P("fsdp"),
            P("fsdp"),
            P("fsdp"),
        ),
        check_vma=False,
    )
```

profile of v0, /device:TPU:9, one launch (start us, length us, event | category | flops | bytes accessed | tf_op | source)
XLA Modules:
  0.0 3238.6 jit_solution(15013341498130785104)
XLA Ops:
  17.2 28.3 all-reduce.19
  48.9 26.2 all_gather.55
  78.7 25.1 all_gather.58
  106.8 3.6 convert_element_type.171
  110.5 3.6 convert_element_type.172
  130.4 25.4 all-to-all-start
  158.1 11.4 all-to-all-done
  169.5 31.4 while.27
  204.5 5.4 all-to-all-start.1
  210.6 13.1 all-to-all-done.1
  228.9 3.7 multiply_reduce_fusion.7
  234.9 177.7 %all-gather.16.cloned.1.call-done = bf16[1152,6912]{1,0:T(8,128)(2,1)} async-done(((bf16[144,6912]{1,0:T(8,128)(2,1)}), bf16[1152,6912]{1,0:T(8,128)(2,1)}) %all-gather.16.cloned.1.call-update) | async-done | bytes 15925264 | tf_op jit(solution)/shard_map/all_gather | solution.py:101
  412.6 16.2 fusion.80
  428.8 201.8 %all-gather.18.cloned.1.call-done = bf16[1152,6912]{1,0:T(8,128)(2,1)} async-done(((bf16[144,6912]{1,0:T(8,128)(2,1)}), bf16[1152,6912]{1,0:T(8,128)(2,1)}) %all-gather.18.cloned.1.call-update) | async-done | bytes 15925264 | tf_op jit(solution)/shard_map/all_gather | solution.py:102
  630.7 21.2 multiply_convert_fusion.2
  651.9 196.4 %all-gather.20.cloned.1.call-done = bf16[6912,1152]{1,0:T(8,128)(2,1)} async-done(((bf16[864,1152]{1,0:T(8,128)(2,1)}), bf16[6912,1152]{1,0:T(8,128)(2,1)}) %all-gather.20.cloned.1.call-update) | async-done | bytes 15925264 | tf_op jit(solution)/shard_map/all_gather | solution.py:103
  848.3 14.6 multiply_reduce_fusion.5
  866.6 27.9 multiply_convert_fusion.1
  894.6 14.8 fusion.81
  909.5 16.7 multiply_reduce_fusion.1
  933.3 5.3 all-to-all-start.2
  938.6 13.7 all-to-all-done.2
  953.4 75.1 %while.28 = (s32[]{:T(128)}, f32[2048,256]{1,0:T(8,128)}, f32[2048,256]{1,0:T(8,128)}, bf16[4,512,256]{2,1,0:T(8,128)(2,1)}, s32[2048]{0:T(1024)S(1)}, /*index=5...) while((s32[]{:T(128)}, f32[2048,256]{1,0:T(8,128)}, ...), condition=%wide.region_15.16_spmd.clone, body=%wide.region_13.15_spmd.clone.sunk | while | flops 2700871168 | bytes 94685560 | solution.py:244
  956.8 3.6 multiply_reduce_fusion.14
  974.9 3.6 multiply_reduce_fusion.14
  980.6 3.9 fusion.160
  993.8 3.6 multiply_reduce_fusion.14
  999.5 3.9 fusion.160
  1018.4 3.9 fusion.160
  1032.3 30.1 reduce-scatter.10.cloned.1.call-done
  1068.0 29.1 reduce-scatter.12.cloned.1.call-done
  1099.8 3.6 fusion.83
  1106.5 17.7 all_to_all.54
  1132.2 3.7 fusion.71
  1137.2 17.0 fusion.84
  1154.2 16.9 fusion.85
  1172.4 19.2 fusion.86
  1191.7 38.3 %reduce-scatter.18.cloned.1.call-done = f32[144,256]{1,0:T(8,128)} async-done(((f32[1152,256]{1,0:T(8,128)}), f32[144,256]{1,0:T(8,128)}) %reduce-scatter.18.cloned.1.call-update) | async-done | bytes 147472 | tf_op jit(solution)/shard_map/reduce_scatter | solution.py:279
  1230.0 100.0 %reduce-scatter.20.cloned.1.call-done = f32[128,1152]{1,0:T(8,128)} async-done(((f32[1024,1152]{1,0:T(8,128)}), f32[128,1152]{1,0:T(8,128)}) %reduce-scatter.20.cloned.1.call-update) | async-done | bytes 589840 | tf_op jit(solution)/shard_map/reduce_scatter | solution.py:280
  1330.1 98.8 %reduce-scatter.14.cloned.1.call-done = f32[144,1024]{1,0:T(8,128)} async-done(((f32[1152,1024]{1,0:T(8,128)}), f32[144,1024]{1,0:T(8,128)}) %reduce-scatter.14.cloned.1.call-update) | async-done | bytes 589840 | tf_op jit(solution)/shard_map/reduce_scatter | solution.py:277
  1428.9 514.5 %reduce-scatter.22.cloned.1.call-done = f32[144,6912]{1,0:T(8,128)} async-done(((f32[1152,6912]{1,0:T(8,128)}), f32[144,6912]{1,0:T(8,128)}) %reduce-scatter.22.cloned.1.call-update) | async-done | bytes 3981328 | tf_op jit(solution)/shard_map/reduce_scatter | solution.py:281
  1943.4 515.5 %reduce-scatter.24.cloned.1.call-done = f32[144,6912]{1,0:T(8,128)} async-done(((f32[1152,6912]{1,0:T(8,128)}), f32[144,6912]{1,0:T(8,128)}) %reduce-scatter.24.cloned.1.call-update) | async-done | bytes 3981328 | tf_op jit(solution)/shard_map/reduce_scatter | solution.py:282
  2458.8 515.3 %reduce-scatter.26.cloned.1.call-done = f32[864,1152]{1,0:T(8,128)} async-done(((f32[6912,1152]{1,0:T(8,128)}), f32[864,1152]{1,0:T(8,128)}) %reduce-scatter.26.cloned.1.call-update) | async-done | bytes 3981328 | tf_op jit(solution)/shard_map/reduce_scatter | solution.py:283
  2983.0 28.5 all-reduce.16
  3018.2 13.4 all-reduce.17
  3032.4 3.7 fusion.38
  3036.1 178.6 %all-reduce.22.cloned.1.call-done = (f32[144,1024]{1,0:T(8,128)}, f32[144,256]{1,0:T(8,128)}, f32[144,256]{1,0:T(8,128)}, f32[128,1152]{1,0:T(8,128)}, f32[144,6...) async-done(((f32[144,1024]{1,0:T(8,128)}, f32[144,256]{1,0:T(8,128)}, f32[144,256]{1,0:T(8,128)}, f32[128,1152]{1,0:T(8,128)}, f32[144,6912]{1,0:T(8,128)}, ...) | async-done | bytes 13418512 | tf_op jit(solution)/shard_map/psum | solution.py:291
  3221.7 4.5 copy.175
  (424 shorter events, 191.7 us)
Async XLA Ops:
  7.2 67.9 %copy-start.12 = (bf16[512,1152]{1,0:T(8,128)(2,1)S(1)}, bf16[512,1152]{1,0:T(8,128)(2,1)}, u32[]{:S(2)}) copy-start(bf16[512,1152]{1,0:T(8,128)(2,1)} %param.21) | copy-start | bytes 3538948
  7.2 111.6 %all-gather.8.cloned.1.call-start = ((), (), s32[]{:S(2)}) async-start(), calls=%async_computation.13 | async-start | bytes 2654208 | tf_op jit(solution)/shard_map/all_gather | solution.py:91
  9.2 146.6 %all-gather.10.cloned.1.call-start = ((), (), s32[]{:S(2)}) async-start(), calls=%async_computation.14 | async-start | bytes 1310720 | tf_op jit(solution)/shard_map/all_gather | solution.py:144
  45.5 73.3 %copy-start.50 = (f32[1152]{0:T(1024)}, f32[1152]{0:T(1024)S(1)}, u32[]{:S(2)}) copy-start(f32[1152]{0:T(1024)S(1)} %convert_element_type.154) | copy-start | bytes 13828
  46.5 29.3 copy-start.72
  46.5 30.1 copy-start.82
  47.3 29.4 copy-start.65
  48.8 27.0 copy-start.67
  48.9 69.9 %copy-start.62 = (f32[512]{0:T(512)}, f32[512]{0:T(512)S(1)}, u32[]{:S(2)}) copy-start(f32[512]{0:T(512)S(1)} %fusion.63) | copy-start | bytes 6148
  75.8 30.1 copy-start.55
  78.6 27.4 copy-start.41
  78.6 79.5 %all-gather.12.cloned.1.call-start = ((), (), s32[]{:S(2)}) async-start(), calls=%async_computation.15 | async-start | bytes 1310720 | tf_op jit(solution)/shard_map/all_gather | solution.py:145
  105.9 123.0 %all-gather.14.cloned.1.call-start = ((), (), s32[]{:S(2)}) async-start(), calls=%async_computation.16 | async-start | bytes 2654208 | tf_op jit(solution)/shard_map/all_gather | solution.py:94
  106.7 305.9 %all-gather.16.cloned.1.call-start = ((), (), s32[]{:S(2)}) async-start(), calls=%async_computation.17 | async-start | bytes 17915904 | tf_op jit(solution)/shard_map/all_gather | solution.py:101
  110.4 520.2 %all-gather.18.cloned.1.call-start = ((), (), s32[]{:S(2)}) async-start(), calls=%async_computation.18 | async-start | bytes 17915904 | tf_op jit(solution)/shard_map/all_gather | solution.py:102
  114.1 734.1 %all-gather.20.cloned.1.call-start = ((), (), s32[]{:S(2)}) async-start(), calls=%async_computation.19 | async-start | bytes 17915904 | tf_op jit(solution)/shard_map/all_gather | solution.py:103
  130.4 39.1 %copy-start.36 = (s32[2048]{0:T(1024)S(1)}, s32[2048]{0:T(1024)}, u32[]{:S(2)}) copy-start(s32[2048]{0:T(1024)} %param.24) | copy-start | bytes 24580
  130.4 39.1 %copy-start.53 = (s32[2048]{0:T(1024)S(1)}, s32[2048]{0:T(1024)}, u32[]{:S(2)}) copy-start(s32[2048]{0:T(1024)} %param.23) | copy-start | bytes 24580
  130.4 39.0 %all-to-all-start = ((bf16[512,4,256]{2,0,1:T(8,128)(2,1)}), bf16[512,4,256]{2,0,1:T(8,128)(2,1)}, u32[]{:S(2)}, u32[]{:S(2)}) async-start(bf16[512,4,256]{2,0,1:T(8,128)(2,1)} %pad_maximum_fusion), calls=%async_computation | async-start | bytes 2097152 | tf_op jit(solution)/shard_map/all_to_all | solution.py:136
  204.5 19.1 all-to-all-start.1
  209.9 23.3 copy-start.46
  234.6 194.2 %copy-start.70 = (f32[512]{0:T(512)}, f32[512]{0:T(512)S(1)}, u32[]{:S(2)}) copy-start(f32[512]{0:T(512)S(1)} %fusion.66) | copy-start | bytes 6148
  234.9 395.8 %copy-start.16 = (bf16[512,1152]{1,0:T(8,128)(2,1)}, bf16[512,1152]{1,0:T(8,128)(2,1)S(1)}, u32[]{:S(2)}) copy-start(bf16[512,1152]{1,0:T(8,128)(2,1)S(1)} %multiply_convert_fusion.3) | copy-start | bytes 3538948
  932.2 21.2 copy-start.9
  932.2 21.2 copy-start.37
  933.3 19.0 all-to-all-start.2
  938.6 123.7 %reduce-scatter.10.cloned.1.call-start = ((), (), s32[]{:S(2)}) async-start(), calls=%async_computation.20 | async-start | bytes 2621440 | tf_op jit(solution)/shard_map/reduce_scatter | solution.py:256
  1031.4 32.0 copy-start.66
  1031.4 32.0 copy-start.83
  1031.4 33.2 %copy-start.21 = (f32[512,256]{0,1:T(8,128)S(1)}, f32[512,256]{0,1:T(8,128)}, u32[]{:S(2)}) copy-start(f32[512,256]{0,1:T(8,128)} %copy-done.20) | copy-start | bytes 1572868
  1031.4 33.2 %copy-start.56 = (f32[512]{0:T(512)S(1)}, f32[512]{0:T(512)}, u32[]{:S(2)}) copy-start(f32[512]{0:T(512)} %copy-done.55) | copy-start | bytes 6148
  1031.5 33.2 %copy-start.73 = (f32[256]{0:T(256)S(1)}, f32[256]{0:T(256)}, u32[]{:S(2)}) copy-start(f32[256]{0:T(256)} %copy-done.72) | copy-start | bytes 3076
  1031.5 65.6 %reduce-scatter.12.cloned.1.call-start = ((), (), s32[]{:S(2)}) async-start(), calls=%async_computation.21 | async-start | bytes 2621440 | tf_op jit(solution)/shard_map/reduce_scatter | solution.py:257
  1031.5 33.9 %copy-start.77 = (f32[512]{0:T(512)S(1)}, f32[512]{0:T(512)}, u32[]{:S(2)}) copy-start(f32[512]{0:T(512)} %copy-done.76) | copy-start | bytes 6148
  1032.2 34.1 %copy-start.13 = (bf16[512,1152]{1,0:T(8,128)(2,1)S(1)}, bf16[512,1152]{1,0:T(8,128)(2,1)}, u32[]{:S(2)}) copy-start(bf16[512,1152]{1,0:T(8,128)(2,1)} %param.21) | copy-start | bytes 3538948
  1032.2 34.0 %copy-start.51 = (f32[1152]{0:T(1024)S(1)}, f32[1152]{0:T(1024)}, u32[]{:S(2)}) copy-start(f32[1152]{0:T(1024)} %copy-done.50) | copy-start | bytes 13828
  1032.2 34.0 %copy-start.63 = (f32[512]{0:T(512)S(1)}, f32[512]{0:T(512)}, u32[]{:S(2)}) copy-start(f32[512]{0:T(512)} %copy-done.62) | copy-start | bytes 6148
  1032.2 159.5 %reduce-scatter.16.cloned.1.call-start = ((), (), s32[]{:S(2)}) async-start(), calls=%async_computation.23 | async-start | bytes 1327104 | tf_op jit(solution)/shard_map/reduce_scatter | solution.py:278
  1067.9 31.9 copy-start.15
  1067.9 31.9 copy-start.23
  1067.9 162.1 %reduce-scatter.18.cloned.1.call-start = ((), (), s32[]{:S(2)}) async-start(), calls=%async_computation.24 | async-start | bytes 1327104 | tf_op jit(solution)/shard_map/reduce_scatter | solution.py:279
  1099.8 230.3 %reduce-scatter.20.cloned.1.call-start = ((), (), s32[]{:S(2)}) async-start(), calls=%async_computation.25 | async-start | bytes 5308416 | tf_op jit(solution)/shard_map/reduce_scatter | solution.py:280
  1103.5 325.4 %reduce-scatter.14.cloned.1.call-start = ((), (), s32[]{:S(2)}) async-start(), calls=%async_computation.22 | async-start | bytes 5308416 | tf_op jit(solution)/shard_map/reduce_scatter | solution.py:277
  1135.9 807.5 %reduce-scatter.22.cloned.1.call-start = ((), (), s32[]{:S(2)}) async-start(), calls=%async_computation.26 | async-start | bytes 35831808 | tf_op jit(solution)/shard_map/reduce_scatter | solution.py:281
  1154.2 1304.7 %reduce-scatter.24.cloned.1.call-start = ((), (), s32[]{:S(2)}) async-start(), calls=%async_computation.27 | async-start | bytes 35831808 | tf_op jit(solution)/shard_map/reduce_scatter | solution.py:282
  1171.2 1803.0 %reduce-scatter.26.cloned.1.call-start = ((), (), s32[]{:S(2)}) async-start(), calls=%async_computation.28 | async-start | bytes 35831808 | tf_op jit(solution)/shard_map/reduce_scatter | solution.py:283
  1191.6 2023.0 %all-reduce.22.cloned.1.call-start = ((), (), s32[]{:S(2)}) async-start(), calls=%async_computation.29 | async-start | bytes 26836992 | tf_op jit(solution)/shard_map/psum | solution.py:291
  2980.0 52.3 %copy-start.11 = (f32[512,1152]{1,0:T(8,128)S(1)}, f32[512,1152]{1,0:T(8,128)}, u32[]{:S(2)}) copy-start(f32[512,1152]{1,0:T(8,128)} %copy-done.10) | copy-start | bytes 7077892
  (71 other events, 319.0 us)
Sparse Core Ops, SparseCore 0:
  10.8 54.3 all-gather.7
  78.7 30.3 all-gather.9
  110.7 31.9 all-gather.11
  144.8 50.6 all-gather.13
  198.0 214.5 all-gather.15
  415.2 215.3 all-gather.17
  632.8 215.3 all-gather.19
  1031.6 30.7 reduce-scatter.9
  1065.6 31.4 reduce-scatter.11
  1100.9 62.0 reduce-scatter.15
  1167.0 63.0 reduce-scatter.17
  1233.5 96.4 reduce-scatter.19
  1333.7 95.1 reduce-scatter.13
  1432.6 510.6 reduce-scatter.21
  1947.1 511.6 reduce-scatter.23
  2462.6 511.5 reduce-scatter.25
  2977.3 237.3 all-reduce.21
where the time goes:
time: 3250 us; the launch traced here: 3240 us
  waiting for transfers between devices  2640 us (81%)
  matrix products  270 us (8%)
  blocking collectives  139 us (4%)
  local copies, waits for them, and re-layouts  81.5 us (3%)
  other arithmetic  52.5 us (2%)
  starting transfers between devices  36.7 us (1%)
    reduce_scatter x1, waiting for transfers between devices, body(): lax.psum_scatter(grad_up, 'fsdp', scatter_dimension=0, tiled=True)  515 us
    reduce_scatter x1, waiting for transfers between devices, body(): lax.psum_scatter(grad_down, 'fsdp', scatter_dimension=0, tiled=True)  515 us
    reduce_scatter x1, waiting for transfers between devices, body(): lax.psum_scatter(grad_gate, 'fsdp', scatter_dimension=0, tiled=True)  514 us
    all_gather x1, waiting for transfers between devices, body(): lax.all_gather(to_half(up_weight), 'fsdp', axis=0, tiled=True)  202 us
    all_gather x1, waiting for transfers between devices, body(): lax.all_gather(to_half(down_weight), 'fsdp', axis=0, tiled=True)  196 us
    psum x1, waiting for transfers between devices, body(): lax.psum((shares[0], shares[1], shares[2], shares[3], shares[4], shares[5...  179 us
    all_gather x1, waiting for transfers between devices, body(): lax.all_gather(to_half(gate_weight), 'fsdp', axis=0, tiled=True)  178 us
    dot_general x19, matrix products, outer_cols(): lax.dot_general(left, right, (((1,), (1,)), ((), ())), preferred_element_...  101 us
  transfers between devices with their start and end apart: 20, of which 15 were waited for; matrix products, arithmetic and copies ran while one was open for 7% of the time, Pallas kernels for 0%

commit v1 on v0

v1 whole, which is shorter than its diff:
```python
from functools import partial

import jax
import jax.numpy as jnp
from jax import lax
from jax.experimental import pallas as pl
from jax.experimental.pallas import tpu as pltpu
from jax.sharding import PartitionSpec as P

epsilon = 1e-06
f32 = jnp.float32
bf16 = jnp.bfloat16
SEQ = 4


def rms_scale(values, gain):
    return values * lax.rsqrt(jnp.mean(values * values, axis=-1, keepdims=True) + epsilon) * gain


def rotate(values, cosine, sine):
    half_width = values.shape[-1] // 2
    first_half = values[..., :half_width]
    second_half = values[..., half_width:]
    return jnp.concatenate(
        [first_half * cosine - second_half * sine, second_half * cosine + first_half * sine],
        axis=-1,
    )


def rope_tables(places, width):
    half_width = width // 2
    inverse = 1.0 / 1000000.0 ** (jnp.arange(half_width, dtype=f32) * 2.0 / width)
    angles = places.astype(f32)[:, None] * inverse[None, :]
    return (jnp.cos(angles), jnp.sin(angles))


def head_norm(raw, gain, cosine, sine):
    return rotate(rms_scale(raw, gain), cosine, sine)


def mult(left, right):
    return jnp.dot(left, right, preferred_element_type=f32)


def inner_rows(left, right):
    return lax.dot_general(left, right, (((0,), (0,)), ((), ())), preferred_element_type=f32)


def outer_cols(left, right):
    return lax.dot_general(left, right, (((1,), (1,)), ((), ())), preferred_element_type=f32)


def to_half(values):
    return values.astype(bf16)


def gated(gate_in, up_in):
    return jax.nn.gelu(gate_in, approximate=True) * up_in


def attend_kernel(scale, q_ref, k_ref, v_ref, code_ref, low_ref, high_ref, out_ref, probs_ref):
    scores = outer_cols(q_ref[...], k_ref[...])
    code = code_ref[...]
    seen = (code >= low_ref[...]) & (code <= high_ref[...])
    expd = jnp.where(seen, jnp.exp2(scores * (scale * 1.4426950408889634)), 0.0)
    total = jnp.sum(expd, axis=1, keepdims=True)
    probs = to_half(expd * (1.0 / total))
    probs_ref[...] = probs
    out_ref[...] = to_half(mult(probs, v_ref[...]))


def attend(queries, keys, values, code, low, high, scale, block):
    rows, width = queries.shape
    count = keys.shape[0]
    whole = pl.BlockSpec((count, width), lambda i: (0, 0))
    slab = pl.BlockSpec((block, width), lambda i: (i, 0))
    thin = pl.BlockSpec((block, 1), lambda i: (i, 0))
    return pl.pallas_call(
        partial(attend_kernel, scale),
        grid=(rows // block,),
        in_specs=[slab, whole, whole, pl.BlockSpec((1, count), lambda i: (0, 0)), thin, thin],
        out_specs=[slab, pl.BlockSpec((block, count), lambda i: (i, 0))],
        out_shape=[
            jax.ShapeDtypeStruct((rows, width), bf16),
            jax.ShapeDtypeStruct((rows, count), bf16),
        ],
        compiler_params=pltpu.CompilerParams(vmem_limit_bytes=40 * 2**20),
        cost_estimate=pl.CostEstimate(
            flops=4 * rows * count * width,
            bytes_accessed=2 * rows * count + 8 * rows * width,
            transcendentals=rows * count,
        ),
    )(queries, keys, values, code, low, high)


def attend_back_kernel(scale, q_ref, k_ref, v_ref, p_ref, g_ref, dq_ref, dk_ref, dv_ref):
    @pl.when(pl.program_id(0) == 0)
    def _():
        dk_ref[...] = jnp.zeros_like(dk_ref)
        dv_ref[...] = jnp.zeros_like(dv_ref)

    probs = p_ref[...]
    grads = g_ref[...]
    wide = probs.astype(f32)
    grad_probs = outer_cols(grads, v_ref[...])
    centre = jnp.sum(wide * grad_probs, axis=1, keepdims=True)
    grad_scores = to_half(wide * (grad_probs - centre))
    dq_ref[...] = to_half(scale * mult(grad_scores, k_ref[...]))
    dk_ref[...] += scale * inner_rows(grad_scores, q_ref[...])
    dv_ref[...] += inner_rows(probs, grads)


def attend_back(queries, keys, values, probs, grads, scale, block):
    rows, width = queries.shape
    count = keys.shape[0]
    whole = pl.BlockSpec((count, width), lambda i: (0, 0))
    slab = pl.BlockSpec((block, width), lambda i: (i, 0))
    return pl.pallas_call(
        partial(attend_back_kernel, scale),
        grid=(rows // block,),
        in_specs=[slab, whole, whole, pl.BlockSpec((block, count), lambda i: (i, 0)), slab],
        out_specs=[slab, whole, whole],
        out_shape=[
            jax.ShapeDtypeStruct((rows, width), bf16),
            jax.ShapeDtypeStruct((count, width), f32),
            jax.ShapeDtypeStruct((count, width), f32),
        ],
        compiler_params=pltpu.CompilerParams(vmem_limit_bytes=48 * 2**20),
        cost_estimate=pl.CostEstimate(
            flops=8 * rows * count * width,
            bytes_accessed=2 * rows * count + 20 * rows * width,
            transcendentals=0,
        ),
    )(queries, keys, values, probs, grads)


def swap_seq(values, bits):
    return lax.ppermute(values, "seq", [(i, i ^ bits) for i in range(SEQ)])


def gather_seq(own):
    one = swap_seq(own, 1)
    two = swap_seq(own, 2)
    return [own, one, two, swap_seq(two, 1)]


def natural(blocks, me):
    stack = jnp.stack(blocks)
    return [lax.dynamic_index_in_dim(stack, me ^ j, 0, keepdims=False) for j in range(SEQ)]


def reduce_seq(blocks):
    three = swap_seq(blocks[3], 1)
    pair = to_half(blocks[2].astype(f32) + three.astype(f32))
    two = swap_seq(pair, 2)
    one = swap_seq(blocks[1], 1)
    return blocks[0].astype(f32) + one.astype(f32) + two.astype(f32)


class Owners:
    def __init__(self, count):
        self.count = count
        self.rows = count // 2
        self.groups = [[2 * z + y for z in range(self.rows)] for y in range(2)]
        index = lax.axis_index("fsdp")
        self.low = index % 2
        self.high = index // 2
        self.direct = self.rows <= 4

    def swap(self, values):
        return lax.ppermute(values, "fsdp", [(i, i ^ 1) for i in range(self.count)])

    def shift(self, values, by):
        return lax.ppermute(
            values, "fsdp", [(i, (i + 2 * by) % self.count) for i in range(self.count)]
        )

    def gather_row(self, values):
        return lax.all_gather(values, "fsdp", axis=0, tiled=True, axis_index_groups=self.groups)

    def pair(self, mine, other, axis):
        first = jnp.where(self.low == 0, mine, other)
        second = jnp.where(self.low == 0, other, mine)
        return jnp.stack([first, second], axis=axis)

    def gather_small(self, own):
        if not self.direct:
            return lax.all_gather(own, "fsdp", axis=0, tiled=True)
        size, width = own.shape
        whole = jnp.zeros((self.rows, 2, size, width), own.dtype)

        def put(whole, block, by, flip):
            z = lax.rem(self.high - by + self.rows, self.rows)
            y = self.low ^ flip
            return lax.dynamic_update_slice(whole, block[None, None], (z, y, 0, 0))

        far = [self.shift(own, by) for by in range(1, self.rows)]
        parts = [own] + far
        flipped = [self.swap(p) for p in parts]
        for by in range(self.rows):
            whole = put(whole, parts[by], by, 0)
            whole = put(whole, flipped[by], by, 1)
        return whole.reshape(self.count * size, width)

    def gather_wide(self, own):
        size, width = own.shape
        mine = self.gather_row(own).reshape(self.rows, size, width)
        other = self.swap(mine)
        return self.pair(mine, other, 1).reshape(self.count * size, width)

    def gather_pair_first(self, own):
        size, width = own.shape
        both = self.pair(own, self.swap(own), 0).reshape(2 * size, width)
        return self.gather_row(both)

    def fold(self, whole):
        size = whole.shape[0] // self.count
        view = whole.reshape(self.rows, 2, size, whole.shape[1])
        away = lax.dynamic_index_in_dim(view, 1 - self.low, 1, keepdims=False)
        here = lax.dynamic_index_in_dim(view, self.low, 1, keepdims=False)
        come = self.swap(away)
        return to_half(here.astype(f32) + come.astype(f32))

    def scatter_wide(self, whole):
        half = self.fold(whole)
        return lax.psum_scatter(
            half.reshape(-1, half.shape[2]),
            "fsdp",
            scatter_dimension=0,
            axis_index_groups=self.groups,
            tiled=True,
        ).astype(f32)

    def scatter_small(self, whole):
        half = self.fold(whole)
        if not self.direct:
            return lax.psum_scatter(
                half.reshape(-1, half.shape[2]),
                "fsdp",
                scatter_dimension=0,
                axis_index_groups=self.groups,
                tiled=True,
            ).astype(f32)
        total = lax.dynamic_index_in_dim(half, self.high, 0, keepdims=False).astype(f32)
        for by in range(1, self.rows):
            z = lax.rem(self.high + by, self.rows)
            away = lax.dynamic_index_in_dim(half, z, 0, keepdims=False)
            total = total + self.shift(away, by).astype(f32)
        return total


def body(
    tokens,
    cotangent,
    positions,
    segment,
    query_weight,
    key_weight,
    value_weight,
    out_weight,
    gate_weight,
    up_weight,
    down_weight,
    gain_input,
    gain_query,
    gain_key,
    gain_mixed,
    gain_feed,
    gain_final,
    fsdp,
):
    owners = Owners(fsdp)
    me = lax.axis_index("seq")
    core = me & 1
    tok_rows, model = tokens.shape
    group_len = positions.shape[0]
    rows = query_weight.shape[0]
    head_width = key_weight.shape[1]
    hidden = gate_weight.shape[1]
    slab = hidden // fsdp
    part = slab // SEQ
    scale = head_width ** (-0.5)

    head_cols = lax.dynamic_slice_in_dim(query_weight, me * head_width, head_width, axis=1)
    key_or_value = jnp.where(core == 0, key_weight, value_weight)
    short = jnp.stack([gain_query, gain_key], axis=1)
    short = jnp.pad(short, ((0, rows - short.shape[0]), (0, 0)))
    gains_own = jnp.concatenate(
        [jnp.stack([gain_input, gain_mixed, gain_feed, gain_final], axis=1), short], axis=1
    )
    gains_own = jnp.pad(gains_own, ((0, 0), (0, 128 - gains_own.shape[1])))
    attn_own = to_half(jnp.concatenate([head_cols, key_or_value, gains_own], axis=1))

    def columns(weight):
        return to_half(
            jnp.concatenate(
                [
                    lax.dynamic_slice_in_dim(weight, f * slab + me * part, part, axis=1)
                    for f in range(fsdp)
                ],
                axis=1,
            )
        )

    gate_own = columns(gate_weight)
    up_own = columns(up_weight)
    down_own = to_half(lax.dynamic_slice_in_dim(down_weight, me * part, part, axis=0))
    out_rows = out_weight.shape[0]
    out_half = out_rows // 2
    out_own = to_half(lax.dynamic_slice_in_dim(out_weight, core * out_half, out_half, axis=0))

    token_blocks = gather_seq(tokens)
    attn_pack = owners.gather_small(attn_own)
    w_gate = owners.gather_wide(gate_own)
    w_out_half = owners.gather_pair_first(out_own)
    w_up = owners.gather_wide(up_own)
    w_down = owners.gather_pair_first(down_own)

    gains = attn_pack[:, 2 * head_width :].astype(f32).T
    g_input, g_mixed, g_feed, g_final = gains[0], gains[1], gains[2], gains[3]
    short_rows = head_width // fsdp
    g_query = gains[4].reshape(fsdp, rows)[:, :short_rows].reshape(head_width)
    g_key = gains[5].reshape(fsdp, rows)[:, :short_rows].reshape(head_width)
    mine_kv = attn_pack[:, head_width : 2 * head_width]
    other_kv = swap_seq(mine_kv, 1)
    w_qkv = jnp.concatenate(
        [
            attn_pack[:, :head_width],
            jnp.where(core == 0, mine_kv, other_kv),
            jnp.where(core == 0, other_kv, mine_kv),
        ],
        axis=1,
    )

    def own_order(values):
        return jnp.concatenate(
            [
                lax.dynamic_slice_in_dim(values, (me ^ r) * tok_rows, tok_rows)
                for r in range(SEQ)
            ]
        )

    places = own_order(positions)
    kinds = own_order(segment)
    cosine, sine = rope_tables(places, head_width)
    second = kinds == 2
    code = jnp.where(second, -places, places).astype(f32)[None, :]
    low = jnp.where(second, -places, 0).astype(f32)[:, None]
    high = jnp.where(second, group_len // 2 - 1, places).astype(f32)[:, None]

    all_tokens = jnp.concatenate(token_blocks).astype(f32)
    normed16 = to_half(rms_scale(all_tokens, g_input))
    qkv = mult(normed16, w_qkv)
    query_raw = qkv[:, :head_width]
    key_raw = qkv[:, head_width : 2 * head_width]
    values = to_half(qkv[:, 2 * head_width :])
    normer = partial(head_norm, cosine=cosine, sine=sine)
    queries, query_back = jax.vjp(normer, query_raw, g_query)
    keys, key_back = jax.vjp(normer, key_raw, g_key)
    queries = to_half(queries)
    keys = to_half(keys)
    attended, probs = attend(queries, keys, values, code, low, high, scale, 256)

    heads = [attended[:tok_rows]] + [
        swap_seq(attended[r * tok_rows : (r + 1) * tok_rows], r) for r in range(1, SEQ)
    ]
    heads16 = jnp.concatenate(natural(heads, me), axis=1)

    other_half = swap_seq(w_out_half, 1).reshape(fsdp, out_half, model)
    mine_half = w_out_half.reshape(fsdp, out_half, model)
    w_out = jnp.stack(
        [
            jnp.where(core == 0, mine_half, other_half),
            jnp.where(core == 0, other_half, mine_half),
        ],
        axis=1,
    ).reshape(fsdp * out_rows, model)
    attn = mult(heads16, w_out)
    inputs32 = tokens.astype(f32)
    post_attn, mixed_back = jax.vjp(rms_scale, attn, g_mixed)
    mixed = inputs32 + post_attn
    fed, feed_back = jax.vjp(lambda v: rms_scale(v, g_feed), mixed)

    fed16 = jnp.concatenate(gather_seq(to_half(fed)))
    gate16 = to_half(mult(fed16, w_gate))
    upper = mult(fed16, w_up)
    act16 = to_half(gated(gate16.astype(f32), upper))
    upper16 = to_half(upper)
    share = to_half(mult(act16, w_down))
    ffo = reduce_seq([share[r * tok_rows : (r + 1) * tok_rows] for r in range(SEQ)])
    post_feed, final_back = jax.vjp(rms_scale, ffo, g_final)
    output = to_half(mixed + post_feed)

    grad_rows = cotangent.astype(f32)
    grad_ffo, gain_final_part = final_back(grad_rows)
    grad_ffo16 = jnp.concatenate(gather_seq(to_half(grad_ffo)))
    grad_act = outer_cols(grad_ffo16, w_down)
    _, act_back = jax.vjp(gated, gate16.astype(f32), upper16.astype(f32))
    grad_gate_in, grad_up_in = act_back(grad_act)
    grad_gate16 = to_half(grad_gate_in)
    grad_up16 = to_half(grad_up_in)
    grad_fed_share = to_half(outer_cols(grad_gate16, w_gate) + outer_cols(grad_up16, w_up))
    grad_gate = owners.scatter_wide(to_half(inner_rows(fed16, grad_gate16)))
    grad_up = owners.scatter_wide(to_half(inner_rows(fed16, grad_up16)))
    grad_down_share = to_half(inner_rows(act16, grad_ffo16))
    grad_fed = reduce_seq([grad_fed_share[r * tok_rows : (r + 1) * tok_rows] for r in range(SEQ)])
    (grad_mixed_part,) = feed_back(grad_fed)
    grad_mixed = grad_rows + grad_mixed_part

    grad_attn, gain_mixed_part = mixed_back(grad_mixed)
    grad_attn16 = to_half(grad_attn)
    grad_heads16 = to_half(outer_cols(grad_attn16, w_out))
    grad_heads = [
        lax.dynamic_slice_in_dim(grad_heads16, (me ^ r) * head_width, head_width, axis=1)
        for r in range(SEQ)
    ]
    grad_heads = [grad_heads[0]] + [swap_seq(grad_heads[r], r) for r in range(1, SEQ)]
    grad_heads = jnp.concatenate(grad_heads)

    grad_out_share = to_half(inner_rows(heads16, grad_attn16))
    out_part = out_rows // SEQ
    grad_out_view = grad_out_share.reshape(fsdp, SEQ, out_part, model)
    grad_out_part = reduce_seq(
        [
            lax.dynamic_index_in_dim(grad_out_view, me ^ r, 1, keepdims=False)
            for r in range(SEQ)
        ]
    )
    grad_rest = owners.scatter_wide(
        jnp.concatenate(
            [grad_down_share.reshape(fsdp, part, model), to_half(grad_out_part)], axis=1
        ).reshape(fsdp * (part + out_part), model)
    )

    grad_queries, grad_keys, grad_values = attend_back(
        queries, keys, values, probs, grad_heads, scale, 256
    )
    grad_query_raw, gain_query_part = query_back(grad_queries.astype(f32))
    grad_key_raw, gain_key_part = key_back(grad_keys)
    grad_qkv16 = jnp.concatenate(
        [to_half(grad_query_raw), to_half(grad_key_raw), to_half(grad_values)], axis=1
    )
    grad_normed_share = to_half(outer_cols(grad_qkv16, w_qkv))
    grad_proj = to_half(inner_rows(normed16, grad_qkv16))
    grad_k = grad_proj[:, head_width : 2 * head_width]
    grad_v = grad_proj[:, 2 * head_width :]
    come = swap_seq(jnp.where(core == 0, grad_v, grad_k), 1)
    grad_kv = jnp.where(core == 0, grad_k, grad_v).astype(f32) + come.astype(f32)
    short = jnp.stack([gain_query_part, gain_key_part], axis=1).reshape(fsdp, short_rows, 2)
    short = jnp.pad(short, ((0, 0), (0, rows - short_rows), (0, 0))).reshape(model, 2)
    gain_parts = jnp.concatenate(
        [jnp.stack([gain_mixed_part, gain_final_part], axis=1), short], axis=1
    )
    gain_parts = jnp.pad(gain_parts, ((0, 0), (0, 128 - gain_parts.shape[1])))
    grad_small = owners.scatter_small(
        jnp.concatenate(
            [grad_proj[:, :head_width], to_half(grad_kv), to_half(gain_parts)], axis=1
        )
    )

    grad_normed = reduce_seq(
        [grad_normed_share[r * tok_rows : (r + 1) * tok_rows] for r in range(SEQ)]
    )
    _, input_back = jax.vjp(lambda v: rms_scale(v, g_input), inputs32)
    (grad_input_part,) = input_back(grad_normed)
    grad_tokens = grad_mixed + grad_input_part

    wide = jnp.concatenate([to_half(grad_gate), to_half(grad_up)], axis=1)
    wide = natural(gather_seq(wide), me)
    rest = natural(gather_seq(to_half(grad_rest)), me)

    def spread(blocks, at):
        width = fsdp * part
        if fsdp <= 8:
            pieces = [
                blocks[t][:, at * width + f * part : at * width + (f + 1) * part]
                for f in range(fsdp)
                for t in range(SEQ)
            ]
            return jnp.concatenate(pieces, axis=1).astype(f32)
        stack = jnp.stack([b[:, at * width : (at + 1) * width].reshape(rows, fsdp, part) for b in blocks], axis=2)
        return stack.reshape(rows, hidden).astype(f32)

    out_gate = spread(wide, 0)
    out_up = spread(wide, 1)
    out_down = jnp.concatenate([b[:part] for b in rest]).astype(f32)
    out_out = jnp.concatenate([b[part:] for b in rest]).astype(f32)

    feed_sum = jnp.sum(grad_gate * gate_own.astype(f32) + grad_up * up_own.astype(f32), axis=1)
    input_sum = jnp.sum(
        grad_small[:, : 2 * head_width] * attn_own[:, : 2 * head_width].astype(f32), axis=1
    )
    tail = jnp.concatenate(
        [grad_small[:, 2 * head_width : 2 * head_width + 4], jnp.stack([input_sum, feed_sum], axis=1)],
        axis=1,
    )
    tail = jnp.pad(tail, ((0, 0), (0, 128 - tail.shape[1])))
    small = gather_seq(to_half(jnp.concatenate([grad_small[:, : 2 * head_width], tail], axis=1)))
    out_query = jnp.concatenate([b[:, :head_width] for b in natural(small, me)], axis=1).astype(f32)
    kv = [b[:, head_width : 2 * head_width].astype(f32) for b in small]
    same, cross = kv[0] + kv[2], kv[1] + kv[3]
    out_key = jnp.where(core == 0, same, cross)
    out_value = jnp.where(core == 0, cross, same)
    tails = sum(b[:, 2 * head_width :].astype(f32) for b in small)
    own_gains = attn_own[:, 2 * head_width :].astype(f32)
    out_g_mixed = tails[:, 0]
    out_g_final = tails[:, 1]
    out_g_query = tails[:short_rows, 2]
    out_g_key = tails[:short_rows, 3]
    out_g_input = tails[:, 4] / own_gains[:, 0]
    out_g_feed = tails[:, 5] / own_gains[:, 2]
    return (
        output,
        grad_tokens,
        out_query,
        out_key,
        out_value,
        out_out,
        out_gate,
        out_up,
        out_down,
        out_g_input,
        out_g_query,
        out_g_key,
        out_g_mixed,
        out_g_feed,
        out_g_final,
    )


def solution(mesh):
    by_token = P(("fsdp", "seq"), None)
    by_row = P("fsdp", None)
    by_one = P("fsdp")
    return jax.shard_map(
        partial(body, fsdp=mesh.shape["fsdp"]),
        mesh=mesh,
        in_specs=(by_token,) * 2 + (by_one,) * 2 + (by_row,) * 7 + (by_one,) * 6,
        out_specs=(by_token,) * 2 + (by_row,) * 7 + (by_one,) * 6,
        check_vma=False,
    )
```

time: 3250 us -> 818 us (0.25)
  waiting for transfers between devices: 2640 us -> 314 us
  blocking collectives: 139 us -> 0 us
  matrix products: 270 us -> 171 us
  other arithmetic: 52.5 us -> 109 us
  local copies, waits for them, and re-layouts: 81.5 us -> 115 us
    reduce_scatter x9 -> x2, waiting for transfers between devices: 1840 us -> 0.01 us  [scatter_wide(): lax.psum_scatter(half.reshape(-1, half.shape[2]), 'fsdp', scatter_dimensi...]
    all_gather x7 -> x4, waiting for transfers between devices: 576 us -> 25.7 us  [gather_row(): lax.all_gather(values, 'fsdp', axis=0, tiled=True, axis_index_groups=self...]
    ppermute x0 -> x57, waiting for transfers between devices: none -> 288 us  [the longest x12 135 us: swap(): return lax.ppermute(values, 'fsdp', [(i, i ^ 1) for i in range(self.count)])]
    psum x1 -> x0, waiting for transfers between devices: 179 us -> none  [body(): lax.psum((shares[0], shares[1], shares[2], shares[3], shares[4], shares[5...]
    unnamed x2 -> x0, blocking collectives: 56.9 us -> none
    ppermute x0 -> x57, starting transfers between devices: none -> 52.4 us  [the longest x39 39.1 us: swap_seq(): return lax.ppermute(values, 'seq', [(i, i ^ bits) for i in range(SEQ)])]
    all_gather x2 -> x0, blocking collectives: 51.3 us -> none  [the longest x1 26.2 us: body(): lax.all_gather(to_half(key_weight), 'fsdp', axis=0, tiled=True)]
    dot_general x15 -> x5, matrix products: 90.7 us -> 49.9 us  [inner_rows(): lax.dot_general(left, right, (((0,), (0,)), ((), ())), preferred_element_...]
  transfers between devices with their start and end apart: 20 -> 64, of which waited for: 15 -> 29; matrix products, arithmetic and copies ran while one was open for 7% -> 36% of each run, Pallas kernels for 0% -> 4%
where the time goes in v1:
time: 818 us; the launch traced here: 809 us
  waiting for transfers between devices  314 us (38%)
  matrix products  171 us (21%)
  local copies, waits for them, and re-layouts  115 us (14%)
  other arithmetic  109 us (13%)
  starting transfers between devices  52.9 us (6%)
  Pallas kernels  30.1 us (4%)
  between operations  16.5 us (2%)
    ppermute x12, waiting for transfers between devices, swap(): return lax.ppermute(values, 'fsdp', [(i, i ^ 1) for i in range(self.count)])  135 us
    ppermute x39, waiting for transfers between devices, swap_seq(): return lax.ppermute(values, 'seq', [(i, i ^ bits) for i in range(SEQ)])  105 us
    dot_general x5, matrix products, outer_cols(): lax.dot_general(left, right, (((1,), (1,)), ((), ())), preferred_element_...  64.9 us
    dot_general x5, matrix products, mult(): return jnp.dot(left, right, preferred_element_type=f32)  56.5 us
    dot_general x5, matrix products, inner_rows(): lax.dot_general(left, right, (((0,), (0,)), ((), ())), preferred_element_...  49.9 us
    ppermute x6, waiting for transfers between devices, shift(): lax.ppermute(values, 'fsdp', [(i, (i + 2 * by) % self.count) for i in ran...  47.9 us
    ppermute x39, starting transfers between devices, swap_seq(): return lax.ppermute(values, 'seq', [(i, i ^ bits) for i in range(SEQ)])  39.1 us
    convert_element_type x15, other arithmetic, to_half(): return values.astype(bf16)  25.8 us
  transfers between devices with their start and end apart: 64, of which 29 were waited for; matrix products, arithmetic and copies ran while one was open for 36% of the time, Pallas kernels for 4%

profile of v1, /device:TPU:9, one launch (start us, length us, event | category | flops | bytes accessed | tf_op | source)
XLA Modules:
  0.0 809.3 jit_solution(3088272117139960856)
XLA Ops:
  9.8 3.5 collective-permute-done.14
  25.1 3.5 dynamic-slice_convert_fusion.2
  43.2 22.1 %collective-permute-done.6 = bf16[144,640]{0,1:T(8,128)(2,1)} collective-permute-done((bf16[144,640]{0,1:T(8,128)(2,1)}, bf16[144,640]{0,1:T(8,128)(2,1)}, u32[]{:S(2)}, u32[]{:S(2)}) %collective-permute-start.6) | collective-permute-done | bytes 184352 | tf_op jit(solution)/shard_map/ppermute | solution.py:174
  67.1 3.9 collective-permute-done.8
  77.1 4.1 collective-permute-done.5
  83.1 5.2 collective-permute-done.7
  90.1 5.2 collective-permute-done.9
  118.3 3.5 fusion.9
  121.8 6.3 fusion.48
  131.6 5.0 fusion.58
  136.9 13.6 %shard_map.280 = (bf16[2048,256]{1,0:T(8,128)(2,1)S(1)}, bf16[2048,2048]{1,0:T(8,128)(2,1)}) custom-call(bf16[2048,256]{1,0:T(8,128)(2,1)S(1)} %pad_maximum_fusion.14.q_ref, bf16[2048,256]{1,0:T(8,128)(2,1)S(1)} %pad_maximum_fusion.15.k_ref, bf16[2048,256]{1,0:T(8,128)(2,1)S(1)} %slice.745.v_ref, f32[1,2048]{1,0:T(1,128)S(1)} %fusion.82.code_ref, ...), custom_call_target="tpu_custom_call" | custom-call | flops 4294967296 | bytes 12582912 | tf_op jit(solution)/shard_map/pallas_call | solution.py:78
  160.6 4.9 collective-permute-done.12
  173.9 25.7 %all-gather.9.cloned.1.call-done = bf16[576,1728]{1,0:T(8,128)(2,1)} async-done(((bf16[144,1728]{1,0:T(8,128)(2,1)}), bf16[576,1728]{1,0:T(8,128)(2,1)}) %all-gather.9.cloned.1.call-update) | async-done | bytes 1990672 | tf_op jit(solution)/shard_map/all_gather | solution.py:179
  204.7 8.2 %collective-permute-done.19 = bf16[4,144,1728]{2,1,0:T(8,128)(2,1)} collective-permute-done((bf16[4,144,1728]{2,1,0:T(8,128)(2,1)}, bf16[4,144,1728]{2,1,0:T(8,128)(2,1)}, u32[]{:S(2)}, u32[]{:S(2)}) %collective-permute-start.19) | collective-permute-done | bytes 1990688 | tf_op jit(solution)/shard_map/ppermute | solution.py:171
  216.3 40.8 %collective-permute-done.20 = bf16[4,144,1728]{2,1,0:T(8,128)(2,1)} collective-permute-done((bf16[4,144,1728]{2,1,0:T(8,128)(2,1)}, bf16[4,144,1728]{2,1,0:T(8,128)(2,1)}, u32[]{:S(2)}, u32[]{:S(2)}) %collective-permute-start.20) | collective-permute-done | bytes 1990688 | tf_op jit(solution)/shard_map/ppermute | solution.py:171
  261.6 13.1 %convolution_convert_fusion.2 = bf16[2048,1728]{0,1:T(8,128)(2,1)} fusion(bf16[1152,1728]{1,0:T(8,128)(2,1)S(1)} %bitcast.219, bf16[512,1152]{1,0:T(8,128)(2,1)} %collective-permute-done.18, bf16[512,1152]{1,0:T(8,128)(2,1)} %collective-permute-done.17, bf16[512,1152]{1,0:T(8,128)(2,1)S(1)} %collective-permute-done.16, ...), kind=kOutput, calls=%fused_computation.24 | convolution fusion | flops 8176140288 | bytes 15777792 | tf_op jit(solution)/shard_map/dot_general | solution.py:42
  274.7 22.0 %multiply_convert_fusion.1 = (bf16[2048,1728]{0,1:T(8,128)(2,1)}, bf16[2048,1728]{0,1:T(8,128)(2,1)}) fusion(bf16[2048,1728]{0,1:T(8,128)(2,1)} %convolution_convert_fusion.2, bf16[1152,1728]{1,0:T(8,128)(2,1)} %bitcast.221, bf16[512,1152]{1,0:T(8,128)(2,1)} %collective-permute-done.18, bf16[512,1152]{1,0:T(8,128)(2,1)} %collective-permute-done.17, ...), kind=kOutput, calls=%fused_computation.15 | convolution fusion | flops 8215068672 | bytes 29933568 | tf_op jit(solution)/shard_map/dot_general | solution.py:42
  296.7 13.4 %convolution_convert_fusion.1 = bf16[2048,1152]{1,0:T(8,128)(2,1)S(1)} fusion(bf16[2048,1728]{0,1:T(8,128)(2,1)} %get-tuple-element.307, bf16[1728,1152]{1,0:T(8,128)(2,1)} %all-gather.11.cloned.1.call-done), kind=kOutput, calls=%fused_computation.23 | convolution fusion | flops 8156086272 | bytes 15777792 | tf_op jit(solution)/shard_map/dot_general | solution.py:42
  316.2 25.9 %collective-permute-done.24 = bf16[512,1152]{1,0:T(8,128)(2,1)S(1)} collective-permute-done((bf16[512,1152]{1,0:T(8,128)(2,1)S(1)}, bf16[512,1152]{1,0:T(8,128)(2,1)S(1)}, u32[]{:S(2)}, u32[]{:S(2)}) %collective-permute-start.24) | collective-permute-done | bytes 1179680 | tf_op jit(solution)/shard_map/ppermute | solution.py:138
  348.8 23.7 %collective-permute-done.26 = bf16[512,1152]{1,0:T(8,128)(2,1)} collective-permute-done((bf16[512,1152]{1,0:T(8,128)(2,1)S(1)}, bf16[512,1152]{1,0:T(8,128)(2,1)}, u32[]{:S(2)}, u32[]{:S(2)}) %collective-permute-start.26) | collective-permute-done | bytes 1179680 | tf_op jit(solution)/shard_map/ppermute | solution.py:138
  377.4 28.8 %multiply_convert_fusion = (bf16[2048,1728]{0,1:T(8,128)(2,1)}, bf16[2048,1728]{0,1:T(8,128)(2,1)}) fusion(bf16[2048,1728]{0,1:T(8,128)(2,1)} %convolution_convert_fusion.2, bf16[2048,1728]{0,1:T(8,128)(2,1)} %get-tuple-element.308, bf16[1728,1152]{1,0:T(8,128)(2,1)} %all-gather.11.cloned.1.call-done, bf16[512,1152]{1,0:T(8,128)(2,1)} %collective-permute-done.27, ...), kind=kOutput, calls=%fused_computation.14 | convolution fusion | flops 8264613888 | bytes 37011456 | tf_op jit(solution)/shard_map/dot_general | solution.py:50
  406.3 16.0 %fusion.109 = f32[2048,1152]{1,0:T(8,128)} fusion(bf16[2048,1728]{0,1:T(8,128)(2,1)} %get-tuple-element.124, bf16[1152,1728]{1,0:T(8,128)(2,1)} %bitcast.220), kind=kOutput, calls=%fused_computation.324 | convolution fusion | flops 8153726976 | bytes 20496384 | tf_op jit(solution)/shard_map/dot_general | solution.py:50
  422.4 12.5 %convolution_convert_fusion.3 = bf16[1152,1728]{0,1:T(8,128)(2,1)} fusion(bf16[2048,1728]{0,1:T(8,128)(2,1)S(1)} %copy-done.128, bf16[512,1152]{1,0:T(8,128)(2,1)} %collective-permute-done.18, bf16[512,1152]{1,0:T(8,128)(2,1)} %collective-permute-done.17, bf16[512,1152]{1,0:T(8,128)(2,1)S(1)} %copy-done.127, bf16[512,1152]{1,0:T(8,128)(2,1)S(1)} %copy-done.40), kind=kOutput, calls=%fused_computation.25 | convolution fusion | flops 8174592000 | bytes 15777792 | tf_op jit(solution)/shard_map/dot_general | solution.py:46
  434.8 6.4 copy.205
  444.0 13.6 %add_convert_fusion = bf16[2048,1152]{1,0:T(8,128)(2,1)S(1)} fusion(f32[2048,1152]{1,0:T(8,128)} %fusion.109, bf16[2048,1728]{0,1:T(8,128)(2,1)} %get-tuple-element.123, bf16[1152,1728]{1,0:T(8,128)(2,1)S(1)} %bitcast.222), kind=kOutput, calls=%fused_computation.21 | convolution fusion | flops 8158445568 | bytes 25214976 | tf_op jit(solution)/shard_map/dot_general | solution.py:50
  461.7 27.6 %collective-permute-done.43 = bf16[4,144,1728]{2,1,0:T(8,128)(2,1)S(1)} collective-permute-done((bf16[4,144,1728]{2,1,0:T(8,128)(2,1)S(1)}, bf16[4,144,1728]{2,1,0:T(8,128)(2,1)S(1)}, u32[]{:S(2)}, u32[]{:S(2)}) %collective-permute-start.43) | collective-permute-done | bytes 1990688 | tf_op jit(solution)/shard_map/ppermute | solution.py:171
  491.2 14.3 %convolution_convert_fusion.4 = bf16[1152,1728]{0,1:T(8,128)(2,1)} fusion(bf16[2048,1728]{0,1:T(8,128)(2,1)} %get-tuple-element.124, bf16[512,1152]{1,0:T(8,128)(2,1)} %collective-permute-done.18, bf16[512,1152]{1,0:T(8,128)(2,1)} %collective-permute-done.17, bf16[512,1152]{1,0:T(8,128)(2,1)} %copy-done.126, bf16[512,1152]{1,0:T(8,128)(2,1)} %copy-done.39), kind=kOutput, calls=%fused_computation.26 | convolution fusion | flops 8174592000 | bytes 15777792 | tf_op jit(solution)/shard_map/dot_general | solution.py:46
  505.5 6.5 copy.204
  518.3 13.9 %convolution_convert_fusion.5 = bf16[1728,1152]{1,0:T(8,128)(2,1)} fusion(bf16[2048,1728]{0,1:T(8,128)(2,1)} %get-tuple-element.307, bf16[512,1152]{1,0:T(8,128)(2,1)} %collective-permute-done.27, bf16[512,1152]{1,0:T(8,128)(2,1)} %collective-permute-done.26, bf16[512,1152]{1,0:T(8,128)(2,1)} %collective-permute-done.25, ...), kind=kOutput, calls=%fused_computation.27 | convolution fusion | flops 8174592000 | bytes 15777792 | tf_op jit(solution)/shard_map/dot_general | solution.py:46
  532.2 26.8 %collective-permute-done.42 = bf16[4,144,1728]{2,1,0:T(8,128)(2,1)S(1)} collective-permute-done((bf16[4,144,1728]{2,1,0:T(8,128)(2,1)S(1)}, bf16[4,144,1728]{2,1,0:T(8,128)(2,1)S(1)}, u32[]{:S(2)}, u32[]{:S(2)}) %collective-permute-start.42) | collective-permute-done | bytes 1990688 | tf_op jit(solution)/shard_map/ppermute | solution.py:171
  564.0 3.7 multiply_reduce_fusion
  573.6 3.4 collective-permute-start.33
  579.7 4.6 collective-permute-done.33
  584.3 5.5 collective-permute-done.32
  589.9 16.5 %shard_map.281 = (bf16[2048,256]{1,0:T(8,128)(2,1)S(1)}, f32[2048,256]{1,0:T(8,128)}, f32[2048,256]{1,0:T(8,128)}) custom-call(bf16[2048,256]{1,0:T(8,128)(2,1)S(1)} %copy-done.5, bf16[2048,256]{1,0:T(8,128)(2,1)S(1)} %copy-done.7, bf16[2048,256]{1,0:T(8,128)(2,1)S(1)} %copy-done.3, bf16[2048,2048]{1,0:T(8,128)(2,1)} %get-tuple-element.21.p_ref, ...), custom_call_target="tpu_custom_call" | custom-call | flops 8589934592 | bytes 18874368 | tf_op jit(solution)/shard_map/pallas_call | solution.py:118
  610.1 4.8 fusion.61
  618.4 4.9 convolution_convert_fusion
  630.2 7.6 convolution_convert_fusion.7
  645.1 10.7 %collective-permute-done.49 = bf16[8,32,1152]{2,1,0:T(8,128)(2,1)} collective-permute-done((bf16[8,32,1152]{2,1,0:T(8,128)(2,1)}, bf16[8,32,1152]{2,1,0:T(8,128)(2,1)}, u32[]{:S(2)}, u32[]{:S(2)}) %collective-permute-start.49) | collective-permute-done | bytes 589856 | tf_op jit(solution)/shard_map/ppermute | solution.py:138
  676.8 11.4 %collective-permute-done.40 = bf16[144,640]{0,1:T(8,128)(2,1)S(1)} collective-permute-done((bf16[144,640]{0,1:T(8,128)(2,1)S(1)}, bf16[144,640]{0,1:T(8,128)(2,1)S(1)}, u32[]{:S(2)}, u32[]{:S(2)}) %collective-permute-start.40) | collective-permute-done | bytes 184352 | tf_op jit(solution)/shard_map/ppermute | solution.py:174
  688.2 7.0 collective-permute-done.39
  697.6 13.6 %collective-permute-done.50 = bf16[4,248,1152]{2,1,0:T(8,128)(2,1)} collective-permute-done((bf16[4,248,1152]{2,1,0:T(8,128)(2,1)}, bf16[4,248,1152]{2,1,0:T(8,128)(2,1)}, u32[]{:S(2)}, u32[]{:S(2)}) %collective-permute-start.50) | collective-permute-done | bytes 2285600 | tf_op jit(solution)/shard_map/ppermute | solution.py:171
  711.2 3.7 fusion.12
  726.4 4.5 fusion.22
  739.8 11.9 %collective-permute-done.55 = bf16[144,3456]{1,0:T(8,128)(2,1)} collective-permute-done((bf16[144,3456]{1,0:T(8,128)(2,1)}, bf16[144,3456]{1,0:T(8,128)(2,1)}, u32[]{:S(2)}, u32[]{:S(2)}) %collective-permute-start.55) | collective-permute-done | bytes 995360 | tf_op jit(solution)/shard_map/ppermute | solution.py:138
  770.2 9.2 %collective-permute-done.52 = bf16[248,1152]{1,0:T(8,128)(2,1)S(1)} collective-permute-done((bf16[248,1152]{1,0:T(8,128)(2,1)}, bf16[248,1152]{1,0:T(8,128)(2,1)S(1)}, u32[]{:S(2)}, u32[]{:S(2)}) %collective-permute-start.52) | collective-permute-done | bytes 571424 | tf_op jit(solution)/shard_map/ppermute | solution.py:138
  784.7 4.1 concatenate.264
  791.0 4.1 concatenate.265
  (544 shorter events, 241.6 us)
Async XLA Ops:
  7.3 110.4 %all-gather.5.cloned.1.call-start = ((), (), s32[]{:S(2)}) async-start(), calls=%async_computation.3 | async-start | bytes 1474560 | tf_op jit(solution)/shard_map/all_gather | solution.py:179
  15.0 151.8 %all-gather.7.cloned.1.call-start = ((), (), s32[]{:S(2)}) async-start(), calls=%async_computation.4 | async-start | bytes 2580480 | tf_op jit(solution)/shard_map/all_gather | solution.py:179
  18.9 17.9 %collective-permute-start.3 = (bf16[144,640]{0,1:T(8,128)(2,1)}, bf16[144,640]{0,1:T(8,128)(2,1)}, u32[]{:S(2)}, u32[]{:S(2)}) collective-permute-start(bf16[144,640]{0,1:T(8,128)(2,1)} %pad_maximum_fusion.26), channel_id=1, source_target_pairs={{0,4},{4,0},{8,12},{12,8},{16,20},{20,16},{24,28},{28,24},{1,5},{5... | collective-permute-start | bytes 552968 | tf_op jit(solution)/shard_map/ppermute | solution.py:171
  20.1 21.3 %collective-permute-start.4 = (bf16[144,640]{0,1:T(8,128)(2,1)}, bf16[144,640]{0,1:T(8,128)(2,1)}, u32[]{:S(2)}, u32[]{:S(2)}) collective-permute-start(bf16[144,640]{0,1:T(8,128)(2,1)} %pad_maximum_fusion.26), channel_id=1, source_target_pairs={{0,8},{4,12},{8,16},{12,20},{16,24},{20,28},{24,0},{28,4},{1,9},{5... | collective-permute-start | bytes 552968 | tf_op jit(solution)/shard_map/ppermute | solution.py:174
  21.4 43.9 %collective-permute-start.6 = (bf16[144,640]{0,1:T(8,128)(2,1)}, bf16[144,640]{0,1:T(8,128)(2,1)}, u32[]{:S(2)}, u32[]{:S(2)}) collective-permute-start(bf16[144,640]{0,1:T(8,128)(2,1)} %pad_maximum_fusion.26), channel_id=1, source_target_pairs={{0,16},{4,20},{8,24},{12,28},{16,0},{20,4},{24,8},{28,12},{1,17},{... | collective-permute-start | bytes 552968 | tf_op jit(solution)/shard_map/ppermute | solution.py:174
  22.4 48.6 %collective-permute-start.8 = (bf16[144,640]{0,1:T(8,128)(2,1)}, bf16[144,640]{0,1:T(8,128)(2,1)}, u32[]{:S(2)}, u32[]{:S(2)}) collective-permute-start(bf16[144,640]{0,1:T(8,128)(2,1)} %pad_maximum_fusion.26), channel_id=1, source_target_pairs={{0,24},{4,28},{8,0},{12,4},{16,8},{20,12},{24,16},{28,20},{1,25},{... | collective-permute-start | bytes 552968 | tf_op jit(solution)/shard_map/ppermute | solution.py:174
  23.9 88.3 %collective-permute-start.1 = (bf16[512,1152]{1,0:T(8,128)(2,1)S(1)}, bf16[512,1152]{1,0:T(8,128)(2,1)}, u32[]{:S(2)}, u32[]{:S(2)}) collective-permute-start(bf16[512,1152]{1,0:T(8,128)(2,1)S(1)} %copy-done.13), channel_id=1, source_target_pairs={{0,2},{1,3},{2,0},{3,1},{4,6},{5,7},{6,4},{7,5},{8,10},{9,11},{10,... | collective-permute-start | bytes 3538952 | tf_op jit(solution)/shard_map/ppermute | solution.py:138
  29.7 169.8 %all-gather.9.cloned.1.call-start = ((), (), s32[]{:S(2)}) async-start(), calls=%async_computation.5 | async-start | bytes 2580480 | tf_op jit(solution)/shard_map/all_gather | solution.py:179
  36.8 81.5 %collective-permute-start = (bf16[512,1152]{1,0:T(8,128)(2,1)S(1)}, bf16[512,1152]{1,0:T(8,128)(2,1)}, u32[]{:S(2)}, u32[]{:S(2)}) collective-permute-start(bf16[512,1152]{1,0:T(8,128)(2,1)S(1)} %copy-done.13), channel_id=1, source_target_pairs={{0,1},{1,0},{2,3},{3,2},{4,5},{5,4},{6,7},{7,6},{8,9},{9,8},{10,11... | collective-permute-start | bytes 3538952 | tf_op jit(solution)/shard_map/ppermute | solution.py:138
  72.5 15.9 %collective-permute-start.7 = (bf16[144,640]{0,1:T(8,128)(2,1)}, bf16[144,640]{0,1:T(8,128)(2,1)}, u32[]{:S(2)}, u32[]{:S(2)}) collective-permute-start(bf16[144,640]{0,1:T(8,128)(2,1)} %collective-permute-done.6), channel_id=1, source_target_pairs={{0,4},{4,0},{8,12},{12,8},{16,20},{20,16},{24,28},{28,24},{1,5},{5... | collective-permute-start | bytes 552968 | tf_op jit(solution)/shard_map/ppermute | solution.py:171
  73.7 21.7 %collective-permute-start.9 = (bf16[144,640]{0,1:T(8,128)(2,1)}, bf16[144,640]{0,1:T(8,128)(2,1)}, u32[]{:S(2)}, u32[]{:S(2)}) collective-permute-start(bf16[144,640]{0,1:T(8,128)(2,1)} %collective-permute-done.8), channel_id=1, source_target_pairs={{0,4},{4,0},{8,12},{12,8},{16,20},{20,16},{24,28},{28,24},{1,5},{5... | collective-permute-start | bytes 552968 | tf_op jit(solution)/shard_map/ppermute | solution.py:171
  117.7 49.5 %collective-permute-start.15 = (bf16[512,1152]{1,0:T(8,128)(2,1)}, bf16[512,1152]{1,0:T(8,128)(2,1)}, u32[]{:S(2)}, u32[]{:S(2)}) collective-permute-start(bf16[512,1152]{1,0:T(8,128)(2,1)} %all-gather.5.cloned.1.call-done), channel_id=1, source_target_pairs={{0,1},{1,0},{2,3},{3,2},{4,5},{5,4},{6,7},{7,6},{8,9},{9,8},{10,11... | collective-permute-start | bytes 3538952 | tf_op jit(solution)/shard_map/ppermute | solution.py:138
  152.8 12.7 %collective-permute-start.12 = (bf16[512,256]{1,0:T(8,128)(2,1)}, bf16[512,256]{1,0:T(8,128)(2,1)}, u32[]{:S(2)}, u32[]{:S(2)}) collective-permute-start(bf16[512,256]{1,0:T(8,128)(2,1)} %get-tuple-element.210), channel_id=1, source_target_pairs={{0,2},{1,3},{2,0},{3,1},{4,6},{5,7},{6,4},{7,5},{8,10},{9,11},{10,... | collective-permute-start | bytes 786440 | tf_op jit(solution)/shard_map/ppermute | solution.py:138
  155.6 45.1 %collective-permute-start.21 = (bf16[216,1152]{1,0:T(8,128)(2,1)}, bf16[216,1152]{1,0:T(8,128)(2,1)}, u32[]{:S(2)}, u32[]{:S(2)}) collective-permute-start(bf16[216,1152]{1,0:T(8,128)(2,1)} %dynamic-slice_convert_fusion), channel_id=1, source_target_pairs={{0,4},{4,0},{8,12},{12,8},{16,20},{20,16},{24,28},{28,24},{1,5},{5... | collective-permute-start | bytes 1493000 | tf_op jit(solution)/shard_map/ppermute | solution.py:171
  157.1 139.5 %all-gather.11.cloned.1.call-start = ((), (), s32[]{:S(2)}) async-start(), calls=%async_computation.6 | async-start | bytes 4976640 | tf_op jit(solution)/shard_map/all_gather | solution.py:179
  166.8 46.1 %collective-permute-start.19 = (bf16[4,144,1728]{2,1,0:T(8,128)(2,1)}, bf16[4,144,1728]{2,1,0:T(8,128)(2,1)}, u32[]{:S(2)}, u32[]{:S(2)}) collective-permute-start(bf16[4,144,1728]{2,1,0:T(8,128)(2,1)} %bitcast.231), channel_id=1, source_target_pairs={{0,4},{4,0},{8,12},{12,8},{16,20},{20,16},{24,28},{28,24},{1,5},{5... | collective-permute-start | bytes 5971976 | tf_op jit(solution)/shard_map/ppermute | solution.py:171
  172.7 31.9 %collective-permute-start.17 = (bf16[512,1152]{1,0:T(8,128)(2,1)S(1)}, bf16[512,1152]{1,0:T(8,128)(2,1)}, u32[]{:S(2)}, u32[]{:S(2)}) collective-permute-start(bf16[512,1152]{1,0:T(8,128)(2,1)S(1)} %multiply_convert_fusion.2), channel_id=1, source_target_pairs={{0,2},{1,3},{2,0},{3,1},{4,6},{5,7},{6,4},{7,5},{8,10},{9,11},{10,... | collective-permute-start | bytes 3538952 | tf_op jit(solution)/shard_map/ppermute | solution.py:138
  199.6 57.6 %collective-permute-start.20 = (bf16[4,144,1728]{2,1,0:T(8,128)(2,1)}, bf16[4,144,1728]{2,1,0:T(8,128)(2,1)}, u32[]{:S(2)}, u32[]{:S(2)}) collective-permute-start(bf16[4,144,1728]{2,1,0:T(8,128)(2,1)} %bitcast.233), channel_id=1, source_target_pairs={{0,4},{4,0},{8,12},{12,8},{16,20},{20,16},{24,28},{28,24},{1,5},{5... | collective-permute-start | bytes 5971976 | tf_op jit(solution)/shard_map/ppermute | solution.py:171
  203.3 515.1 %reduce-scatter.8.cloned.1.call-start = ((), (), s32[]{:S(2)}) async-start(), calls=%async_computation.8 | async-start | bytes 2580480 | tf_op jit(solution)/shard_map/reduce_scatter | solution.py:226
  203.4 58.2 %collective-permute-start.16 = (bf16[512,1152]{1,0:T(8,128)(2,1)S(1)}, bf16[512,1152]{1,0:T(8,128)(2,1)S(1)}, u32[]{:S(2)}, u32[]{:S(2)}) collective-permute-start(bf16[512,1152]{1,0:T(8,128)(2,1)S(1)} %multiply_convert_fusion.2), channel_id=1, source_target_pairs={{0,1},{1,0},{2,3},{3,2},{4,5},{5,4},{6,7},{7,6},{8,9},{9,8},{10,11... | collective-permute-start | bytes 3538952 | tf_op jit(solution)/shard_map/ppermute | solution.py:138
  204.7 56.9 %collective-permute-start.18 = (bf16[512,1152]{1,0:T(8,128)(2,1)}, bf16[512,1152]{1,0:T(8,128)(2,1)}, u32[]{:S(2)}, u32[]{:S(2)}) collective-permute-start(bf16[512,1152]{1,0:T(8,128)(2,1)} %collective-permute-done.17), channel_id=1, source_target_pairs={{0,1},{1,0},{2,3},{3,2},{4,5},{5,4},{6,7},{7,6},{8,9},{9,8},{10,11... | collective-permute-start | bytes 3538952 | tf_op jit(solution)/shard_map/ppermute | solution.py:138
  314.8 27.2 %collective-permute-start.24 = (bf16[512,1152]{1,0:T(8,128)(2,1)S(1)}, bf16[512,1152]{1,0:T(8,128)(2,1)S(1)}, u32[]{:S(2)}, u32[]{:S(2)}) collective-permute-start(bf16[512,1152]{1,0:T(8,128)(2,1)S(1)} %add_convert_fusion.4), channel_id=1, source_target_pairs={{0,2},{1,3},{2,0},{3,1},{4,6},{5,7},{6,4},{7,5},{8,10},{9,11},{10,... | collective-permute-start | bytes 3538952 | tf_op jit(solution)/shard_map/ppermute | solution.py:138
  346.1 26.4 %collective-permute-start.26 = (bf16[512,1152]{1,0:T(8,128)(2,1)S(1)}, bf16[512,1152]{1,0:T(8,128)(2,1)}, u32[]{:S(2)}, u32[]{:S(2)}) collective-permute-start(bf16[512,1152]{1,0:T(8,128)(2,1)S(1)} %get-tuple-element.125), channel_id=1, source_target_pairs={{0,2},{1,3},{2,0},{3,1},{4,6},{5,7},{6,4},{7,5},{8,10},{9,11},{10,... | collective-permute-start | bytes 3538952 | tf_op jit(solution)/shard_map/ppermute | solution.py:138
  347.4 27.9 %collective-permute-start.25 = (bf16[512,1152]{1,0:T(8,128)(2,1)S(1)}, bf16[512,1152]{1,0:T(8,128)(2,1)}, u32[]{:S(2)}, u32[]{:S(2)}) collective-permute-start(bf16[512,1152]{1,0:T(8,128)(2,1)S(1)} %get-tuple-element.125), channel_id=1, source_target_pairs={{0,1},{1,0},{2,3},{3,2},{4,5},{5,4},{6,7},{7,6},{8,9},{9,8},{10,11... | collective-permute-start | bytes 3538952 | tf_op jit(solution)/shard_map/ppermute | solution.py:138
  443.1 46.2 %collective-permute-start.43 = (bf16[4,144,1728]{2,1,0:T(8,128)(2,1)S(1)}, bf16[4,144,1728]{2,1,0:T(8,128)(2,1)S(1)}, u32[]{:S(2)}, u32[]{:S(2)}) collective-permute-start(bf16[4,144,1728]{2,1,0:T(8,128)(2,1)S(1)} %dynamic-slice_bitcast_fusion), channel_id=1, source_target_pairs={{0,4},{4,0},{8,12},{12,8},{16,20},{20,16},{24,28},{28,24},{1,5},{5... | collective-permute-start | bytes 5971976 | tf_op jit(solution)/shard_map/ppermute | solution.py:171
  461.2 53.0 %collective-permute-start.29 = (bf16[512,1152]{1,0:T(8,128)(2,1)}, bf16[512,1152]{1,0:T(8,128)(2,1)}, u32[]{:S(2)}, u32[]{:S(2)}) collective-permute-start(bf16[512,1152]{1,0:T(8,128)(2,1)} %get-tuple-element.134), channel_id=1, source_target_pairs={{0,1},{1,0},{2,3},{3,2},{4,5},{5,4},{6,7},{7,6},{8,9},{9,8},{10,11... | collective-permute-start | bytes 3538952 | tf_op jit(solution)/shard_map/ppermute | solution.py:138
  461.5 99.4 %collective-permute-start.28 = (bf16[512,1152]{1,0:T(8,128)(2,1)}, bf16[512,1152]{1,0:T(8,128)(2,1)}, u32[]{:S(2)}, u32[]{:S(2)}) collective-permute-start(bf16[512,1152]{1,0:T(8,128)(2,1)} %get-tuple-element.133), channel_id=1, source_target_pairs={{0,1},{1,0},{2,3},{3,2},{4,5},{5,4},{6,7},{7,6},{8,9},{9,8},{10,11... | collective-permute-start | bytes 3538952 | tf_op jit(solution)/shard_map/ppermute | solution.py:138
  491.1 227.3 %reduce-scatter.6.cloned.1.call-start = ((), (), s32[]{:S(2)}) async-start(), calls=%async_computation.7 | async-start | bytes 2580480 | tf_op jit(solution)/shard_map/reduce_scatter | solution.py:226
  513.7 45.3 %collective-permute-start.42 = (bf16[4,144,1728]{2,1,0:T(8,128)(2,1)S(1)}, bf16[4,144,1728]{2,1,0:T(8,128)(2,1)S(1)}, u32[]{:S(2)}, u32[]{:S(2)}) collective-permute-start(bf16[4,144,1728]{2,1,0:T(8,128)(2,1)S(1)} %dynamic-slice_bitcast_fusion.1), channel_id=1, source_target_pairs={{0,4},{4,0},{8,12},{12,8},{16,20},{20,16},{24,28},{28,24},{1,5},{5... | collective-permute-start | bytes 5971976 | tf_op jit(solution)/shard_map/ppermute | solution.py:171
  517.1 43.9 %collective-permute-start.30 = (bf16[512,1152]{1,0:T(8,128)(2,1)}, bf16[512,1152]{1,0:T(8,128)(2,1)}, u32[]{:S(2)}, u32[]{:S(2)}) collective-permute-start(bf16[512,1152]{1,0:T(8,128)(2,1)} %add_convert_fusion.2), channel_id=1, source_target_pairs={{0,2},{1,3},{2,0},{3,1},{4,6},{5,7},{6,4},{7,5},{8,10},{9,11},{10,... | collective-permute-start | bytes 3538952 | tf_op jit(solution)/shard_map/ppermute | solution.py:138
  560.9 203.8 %reduce-scatter.10.cloned.1.call-start = ((), (), s32[]{:S(2)}) async-start(), calls=%async_computation.9 | async-start | bytes 2856960
  577.0 12.7 %collective-permute-start.32 = (bf16[512,256]{1,0:T(8,128)(2,1)S(1)}, bf16[512,256]{1,0:T(8,128)(2,1)S(1)}, u32[]{:S(2)}, u32[]{:S(2)}) collective-permute-start(bf16[512,256]{1,0:T(8,128)(2,1)S(1)} %get-tuple-element.202), channel_id=1, source_target_pairs={{0,2},{1,3},{2,0},{3,1},{4,6},{5,7},{6,4},{7,5},{8,10},{9,11},{10,... | collective-permute-start | bytes 786440 | tf_op jit(solution)/shard_map/ppermute | solution.py:138
  577.3 12.5 %collective-permute-start.31 = (bf16[512,256]{1,0:T(8,128)(2,1)S(1)}, bf16[512,256]{1,0:T(8,128)(2,1)S(1)}, u32[]{:S(2)}, u32[]{:S(2)}) collective-permute-start(bf16[512,256]{1,0:T(8,128)(2,1)S(1)} %get-tuple-element.203), channel_id=1, source_target_pairs={{0,1},{1,0},{2,3},{3,2},{4,5},{5,4},{6,7},{7,6},{8,9},{9,8},{10,11... | collective-permute-start | bytes 786440 | tf_op jit(solution)/shard_map/ppermute | solution.py:138
  579.2 59.4 %collective-permute-start.48 = (bf16[8,32,1152]{2,1,0:T(8,128)(2,1)}, bf16[8,32,1152]{2,1,0:T(8,128)(2,1)}, u32[]{:S(2)}, u32[]{:S(2)}) collective-permute-start(bf16[8,32,1152]{2,1,0:T(8,128)(2,1)} %get-tuple-element.162), channel_id=1, source_target_pairs={{0,1},{1,0},{2,3},{3,2},{4,5},{5,4},{6,7},{7,6},{8,9},{9,8},{10,11... | collective-permute-start | bytes 1769480 | tf_op jit(solution)/shard_map/ppermute | solution.py:138
  579.5 65.6 %collective-permute-start.47 = (bf16[8,32,1152]{2,1,0:T(8,128)(2,1)}, bf16[8,32,1152]{2,1,0:T(8,128)(2,1)}, u32[]{:S(2)}, u32[]{:S(2)}) collective-permute-start(bf16[8,32,1152]{2,1,0:T(8,128)(2,1)} %get-tuple-element.161), channel_id=1, source_target_pairs={{0,1},{1,0},{2,3},{3,2},{4,5},{5,4},{6,7},{7,6},{8,9},{9,8},{10,11... | collective-permute-start | bytes 1769480 | tf_op jit(solution)/shard_map/ppermute | solution.py:138
  627.1 40.0 %collective-permute-start.35 = (bf16[512,1152]{1,0:T(8,128)(2,1)}, bf16[512,1152]{1,0:T(8,128)(2,1)}, u32[]{:S(2)}, u32[]{:S(2)}) collective-permute-start(bf16[512,1152]{1,0:T(8,128)(2,1)} %get-tuple-element.132), channel_id=1, source_target_pairs={{0,1},{1,0},{2,3},{3,2},{4,5},{5,4},{6,7},{7,6},{8,9},{9,8},{10,11... | collective-permute-start | bytes 3538952 | tf_op jit(solution)/shard_map/ppermute | solution.py:138
  640.7 15.1 %collective-permute-start.49 = (bf16[8,32,1152]{2,1,0:T(8,128)(2,1)}, bf16[8,32,1152]{2,1,0:T(8,128)(2,1)}, u32[]{:S(2)}, u32[]{:S(2)}) collective-permute-start(bf16[8,32,1152]{2,1,0:T(8,128)(2,1)} %fusion.50), channel_id=1, source_target_pairs={{0,2},{1,3},{2,0},{3,1},{4,6},{5,7},{6,4},{7,5},{8,10},{9,11},{10,... | collective-permute-start | bytes 1769480 | tf_op jit(solution)/shard_map/ppermute | solution.py:138
  644.8 17.4 %collective-permute-start.38 = (bf16[4,144,640]{2,1,0:T(8,128)(2,1)S(1)}, bf16[4,144,640]{2,1,0:T(8,128)(2,1)}, u32[]{:S(2)}, u32[]{:S(2)}) collective-permute-start(bf16[4,144,640]{2,1,0:T(8,128)(2,1)S(1)} %get-tuple-element.184), channel_id=1, source_target_pairs={{0,4},{4,0},{8,12},{12,8},{16,20},{20,16},{24,28},{28,24},{1,5},{5... | collective-permute-start | bytes 2211848 | tf_op jit(solution)/shard_map/ppermute | solution.py:171
  659.0 52.2 %collective-permute-start.50 = (bf16[4,248,1152]{2,1,0:T(8,128)(2,1)}, bf16[4,248,1152]{2,1,0:T(8,128)(2,1)}, u32[]{:S(2)}, u32[]{:S(2)}) collective-permute-start(bf16[4,248,1152]{2,1,0:T(8,128)(2,1)} %fusion.26), channel_id=1, source_target_pairs={{0,4},{4,0},{8,12},{12,8},{16,20},{20,16},{24,28},{28,24},{1,5},{5... | collective-permute-start | bytes 6856712 | tf_op jit(solution)/shard_map/ppermute | solution.py:171
  659.2 55.7 %collective-permute-start.34 = (bf16[512,1152]{1,0:T(8,128)(2,1)}, bf16[512,1152]{1,0:T(8,128)(2,1)}, u32[]{:S(2)}, u32[]{:S(2)}) collective-permute-start(bf16[512,1152]{1,0:T(8,128)(2,1)} %get-tuple-element.131), channel_id=1, source_target_pairs={{0,1},{1,0},{2,3},{3,2},{4,5},{5,4},{6,7},{7,6},{8,9},{9,8},{10,11... | collective-permute-start | bytes 3538952 | tf_op jit(solution)/shard_map/ppermute | solution.py:138
  666.7 21.6 %collective-permute-start.40 = (bf16[144,640]{0,1:T(8,128)(2,1)S(1)}, bf16[144,640]{0,1:T(8,128)(2,1)S(1)}, u32[]{:S(2)}, u32[]{:S(2)}) collective-permute-start(bf16[144,640]{0,1:T(8,128)(2,1)S(1)} %get-tuple-element.193), channel_id=1, source_target_pairs={{0,16},{4,20},{8,24},{12,28},{16,0},{20,4},{24,8},{28,12},{1,17},{... | collective-permute-start | bytes 552968 | tf_op jit(solution)/shard_map/ppermute | solution.py:174
  667.1 28.2 %collective-permute-start.39 = (bf16[144,640]{0,1:T(8,128)(2,1)S(1)}, bf16[144,640]{0,1:T(8,128)(2,1)S(1)}, u32[]{:S(2)}, u32[]{:S(2)}) collective-permute-start(bf16[144,640]{0,1:T(8,128)(2,1)S(1)} %get-tuple-element.191), channel_id=1, source_target_pairs={{0,8},{4,12},{8,16},{12,20},{16,24},{20,28},{24,0},{28,4},{1,9},{5... | collective-permute-start | bytes 552968 | tf_op jit(solution)/shard_map/ppermute | solution.py:174
  674.9 40.0 %collective-permute-start.36 = (bf16[512,1152]{1,0:T(8,128)(2,1)}, bf16[512,1152]{1,0:T(8,128)(2,1)}, u32[]{:S(2)}, u32[]{:S(2)}) collective-permute-start(bf16[512,1152]{1,0:T(8,128)(2,1)} %add_convert_fusion.1), channel_id=1, source_target_pairs={{0,2},{1,3},{2,0},{3,1},{4,6},{5,7},{6,4},{7,5},{8,10},{9,11},{10,... | collective-permute-start | bytes 3538952 | tf_op jit(solution)/shard_map/ppermute | solution.py:138
  726.4 25.3 %collective-permute-start.55 = (bf16[144,3456]{1,0:T(8,128)(2,1)}, bf16[144,3456]{1,0:T(8,128)(2,1)}, u32[]{:S(2)}, u32[]{:S(2)}) collective-permute-start(bf16[144,3456]{1,0:T(8,128)(2,1)} %pad_maximum_fusion.20), channel_id=1, source_target_pairs={{0,2},{1,3},{2,0},{3,1},{4,6},{5,7},{6,4},{7,5},{8,10},{9,11},{10,... | collective-permute-start | bytes 2985992 | tf_op jit(solution)/shard_map/ppermute | solution.py:138
  732.9 28.3 %collective-permute-start.54 = (bf16[144,3456]{1,0:T(8,128)(2,1)}, bf16[144,3456]{1,0:T(8,128)(2,1)}, u32[]{:S(2)}, u32[]{:S(2)}) collective-permute-start(bf16[144,3456]{1,0:T(8,128)(2,1)} %pad_maximum_fusion.20), channel_id=1, source_target_pairs={{0,1},{1,0},{2,3},{3,2},{4,5},{5,4},{6,7},{7,6},{8,9},{9,8},{10,11... | collective-permute-start | bytes 2985992 | tf_op jit(solution)/shard_map/ppermute | solution.py:138
  764.7 14.8 %collective-permute-start.52 = (bf16[248,1152]{1,0:T(8,128)(2,1)}, bf16[248,1152]{1,0:T(8,128)(2,1)S(1)}, u32[]{:S(2)}, u32[]{:S(2)}) collective-permute-start(bf16[248,1152]{1,0:T(8,128)(2,1)} %reduce-scatter.10.cloned.1.call-done), channel_id=1, source_target_pairs={{0,2},{1,3},{2,0},{3,1},{4,6},{5,7},{6,4},{7,5},{8,10},{9,11},{10,... | collective-permute-start | bytes 1714184 | tf_op jit(solution)/shard_map/ppermute | solution.py:138
  769.9 27.5 %collective-permute-start.51 = (bf16[248,1152]{1,0:T(8,128)(2,1)S(1)}, bf16[248,1152]{1,0:T(8,128)(2,1)}, u32[]{:S(2)}, u32[]{:S(2)}) collective-permute-start(bf16[248,1152]{1,0:T(8,128)(2,1)S(1)} %copy-done.55), channel_id=1, source_target_pairs={{0,1},{1,0},{2,3},{3,2},{4,5},{5,4},{6,7},{7,6},{8,9},{9,8},{10,11... | collective-permute-start | bytes 1714184 | tf_op jit(solution)/shard_map/ppermute | solution.py:138
  779.4 17.9 %collective-permute-start.53 = (bf16[248,1152]{1,0:T(8,128)(2,1)S(1)}, bf16[248,1152]{1,0:T(8,128)(2,1)}, u32[]{:S(2)}, u32[]{:S(2)}) collective-permute-start(bf16[248,1152]{1,0:T(8,128)(2,1)S(1)} %collective-permute-done.52), channel_id=1, source_target_pairs={{0,1},{1,0},{2,3},{3,2},{4,5},{5,4},{6,7},{7,6},{8,9},{9,8},{10,11... | collective-permute-start | bytes 1714184 | tf_op jit(solution)/shard_map/ppermute | solution.py:138
  (147 other events, 1440.5 us)
Sparse Core Ops, SparseCore 0:
  15.2 52.5 all-gather.4
  69.3 44.9 all-gather.6
  157.3 42.2 all-gather.8
  203.5 74.5 all-gather.10
  491.3 39.9 reduce-scatter.7
  561.0 40.8 reduce-scatter.5
  715.0 45.3 reduce-scatter.9

commit v2 on v1

v2 whole, which is shorter than its diff:
```python
from functools import partial

import jax
import jax.numpy as jnp
from jax import lax
from jax.experimental import pallas as pl
from jax.experimental.pallas import tpu as pltpu
from jax.sharding import PartitionSpec as P

epsilon = 1e-06
f32 = jnp.float32
bf16 = jnp.bfloat16
SEQ = 4


def rms_scale(values, gain):
    return values * lax.rsqrt(jnp.mean(values * values, axis=-1, keepdims=True) + epsilon) * gain


def rotate(values, cosine, sine):
    half_width = values.shape[-1] // 2
    first_half = values[..., :half_width]
    second_half = values[..., half_width:]
    return jnp.concatenate(
        [first_half * cosine - second_half * sine, second_half * cosine + first_half * sine],
        axis=-1,
    )


def rope_tables(places, width):
    half_width = width // 2
    inverse = 1.0 / 1000000.0 ** (jnp.arange(half_width, dtype=f32) * 2.0 / width)
    angles = places.astype(f32)[:, None] * inverse[None, :]
    return (jnp.cos(angles), jnp.sin(angles))


def head_norm(raw, gain, cosine, sine):
    return rotate(rms_scale(raw, gain), cosine, sine)


def mult(left, right):
    return jnp.dot(left, right, preferred_element_type=f32)


def inner_rows(left, right):
    return lax.dot_general(left, right, (((0,), (0,)), ((), ())), preferred_element_type=f32)


def outer_cols(left, right):
    return lax.dot_general(left, right, (((1,), (1,)), ((), ())), preferred_element_type=f32)


def to_half(values):
    return values.astype(bf16)


def gated(gate_in, up_in):
    return jax.nn.gelu(gate_in, approximate=True) * up_in


MIB = 2**20


def held(shape):
    return pl.BlockSpec(shape, lambda *at: (0,) * len(shape), pipeline_mode=pl.Buffered(1))


def call(kernel, grid, in_specs, out_specs, outs, flops, limit=60, scratch=(), exps=0):
    shapes = [jax.ShapeDtypeStruct(s, d) for s, d in outs]
    size = sum(o.size * o.dtype.itemsize for o in shapes)
    made = pl.pallas_call(
        kernel,
        grid=grid,
        in_specs=in_specs,
        out_specs=out_specs,
        out_shape=shapes,
        scratch_shapes=list(scratch),
        compiler_params=pltpu.CompilerParams(vmem_limit_bytes=limit * MIB),
        cost_estimate=pl.CostEstimate(
            flops=flops // 50, bytes_accessed=size // 50, transcendentals=exps // 50
        ),
    )
    return lambda *operands: list(made(*operands))


def fused_kernel(function, ins, outs, sums, *refs):
    results = function(*[ref[...] for ref in refs[:ins]])
    for ref, value in zip(refs[ins : ins + outs], results[:outs], strict=True):
        ref[...] = value.astype(ref.dtype)
    for ref, value in zip(refs[ins + outs :], results[outs:], strict=True):

        @pl.when(pl.program_id(0) == 0)
        def _():
            ref[...] = jnp.zeros_like(ref)

        ref[...] += value


def fused(function, by_row, whole, outs, steps, sums=()):
    def split(shape):
        return pl.BlockSpec(
            (shape[0] // steps, *shape[1:]), lambda i: (i, *(0 for _ in shape[1:]))
        )

    return call(
        partial(fused_kernel, function, len(by_row) + len(whole), len(outs), len(sums)),
        (steps,),
        [split(v.shape) for v in by_row] + [held(v.shape) for v in whole],
        [split(s) for s, _ in outs] + [pl.BlockSpec(s, lambda i: (0, 0)) for s in sums],
        [*outs, *((s, f32) for s in sums)],
        flops=0,
    )(*by_row, *whole)


def add_half(first, second, steps):
    function = lambda a, b: (a.astype(f32) + b.astype(f32),)
    return fused(function, [first, second], [], [(first.shape, bf16)], steps)[0]


def rms_back(values, gain, grad):
    r = lax.rsqrt(jnp.mean(values * values, axis=-1, keepdims=True) + epsilon)
    scaled = grad * gain
    mean = jnp.mean(values * scaled, axis=-1, keepdims=True)
    return r * scaled - values * (r * r * r * mean), grad * values * r


def column_sum(values):
    return jnp.sum(values, axis=0, keepdims=True)


def mid_kernel(owners, quarters, me_ref, x_ref, *refs):
    heads = refs[:SEQ]
    weights = refs[SEQ : SEQ + quarters]
    gains_ref, all_ref, w_ref, attn_ref, mixed_ref, fed_ref = refs[SEQ + quarters :]
    width = heads[0].shape[1]
    for r, head in enumerate(heads):
        start = pl.multiple_of(jnp.bitwise_xor(me_ref[0], r) * width, 128)
        all_ref[:, pl.ds(start, width)] = head[...]
    if quarters == 1:
        w_ref[...] = weights[0][...]
    else:
        for r, weight in enumerate(weights):
            size = weight.shape[0] // owners
            for f in range(owners):
                start = (f * SEQ + jnp.bitwise_xor(me_ref[0], r)) * size
                start = pl.multiple_of(start, 16)
                w_ref[pl.ds(start, size), :] = weight[f * size : (f + 1) * size, :]
    attn = mult(all_ref[...], w_ref[...])
    attn_ref[...] = attn
    mixed = x_ref[...].astype(f32) + rms_scale(attn, gains_ref[1:2, :])
    mixed_ref[...] = mixed
    fed_ref[...] = to_half(rms_scale(mixed, gains_ref[2:3, :]))


def mid(me, tokens, heads, weights, gains, owners):
    rows, model = tokens.shape
    width = heads[0].shape[1] * SEQ
    specs = [held(v.shape) for v in [tokens, *heads, *weights, gains]]
    outs = [
        ((rows, width), bf16),
        ((width, model), bf16),
        ((rows, model), f32),
        ((rows, model), f32),
        ((rows, model), bf16),
    ]
    return call(
        partial(mid_kernel, owners, len(weights)),
        (1,),
        [pl.BlockSpec(memory_space=pltpu.SMEM)] + specs,
        [pl.BlockSpec(s, lambda i: (0, 0)) for s, _ in outs],
        outs,
        flops=2 * rows * width * model,
    )(me, tokens, *heads, *weights, gains)


def mid_back_kernel(me_ref, a_ref, b_ref, c_ref, dy_ref, mixed_ref, attn_ref, w_ref, gains_ref, *refs):
    grad_ref, grad_attn_ref = refs[:2]
    outs, sum_ref, heads_ref = refs[2 : 2 + SEQ], refs[2 + SEQ], refs[3 + SEQ]
    grad_fed = a_ref[...].astype(f32) + b_ref[...].astype(f32) + c_ref[...].astype(f32)
    part, _ = rms_back(mixed_ref[...], gains_ref[2:3, :], grad_fed)
    grad_mixed = dy_ref[...].astype(f32) + part
    grad_ref[...] = grad_mixed
    grad_attn, terms = rms_back(attn_ref[...], gains_ref[1:2, :], grad_mixed)
    half = to_half(grad_attn)
    grad_attn_ref[...] = half
    heads_ref[...] = to_half(outer_cols(half, w_ref[...]))
    width = outs[0].shape[1]
    for r, out in enumerate(outs):
        start = pl.multiple_of(jnp.bitwise_xor(me_ref[0], r) * width, 128)
        out[...] = heads_ref[:, pl.ds(start, width)]

    @pl.when(pl.program_id(0) == 0)
    def _():
        sum_ref[...] = jnp.zeros_like(sum_ref)

    sum_ref[...] += column_sum(terms)


def mid_back(me, shares, cotangent, mixed, attn, w_out, gains, steps):
    rows, model = mixed.shape
    total = w_out.shape[0]
    by_row = [*shares, cotangent, mixed, attn]
    row = lambda width: pl.BlockSpec((rows // steps, width), lambda i: (i, 0))
    outs = [((rows, model), f32), ((rows, model), bf16)]
    outs += [((rows, total // SEQ), bf16)] * SEQ
    return call(
        mid_back_kernel,
        (steps,),
        [pl.BlockSpec(memory_space=pltpu.SMEM)]
        + [row(model) for _ in by_row]
        + [held(w_out.shape), held(gains.shape)],
        [row(s[1]) for s, _ in outs] + [pl.BlockSpec((1, model), lambda i: (0, 0))],
        [*outs, ((1, model), f32)],
        flops=2 * rows * model * total,
        scratch=[pltpu.VMEM((rows // steps, total), bf16)],
    )(me, *by_row, w_out, gains)


def turn_back(grad, cosine, sine):
    half = grad.shape[-1] // 2
    a, b = grad[:, :half], grad[:, half:]
    return jnp.concatenate([a * cosine + b * sine, b * cosine - a * sine], axis=-1)


def project_back_kernel(core_ref, *refs):
    dq_ref, keep_ref, come_ref, q_raw_ref, kv_raw_ref, cos_ref, sin_ref, gains_ref, w_ref = refs[:9]
    grad_ref, q_sum_ref, k_sum_ref = refs[9:12]
    outs = refs[12:]
    cosine, sine = cos_ref[...], sin_ref[...]
    head = dq_ref.shape[1]
    first = core_ref[0] == 0
    grad_q, q_terms = rms_back(
        q_raw_ref[...], gains_ref[4:5, :], turn_back(dq_ref[...], cosine, sine)
    )
    grad_kv = keep_ref[...] + come_ref[...].astype(f32)
    grad_k, k_terms = rms_back(
        kv_raw_ref[...], gains_ref[5:6, :], turn_back(grad_kv, cosine, sine)
    )
    grad_ref[:, :head] = to_half(grad_q)
    grad_ref[:, head:] = to_half(jnp.where(first, grad_k, grad_kv))
    share = to_half(outer_cols(grad_ref[...], w_ref[...]))
    for r, out in enumerate(outs):

        @pl.when(pl.program_id(0) == r)
        def _():
            out[...] = share

    @pl.when(pl.program_id(0) == 0)
    def _():
        q_sum_ref[...] = jnp.zeros_like(q_sum_ref)
        k_sum_ref[...] = jnp.zeros_like(k_sum_ref)

    q_sum_ref[...] += column_sum(q_terms)
    k_sum_ref[...] += jnp.where(first, column_sum(k_terms), 0.0)


def project_back(core, dq, keep, come, q_raw, kv_raw, cosine, sine, head_gains, w_own):
    rows, head = dq.shape
    model = w_own.shape[0]
    block = rows // SEQ
    by_row = [dq, keep, come, q_raw, kv_raw, cosine, sine]
    row = lambda width: pl.BlockSpec((block, width), lambda i: (i, 0))
    fixed = lambda shape: pl.BlockSpec(shape, lambda i: (0, 0))
    return call(
        project_back_kernel,
        (SEQ,),
        [pl.BlockSpec(memory_space=pltpu.SMEM)]
        + [row(v.shape[1]) for v in by_row]
        + [held(head_gains.shape), held(w_own.shape)],
        [row(2 * head), fixed((1, head)), fixed((1, head))] + [fixed((block, model))] * SEQ,
        [((rows, 2 * head), bf16), ((1, head), f32), ((1, head), f32)]
        + [((block, model), bf16)] * SEQ,
        flops=4 * rows * head * model,
    )(core, *by_row, head_gains, w_own)


def front_kernel(count, rows, short, packed, meta_ref, *refs):
    tokens = refs[:SEQ]
    pieces = refs[SEQ : SEQ + count]
    cos_ref, sin_ref = refs[SEQ + count : SEQ + count + 2]
    normed_ref, q_ref, kv_ref, q_raw_ref, kv_raw_ref, w_ref, out_ref, gains_ref, head_gains_ref = (
        refs[SEQ + count + 2 : -2]
    )
    x_ref, columns_ref = refs[-2:]
    at = pl.program_id(0)
    head = q_ref.shape[1]

    @pl.when(at == 0)
    def _():
        for j, piece in enumerate(pieces):
            size = piece.shape[0] - 2 * packed
            start = pl.multiple_of(meta_ref[1 + j] * rows, 16)
            w_ref[pl.ds(start, size), :] = piece[:size, : 2 * head]
            columns_ref[pl.ds(start, size), :] = piece[:size, 2 * head :].astype(f32)
            if packed:
                start = pl.multiple_of(meta_ref[1 + j] * packed, 16)
                wide = piece.shape[1]
                rest = out_ref.shape[1] - wide
                out_ref[pl.ds(start, packed), :wide] = piece[size : size + packed, :]
                out_ref[pl.ds(start, packed), wide:] = piece[size + packed :, :rest]
        gains = columns_ref[...].T[:8]
        gains_ref[...] = gains
        model = gains.shape[1]
        from_row = lax.broadcasted_iota(jnp.int32, (model, head), 0)
        to_col = lax.broadcasted_iota(jnp.int32, (model, head), 1)
        owner = to_col >> (short.bit_length() - 1)
        wanted = owner * rows + (to_col & (short - 1))
        pick = jnp.where(from_row == wanted, 1.0, 0.0)
        head_gains_ref[...] = mult(to_half(gains), to_half(pick))

    for r in range(SEQ):

        @pl.when(at == r)
        def _():
            x_ref[...] = tokens[r][...].astype(f32)

    values = x_ref[...]
    normed = to_half(rms_scale(values, gains_ref[0:1, :]))
    normed_ref[...] = normed
    raw = mult(normed, w_ref[...])
    q_raw = raw[:, :head]
    kv_raw = raw[:, head:]
    q_raw_ref[...] = q_raw
    kv_raw_ref[...] = kv_raw
    cosine, sine = cos_ref[...], sin_ref[...]
    q_ref[...] = to_half(head_norm(q_raw, head_gains_ref[4:5, :], cosine, sine))
    keyed = head_norm(kv_raw, head_gains_ref[5:6, :], cosine, sine)
    kv_ref[...] = to_half(jnp.where(meta_ref[0] == 0, keyed, kv_raw))


def front(tokens, pieces, meta, cosine, sine, rows, short, packed):
    block, model = tokens[0].shape
    head = 2 * cosine.shape[1]
    total = block * SEQ
    out_shape = (max(8, packed * len(pieces)), model)
    slab = lambda width: pl.BlockSpec((block, width), lambda i: (i, 0))
    fixed = lambda shape: pl.BlockSpec(shape, lambda i: (0, 0))
    return call(
        partial(front_kernel, len(pieces), rows, short, packed),
        (SEQ,),
        [pl.BlockSpec(memory_space=pltpu.SMEM)]
        + [held(t.shape) for t in tokens]
        + [held(p.shape) for p in pieces]
        + [slab(head // 2)] * 2,
        [slab(model), slab(head), slab(head), slab(head), slab(head)]
        + [fixed((model, 2 * head)), fixed(out_shape), fixed((8, model)), fixed((8, head))],
        [
            ((total, model), bf16),
            ((total, head), bf16),
            ((total, head), bf16),
            ((total, head), f32),
            ((total, head), f32),
            ((model, 2 * head), bf16),
            (out_shape, bf16),
            ((8, model), f32),
            ((8, head), f32),
        ],
        flops=4 * total * model * head,
        scratch=[
            pltpu.VMEM((block, model), f32),
            pltpu.VMEM((model, 128), f32),
        ],
    )(meta, *tokens, *pieces, cosine, sine)


def twins(values):
    size = values.shape[0] // SEQ
    return jnp.concatenate([values[(r ^ 1) * size : (r ^ 1) * size + size] for r in range(SEQ)])


def split_pair(meta_ref, mine_ref, other_ref, keys_ref, values_ref):
    mine, other = mine_ref[...], twins(other_ref[...])
    first = meta_ref[0] == 0

    @pl.when(first)
    def _():
        keys_ref[...] = mine
        values_ref[...] = other

    @pl.when(jnp.logical_not(first))
    def _():
        keys_ref[...] = other
        values_ref[...] = mine


def attend_kernel(
    scale, meta_ref, q_ref, mine_ref, other_ref, code_ref, low_ref, high_ref, *refs
):
    outs, (probs_ref, keys_ref, values_ref) = refs[:SEQ], refs[SEQ:]
    at = pl.program_id(0)

    @pl.when(at == 0)
    def _():
        split_pair(meta_ref, mine_ref, other_ref, keys_ref, values_ref)

    scores = outer_cols(q_ref[...], keys_ref[...])
    code = code_ref[...]
    seen = (code >= low_ref[...]) & (code <= high_ref[...])
    expd = jnp.where(seen, jnp.exp2(scores * (scale * 1.4426950408889634)), 0.0)
    total = jnp.sum(expd, axis=1, keepdims=True)
    probs = to_half(expd * (1.0 / total))
    probs_ref[...] = probs
    out = to_half(mult(probs, values_ref[...]))
    block = out.shape[0]
    steps = outs[0].shape[0] // block
    for r in range(SEQ):
        for s in range(steps):

            @pl.when(at == r * steps + s)
            def _():
                outs[r][s * block : (s + 1) * block, :] = out


def attend(meta, queries, mine, other, code, low, high, scale, block):
    rows, width = queries.shape
    count = mine.shape[0]
    slab = pl.BlockSpec((block, width), lambda i: (i, 0))
    thin = pl.BlockSpec((block, 1), lambda i: (i, 0))
    part = pl.BlockSpec((rows // SEQ, width), lambda i: (0, 0))
    return call(
        partial(attend_kernel, scale),
        (rows // block,),
        [pl.BlockSpec(memory_space=pltpu.SMEM), slab, held(mine.shape), held(mine.shape)]
        + [pl.BlockSpec((1, count), lambda i: (0, 0)), thin, thin],
        [part] * SEQ + [pl.BlockSpec((block, count), lambda i: (i, 0))],
        [((rows // SEQ, width), bf16)] * SEQ + [((rows, count), bf16)],
        flops=4 * rows * count * width,
        exps=rows * count,
        scratch=[pltpu.VMEM((count, width), bf16)] * 2,
    )(meta, queries, mine, other, code, low, high)


def attend_back_kernel(scale, meta_ref, q_ref, mine_ref, other_ref, p_ref, *refs):
    grads_in = refs[:SEQ]
    dq_ref, keep_ref, send_ref, keys_ref, values_ref, dk_ref, dv_ref, g_ref = refs[SEQ:]
    at = pl.program_id(0)

    @pl.when(at == 0)
    def _():
        split_pair(meta_ref, mine_ref, other_ref, keys_ref, values_ref)
        dk_ref[...] = jnp.zeros_like(dk_ref)
        dv_ref[...] = jnp.zeros_like(dv_ref)

    block = g_ref.shape[0]
    steps = grads_in[0].shape[0] // block
    for r in range(SEQ):
        for s in range(steps):

            @pl.when(at == r * steps + s)
            def _():
                g_ref[...] = grads_in[r][s * block : (s + 1) * block, :]

    probs = p_ref[...]
    grads = g_ref[...]
    wide = probs.astype(f32)
    grad_probs = outer_cols(grads, values_ref[...])
    centre = jnp.sum(wide * grad_probs, axis=1, keepdims=True)
    grad_scores = to_half(wide * (grad_probs - centre))
    dq_ref[...] = scale * mult(grad_scores, keys_ref[...])
    dk_ref[...] += scale * inner_rows(grad_scores, q_ref[...])
    dv_ref[...] += inner_rows(probs, grads)

    @pl.when(at == pl.num_programs(0) - 1)
    def _():
        first = meta_ref[0] == 0
        keep_ref[...] = jnp.where(first, dk_ref[...], dv_ref[...])
        send_ref[...] = twins(to_half(jnp.where(first, dv_ref[...], dk_ref[...])))


def attend_back(meta, queries, mine, other, probs, grads, scale, block):
    rows, width = queries.shape
    count = mine.shape[0]
    whole = pl.BlockSpec((count, width), lambda i: (0, 0))
    slab = pl.BlockSpec((block, width), lambda i: (i, 0))
    return call(
        partial(attend_back_kernel, scale),
        (rows // block,),
        [pl.BlockSpec(memory_space=pltpu.SMEM), slab, held(mine.shape), held(mine.shape)]
        + [pl.BlockSpec((block, count), lambda i: (i, 0))]
        + [held(g.shape) for g in grads],
        [slab, whole, whole],
        [((rows, width), f32), ((count, width), f32), ((count, width), bf16)],
        flops=8 * rows * count * width,
        scratch=[pltpu.VMEM((count, width), bf16)] * 2
        + [pltpu.VMEM((count, width), f32)] * 2
        + [pltpu.VMEM((block, width), bf16)],
    )(meta, queries, mine, other, probs, *grads)


def pick_block(blocks, into_ref):
    for r, block in enumerate(blocks):

        @pl.when(pl.program_id(0) == r)
        def _():
            into_ref[...] = block[...]


def gate_up_kernel(count, pieces, meta_ref, *refs):
    parts, outs = refs[count : count + 2 * pieces], refs[count + 2 * pieces :]
    act_ref, value_ref, slope_ref = outs[:3]
    x_ref = outs[-1]
    gate_ref, up_ref = outs[3:5] if pieces == 2 else parts

    if pieces == 2:

        @pl.when(pl.program_id(0) == 0)
        def _():
            for w_ref, own in ((gate_ref, parts[:2]), (up_ref, parts[2:])):
                for half, ref in enumerate(own):
                    size = ref.shape[1]
                    for z in range(ref.shape[0]):
                        start = (2 * z + jnp.bitwise_xor(meta_ref[0], half)) * size
                        w_ref[pl.ds(pl.multiple_of(start, 16), size), :] = ref[z]

    pick_block(refs[:count], x_ref)
    rows = x_ref[...]
    gate = mult(rows, gate_ref[...])
    upper = mult(rows, up_ref[...])
    c = 0.7978845608028654
    square = gate * gate
    bend = jnp.tanh(gate * (c + (c * 0.044715) * square))
    half = 0.5 + 0.5 * bend
    value = gate * half
    slope = half + (0.5 * gate) * (1.0 - bend * bend) * (c + (3 * c * 0.044715) * square)
    act_ref[...] = to_half(value * upper)
    value_ref[...] = to_half(value)
    slope_ref[...] = to_half(slope * upper)


def gate_up(meta, blocks, gate_parts, up_parts):
    block, model = blocks[0].shape
    width = gate_parts[0].shape[-1]
    total = block * len(blocks)
    slab = pl.BlockSpec((block, width), lambda i: (i, 0))
    whole = pl.BlockSpec((model, width), lambda i: (0, 0))
    parts = [*gate_parts, *up_parts]
    made = len(parts) - 2
    out = call(
        partial(gate_up_kernel, len(blocks), len(gate_parts)),
        (len(blocks),),
        [pl.BlockSpec(memory_space=pltpu.SMEM)] + [held(b.shape) for b in [*blocks, *parts]],
        [slab] * 3 + [whole] * made,
        [((total, width), bf16)] * 3 + [((model, width), bf16)] * made,
        flops=4 * total * model * width,
        exps=total * width,
        scratch=[pltpu.VMEM((block, model), bf16)],
        limit=62,
    )(meta, *blocks, *parts)
    return out if made else out + parts


def down_kernel(x_ref, w_ref, *outs):
    out = to_half(mult(x_ref[...], w_ref[...]))
    for r, ref in enumerate(outs):

        @pl.when(pl.program_id(0) == r)
        def _():
            ref[...] = out


def down(rows, w_down, count):
    block = rows.shape[0] // count
    width, model = w_down.shape
    out = pl.BlockSpec((block, model), lambda i: (0, 0))
    return call(
        down_kernel,
        (count,),
        [pl.BlockSpec((block, width), lambda i: (i, 0)), held(w_down.shape)],
        [out] * count,
        [((block, model), bf16)] * count,
        flops=2 * count * block * model * width,
    )(rows, w_down)


def back_kernel(count, *refs):
    y_refs = refs[:count]
    value_ref, slope_ref, down_ref, gate_ref, up_ref, dg_ref, du_ref = refs[count : count + 7]
    outs, y_ref = refs[count + 7 : -1], refs[-1]
    pick_block(y_refs, y_ref)
    grad_act = outer_cols(y_ref[...], down_ref[...])
    dg_ref[...] = to_half(grad_act * slope_ref[...].astype(f32))
    du_ref[...] = to_half(grad_act * value_ref[...].astype(f32))
    out = to_half(outer_cols(dg_ref[...], gate_ref[...]) + outer_cols(du_ref[...], up_ref[...]))
    for r, ref in enumerate(outs):

        @pl.when(pl.program_id(0) == r)
        def _():
            ref[...] = out


def back(blocks, value, slope, w_down, w_gate, w_up):
    block, model = blocks[0].shape
    count = len(blocks)
    width = w_gate.shape[1]
    slab = pl.BlockSpec((block, width), lambda i: (i, 0))
    out = pl.BlockSpec((block, model), lambda i: (0, 0))
    return call(
        partial(back_kernel, count),
        (count,),
        [held(b.shape) for b in blocks]
        + [slab, slab, held(w_down.shape), held(w_gate.shape), held(w_up.shape)],
        [slab, slab] + [out] * count,
        [((block * count, width), bf16)] * 2 + [((block, model), bf16)] * count,
        flops=6 * count * block * model * width,
        scratch=[pltpu.VMEM((block, model), bf16)],
    )(*blocks, value, slope, w_down, w_gate, w_up)


def cut_rows(blocks, many):
    each = many // len(blocks)
    size = blocks[0].shape[0] // each
    return [b[r * size : (r + 1) * size] for b in blocks for r in range(each)]


def rows_sum(left, right):
    total = inner_rows(left[0], right[0])
    for a, b in zip(left[1:], right[1:], strict=True):
        total = total + inner_rows(a, b)
    return total


def rows_kernel(counts, many, meta_ref, *refs):
    total_in = sum(counts)
    results = len(counts) - 1
    values = [ref[...] for ref in refs[:total_in]]
    left = cut_rows(values[: counts[0]], many)
    at = counts[0]
    totals = []
    for count in counts[1:]:
        totals.append(rows_sum(left, cut_rows(values[at : at + count], many)))
        at += count
    if len(refs) == total_in + results:
        for ref, total in zip(refs[total_in:], totals, strict=True):
            ref[...] = to_half(total)
        return
    outs, sums = refs[total_in : total_in + 2 * results], refs[total_in + 2 * results :]
    tile = left[0].shape[1]
    here = pl.ds(pl.multiple_of(pl.program_id(0) * tile, 128), tile)
    for ref, total in zip(sums, totals, strict=True):
        ref[here, :] = total

    @pl.when(pl.program_id(0) == pl.num_programs(0) - 1)
    def _():
        for o in range(results):
            for half, ref in enumerate(outs[2 * o : 2 * o + 2]):
                size = ref.shape[1]
                for z in range(ref.shape[0]):
                    start = (2 * z + jnp.bitwise_xor(meta_ref[0], 1 - half)) * size
                    ref[z] = to_half(sums[o][pl.ds(pl.multiple_of(start, 8), size), :])


def rows_product(meta, left, rights, tile, owners, cut=True):
    counts = [len(v) for v in [left, *rights]]
    many = max(counts)
    height = left[0].shape[1]
    widths = [r[0].shape[1] for r in rights]
    flat = [v for r in rights for v in r]
    steps = pl.cdiv(height, tile)
    shape = lambda w: (owners // 2, height // owners, w)
    if cut:
        specs = [pl.BlockSpec(shape(w), lambda i: (0, 0, 0)) for w in widths for _ in range(2)]
        outs = [(shape(w), bf16) for w in widths for _ in range(2)]
    else:
        specs = [pl.BlockSpec((tile, w), lambda i: (i, 0)) for w in widths]
        outs = [((height, w), bf16) for w in widths]
    return call(
        partial(rows_kernel, counts, many),
        (steps,),
        [pl.BlockSpec(memory_space=pltpu.SMEM)]
        + [pl.BlockSpec((v.shape[0], tile), lambda i: (0, i)) for v in left]
        + [held(v.shape) for v in flat],
        specs,
        outs,
        flops=2 * sum(v.shape[0] for v in left) * height * sum(widths),
        scratch=[pltpu.VMEM((steps * tile, w), f32) for w in widths] if cut else [],
        limit=62,
    )(meta, *left, *flat)


def after(value, *others):
    return lax.optimization_barrier((value, others))[0]


def swap_seq(values, bits):
    return lax.ppermute(values, "seq", [(i, i ^ bits) for i in range(SEQ)])


def gather_seq(own):
    one = swap_seq(own, 1)
    two = swap_seq(own, 2)
    return [own, one, two, swap_seq(two, 1)]


def natural(blocks, me):
    stack = jnp.stack(blocks)
    return [lax.dynamic_index_in_dim(stack, me ^ j, 0, keepdims=False) for j in range(SEQ)]


def reduce_seq(blocks):
    three = swap_seq(blocks[3], 1)
    pair = to_half(blocks[2].astype(f32) + three.astype(f32))
    two = swap_seq(pair, 2)
    one = swap_seq(blocks[1], 1)
    return blocks[0].astype(f32) + one.astype(f32) + two.astype(f32)


class Owners:
    def __init__(self, count):
        self.count = count
        self.rows = count // 2
        self.groups = [[2 * z + y for z in range(self.rows)] for y in range(2)]
        index = lax.axis_index("fsdp")
        self.low = index % 2
        self.high = index // 2
        self.direct = self.rows <= 4

    def swap(self, values):
        return lax.ppermute(values, "fsdp", [(i, i ^ 1) for i in range(self.count)])

    def shift(self, values, by):
        return lax.ppermute(
            values, "fsdp", [(i, (i + 2 * by) % self.count) for i in range(self.count)]
        )

    def gather_row(self, values):
        return lax.all_gather(values, "fsdp", axis=0, tiled=True, axis_index_groups=self.groups)

    def pair(self, mine, other, axis):
        first = jnp.where(self.low == 0, mine, other)
        second = jnp.where(self.low == 0, other, mine)
        return jnp.stack([first, second], axis=axis)

    def gather_pieces(self, own):
        if not self.direct:
            return [lax.all_gather(own, "fsdp", axis=0, tiled=True)], [jnp.int32(0)]
        far = [own] + [self.shift(own, by) for by in range(1, self.rows)]
        near = [self.swap(p) for p in far]
        starts = [lax.rem(self.high - by + self.rows, self.rows) * 2 for by in range(self.rows)]
        places = [s + self.low for s in starts] + [s + 1 - self.low for s in starts]
        return far + near, places

    def gather_wide(self, own, later):
        if not self.direct:
            return [lax.all_gather(own, "fsdp", axis=0, tiled=True)]
        size, width = own.shape
        mine = after(self.gather_row(own), later).reshape(self.rows, size, width)
        return [mine, self.swap(mine)]

    def gather_pair_first(self, own):
        size, width = own.shape
        both = self.pair(own, self.swap(own), 0).reshape(2 * size, width)
        return self.gather_row(both)

    def halves(self, whole):
        size = whole.shape[0] // self.count
        view = whole.reshape(self.rows, 2, size, whole.shape[1])
        away = lax.dynamic_index_in_dim(view, 1 - self.low, 1, keepdims=False)
        here = lax.dynamic_index_in_dim(view, self.low, 1, keepdims=False)
        return away, here

    def product_halves(self, side, left, right, tile):
        if (left[0].shape[1] // self.count) % 8 == 0:
            return rows_product(side, left, [right], tile, self.count)
        return self.halves(rows_product(side, left, [right], tile, self.count, False)[0])

    def fold(self, here, come):
        return add_half(here, come, here.shape[0])

    def scatter_row(self, half):
        return lax.psum_scatter(
            half.reshape(-1, half.shape[2]),
            "fsdp",
            scatter_dimension=0,
            axis_index_groups=self.groups,
            tiled=True,
        )

    def scatter_direct(self, half):
        if not self.direct:
            return self.scatter_row(half).astype(f32)
        total = lax.dynamic_index_in_dim(half, self.high, 0, keepdims=False).astype(f32)
        for by in range(1, self.rows):
            z = lax.rem(self.high + by, self.rows)
            away = lax.dynamic_index_in_dim(half, z, 0, keepdims=False)
            total = total + self.shift(away, by).astype(f32)
        return total


def body(
    tokens,
    cotangent,
    positions,
    segment,
    query_weight,
    key_weight,
    value_weight,
    out_weight,
    gate_weight,
    up_weight,
    down_weight,
    gain_input,
    gain_query,
    gain_key,
    gain_mixed,
    gain_feed,
    gain_final,
    fsdp,
):
    owners = Owners(fsdp)
    me = lax.axis_index("seq")
    core = me & 1
    tok_rows, model = tokens.shape
    group_len = positions.shape[0]
    rows = query_weight.shape[0]
    head_width = key_weight.shape[1]
    hidden = gate_weight.shape[1]
    slab = hidden // fsdp
    part = slab // SEQ
    scale = head_width ** (-0.5)

    head_cols = lax.dynamic_slice_in_dim(query_weight, me * head_width, head_width, axis=1)
    key_or_value = jnp.where(core == 0, key_weight, value_weight)
    short = jnp.stack([gain_query, gain_key], axis=1)
    short = jnp.pad(short, ((0, rows - short.shape[0]), (0, 0)))
    gains_own = jnp.concatenate(
        [jnp.stack([gain_input, gain_mixed, gain_feed, gain_final], axis=1), short], axis=1
    )
    gains_own = jnp.pad(gains_own, ((0, 0), (0, 128 - gains_own.shape[1])))
    out_rows = out_weight.shape[0]
    out_part = out_rows // SEQ
    out_own = lax.dynamic_slice_in_dim(out_weight, me * out_part, out_part, axis=0)
    out_own = to_half(out_own)
    attn_own = jnp.concatenate(
        [to_half(head_cols), to_half(key_or_value), to_half(gains_own)], axis=1
    )
    packed = out_part if owners.direct and out_part % 16 == 0 else 0
    if packed:
        wide = attn_own.shape[1]
        rest = jnp.pad(out_own[:, wide:], ((0, 0), (0, 2 * wide - model)))
        pack_own = jnp.concatenate([attn_own, out_own[:, :wide], rest])
    else:
        pack_own = attn_own

    def columns(weight):
        return to_half(
            jnp.concatenate(
                [
                    lax.dynamic_slice_in_dim(weight, f * slab + me * part, part, axis=1)
                    for f in range(fsdp)
                ],
                axis=1,
            )
        )

    pieces, starts = owners.gather_pieces(pack_own)
    ahead = pieces[: (len(pieces) + 1) // 2]
    tokens_out = after(tokens, pack_own)
    token_blocks = [tokens, swap_seq(tokens_out, 1), swap_seq(tokens_out, 2)]
    token_blocks.append(swap_seq(after(token_blocks[2], *ahead), 1))
    gate_own = columns(after(gate_weight, token_blocks[2], *ahead))
    up_own = columns(after(up_weight, gate_own))
    down_own = lax.dynamic_slice_in_dim(after(down_weight, up_own), me * part, part, axis=0)
    down_own = to_half(down_own)

    def own_order(values):
        return jnp.concatenate(
            [
                lax.dynamic_slice_in_dim(values, (me ^ r) * tok_rows, tok_rows)
                for r in range(SEQ)
            ]
        )

    places = own_order(positions)
    kinds = own_order(segment)
    cosine, sine = rope_tables(places, head_width)
    second = kinds == 2
    code = jnp.where(second, -places, places).astype(f32)[None, :]
    low = jnp.where(second, -places, 0).astype(f32)[:, None]
    high = jnp.where(second, group_len // 2 - 1, places).astype(f32)[:, None]
    short_rows = head_width // fsdp

    meta = jnp.stack([core] + starts).astype(jnp.int32)
    normed16, queries, mine_kv, query_raw, kv_raw, w_own, out_flat, gains, head_gains = front(
        token_blocks, pieces, meta, cosine, sine, rows, short_rows, packed
    )
    gate_parts = owners.gather_wide(gate_own, queries)
    g_input = gains[0]
    other_kv = swap_seq(mine_kv, 1)
    *heads, probs = attend(meta, queries, mine_kv, other_kv, code, low, high, scale, 256)
    up_parts = owners.gather_wide(up_own, probs)
    w_down = owners.gather_pair_first(down_own)
    heads = [heads[0]] + [swap_seq(heads[r], r) for r in range(1, SEQ)]
    self_index = jnp.stack([me]).astype(jnp.int32)
    if packed:
        quarters = gather_seq(after(out_flat, probs))
    else:
        out_flat = lax.all_gather(out_own, "fsdp", axis=0, tiled=True)
        w_out = jnp.stack(natural(gather_seq(out_flat), me)).reshape(SEQ, fsdp, out_part, model)
        quarters = [w_out.transpose(1, 0, 2, 3).reshape(fsdp * out_rows, model)]
    heads[0] = after(heads[0], *gate_parts)
    heads16, w_out, attn, mixed, fed_own = mid(self_index, tokens, heads, quarters, gains, fsdp)
    inputs32 = tokens.astype(f32)

    side = jnp.stack([owners.low]).astype(jnp.int32)
    fed_blocks = [fed_own, swap_seq(fed_own, 1), swap_seq(fed_own, 2)]
    near_act, near_value, near_slope, w_gate, w_up = gate_up(
        side, fed_blocks[:2], gate_parts, up_parts
    )
    fed_two = after(fed_blocks[2], near_act)
    fed_blocks = fed_blocks[:2] + [fed_two, swap_seq(fed_two, 1)]
    far_act, far_value, far_slope, *_ = gate_up(side, fed_blocks[2:], [w_gate], [w_up])
    far_share = down(far_act, w_down, 2)
    near_act = after(near_act, *far_share)
    share = down(near_act, w_down, 2) + far_share
    share_pair = add_half(share[2], swap_seq(share[3], 1), 4)
    shares = [share[0], swap_seq(share[1], 1), swap_seq(share_pair, 2)]

    def feed_end(first, second, third, mixed, grad, gains):
        ffo = first.astype(f32) + second.astype(f32) + third.astype(f32)
        gain = gains[3:4]
        grad_ffo, terms = rms_back(ffo, gain, grad.astype(f32))
        return mixed + rms_scale(ffo, gain), grad_ffo, column_sum(terms)

    output, ffo_own, gain_final_part = fused(
        feed_end,
        [*shares, mixed, cotangent],
        [gains],
        [(tokens.shape, bf16), (tokens.shape, bf16)],
        4,
        [(1, model)],
    )

    ffo_blocks = [ffo_own, swap_seq(ffo_own, 1), swap_seq(ffo_own, 2)]
    near_gate, near_up, *near_share = back(
        ffo_blocks[:2], near_value, near_slope, w_down, w_gate, w_up
    )
    ffo_two = after(ffo_blocks[2], near_gate)
    ffo_blocks = ffo_blocks[:2] + [ffo_two, swap_seq(ffo_two, 1)]
    away_down, here_down = owners.product_halves(side, [near_act, far_act], ffo_blocks, 256)
    come_down = owners.swap(away_down)
    far_blocks = list(lax.optimization_barrier((away_down, *ffo_blocks[2:]))[1:])
    far_gate, far_up, *far_share = back(far_blocks, far_value, far_slope, w_down, w_gate, w_up)
    pair = add_half(far_share[0], swap_seq(far_share[1], 1), 4)
    far_sum = swap_seq(pair, 2)
    near_one = swap_seq(near_share[1], 1)
    fed_left = [after(fed_blocks[0], pair, near_one)] + fed_blocks[1:]
    away_gate, here_gate = owners.product_halves(side, fed_left, [near_gate, far_gate], 384)
    come_gate = owners.swap(away_gate)
    half_down = owners.fold(after(here_down, away_gate), come_down)
    grad_down = owners.scatter_row(half_down)
    fed_left = [after(fed_left[0], half_down)] + fed_left[1:]
    away_up, here_up = owners.product_halves(side, fed_left, [near_up, far_up], 384)
    come_up = owners.swap(away_up)
    shares = [after(near_share[0], away_up), near_one, far_sum]
    grad_mixed, grad_attn16, *grad_heads, gain_mixed_part = mid_back(
        self_index, shares, cotangent, mixed, attn, w_out, gains, 4
    )
    grad_heads = [grad_heads[0]] + [swap_seq(grad_heads[r], r) for r in range(1, SEQ)]

    half_gate = owners.fold(after(here_gate, *grad_heads), come_gate)
    grad_gate = owners.scatter_row(half_gate)
    grad_heads[0] = after(grad_heads[0], half_gate)
    grad_queries, keep_kv, send_kv = attend_back(
        meta, queries, mine_kv, other_kv, probs, grad_heads, scale, 256
    )
    come_kv = swap_seq(send_kv, 1)
    grad_qkv16, gain_query_part, gain_key_part, *normed_blocks = project_back(
        jnp.stack([core]).astype(jnp.int32),
        grad_queries,
        after(keep_kv, grad_down),
        come_kv,
        query_raw,
        kv_raw,
        cosine,
        sine,
        head_gains,
        w_own,
    )
    grad_normed = reduce_seq(normed_blocks)
    grad_proj = to_half(inner_rows(normed16, after(grad_qkv16, normed_blocks[0])))
    grad_out_share = to_half(inner_rows(heads16, after(grad_attn16, grad_proj)))
    grad_out_view = grad_out_share.reshape(fsdp, SEQ, out_part, model)
    grad_out_part = reduce_seq(
        [
            lax.dynamic_index_in_dim(grad_out_view, me ^ r, 1, keepdims=False)
            for r in range(SEQ)
        ]
    )
    extra = out_part * model // rows
    grad_out_part = to_half(grad_out_part).reshape(fsdp * rows, extra)

    short = jnp.stack([gain_query_part[0], gain_key_part[0]], axis=1).reshape(fsdp, short_rows, 2)
    short = jnp.pad(short, ((0, 0), (0, rows - short_rows), (0, 0))).reshape(model, 2)
    gain_parts = jnp.concatenate(
        [jnp.stack([gain_mixed_part[0], gain_final_part[0]], axis=1), short], axis=1
    )
    gain_parts = jnp.pad(gain_parts, ((0, 0), (0, 128 - gain_parts.shape[1])))
    half_up = owners.fold(after(here_up, grad_proj), come_up)
    grad_up = owners.scatter_row(half_up)
    downs = natural(gather_seq(grad_down), me)
    out_down = jnp.concatenate(downs).astype(f32)
    away_small, here_small = owners.halves(
        jnp.concatenate([grad_proj, to_half(gain_parts), grad_out_part], axis=1)
    )
    half_small = owners.fold(here_small, owners.swap(after(away_small, out_down, grad_gate)))
    grad_small = owners.scatter_direct(half_small)
    _, input_back = jax.vjp(lambda v: rms_scale(v, g_input), inputs32)
    (grad_input_part,) = input_back(grad_normed)
    grad_tokens = grad_mixed + grad_input_part

    gates = natural(gather_seq(grad_gate), me)
    ups = natural(gather_seq(grad_up), me)

    def spread(blocks):
        if fsdp <= 8:
            pieces = [
                blocks[t][:, f * part : (f + 1) * part]
                for f in range(fsdp)
                for t in range(SEQ)
            ]
            return jnp.concatenate(pieces, axis=1).astype(f32)
        stack = jnp.stack([b[:, : fsdp * part].reshape(rows, fsdp, part) for b in blocks], axis=2)
        return stack.reshape(rows, hidden).astype(f32)

    out_gate = spread(gates)
    out_up = spread(ups)

    feed_sum = jnp.sum(
        grad_gate.astype(f32) * gate_own.astype(f32)
        + grad_up.astype(f32) * up_own.astype(f32),
        axis=1,
    )
    input_sum = jnp.sum(
        grad_small[:, : 2 * head_width] * attn_own[:, : 2 * head_width].astype(f32), axis=1
    )
    tail = jnp.concatenate(
        [grad_small[:, 2 * head_width : 2 * head_width + 4], jnp.stack([input_sum, feed_sum], axis=1)],
        axis=1,
    )
    tail = jnp.pad(tail, ((0, 0), (0, 128 - tail.shape[1])))
    small = gather_seq(
        to_half(
            jnp.concatenate(
                [grad_small[:, : 2 * head_width], tail, grad_small[:, 2 * head_width + 128 :]], axis=1
            )
        )
    )
    outs = [b[:, 2 * head_width + 128 :].reshape(out_part, model) for b in natural(small, me)]
    out_out = jnp.concatenate(outs).astype(f32)
    out_query = jnp.concatenate([b[:, :head_width] for b in natural(small, me)], axis=1).astype(f32)
    kv = [b[:, head_width : 2 * head_width].astype(f32) for b in small]
    same, cross = kv[0] + kv[2], kv[1] + kv[3]
    out_key = jnp.where(core == 0, same, cross)
    out_value = jnp.where(core == 0, cross, same)
    tails = sum(b[:, 2 * head_width : 2 * head_width + 128].astype(f32) for b in small)
    own_gains = attn_own[:, 2 * head_width : 2 * head_width + 128].astype(f32)
    out_g_mixed = tails[:, 0]
    out_g_final = tails[:, 1]
    out_g_query = tails[:short_rows, 2]
    out_g_key = tails[:short_rows, 3]
    out_g_input = tails[:, 4] / own_gains[:, 0]
    out_g_feed = tails[:, 5] / own_gains[:, 2]
    return (
        output,
        grad_tokens,
        out_query,
        out_key,
        out_value,
        out_out,
        out_gate,
        out_up,
        out_down,
        out_g_input,
        out_g_query,
        out_g_key,
        out_g_mixed,
        out_g_feed,
        out_g_final,
    )


def solution(mesh):
    by_token = P(("fsdp", "seq"), None)
    by_row = P("fsdp", None)
    by_one = P("fsdp")
    return jax.shard_map(
        partial(body, fsdp=mesh.shape["fsdp"]),
        mesh=mesh,
        in_specs=(by_token,) * 2 + (by_one,) * 2 + (by_row,) * 7 + (by_one,) * 6,
        out_specs=(by_token,) * 2 + (by_row,) * 7 + (by_one,) * 6,
        check_vma=False,
    )
```

time: 818 us -> 670 us (0.82)
  Pallas kernels: 30.1 us -> 258 us
  matrix products: 171 us -> 8.56 us
  waiting for transfers between devices: 314 us -> 226 us
  other arithmetic: 109 us -> 48.8 us
  local copies, waits for them, and re-layouts: 115 us -> 55.4 us
    pallas_call x2 -> x22, Pallas kernels: 30.1 us -> 258 us  [call(): return lambda *operands: list(made(*operands))]
    dot_general x10 -> x0, matrix products: 121 us -> none  [the longest x5 64.9 us: outer_cols(): lax.dot_general(left, right, (((1,), (1,)), ((), ())), preferred_element_...]
    ppermute x12 -> x11, waiting for transfers between devices: 135 us -> 78.9 us  [swap(): return lax.ppermute(values, 'fsdp', [(i, i ^ 1) for i in range(self.count)])]
    dot_general x5 -> x2, matrix products: 49.9 us -> 8.56 us  [inner_rows(): lax.dot_general(left, right, (((0,), (0,)), ((), ())), preferred_element_...]
    convert_element_type x15 -> x4, other arithmetic: 25.8 us -> 7.12 us  [to_half(): return values.astype(bf16)]
    convert_element_type x4 -> x2, local copies, waits for them, and re-layouts: 16.1 us -> 1.28 us  [to_half(): return values.astype(bf16)]
    all_gather x4 -> x3, waiting for transfers between devices: 25.7 us -> 11 us  [gather_row(): lax.all_gather(values, 'fsdp', axis=0, tiled=True, axis_index_groups=self...]
    broadcast_in_dim x8 -> x0, local copies, waits for them, and re-layouts: 12 us -> none  [the longest x7 11.9 us: put(): return lax.dynamic_update_slice(whole, block[None, None], (z, y, 0, 0))]
  transfers between devices with their start and end apart: 64 -> 67, of which waited for: 29 -> 32; matrix products, arithmetic and copies ran while one was open for 36% -> 12% of each run, Pallas kernels for 4% -> 34%
where the time goes in v2:
time: 670 us; the launch traced here: 660 us
  Pallas kernels  258 us (39%)
  waiting for transfers between devices  226 us (34%)
  local copies, waits for them, and re-layouts  55.4 us (8%)
  other arithmetic  48.8 us (7%)
  starting transfers between devices  47.4 us (7%)
  between operations  15.4 us (2%)
  matrix products  8.56 us (1%)
    pallas_call x22, Pallas kernels, call(): return lambda *operands: list(made(*operands))  258 us
    ppermute x44, waiting for transfers between devices, swap_seq(): return lax.ppermute(values, 'seq', [(i, i ^ bits) for i in range(SEQ)])  99.8 us
    ppermute x11, waiting for transfers between devices, swap(): return lax.ppermute(values, 'fsdp', [(i, i ^ 1) for i in range(self.count)])  78.9 us
    ppermute x6, waiting for transfers between devices, shift(): lax.ppermute(values, 'fsdp', [(i, (i + 2 * by) % self.count) for i in ran...  36.2 us
    ppermute x44, starting transfers between devices, swap_seq(): return lax.ppermute(values, 'seq', [(i, i ^ bits) for i in range(SEQ)])  28.6 us
  transfers between devices with their start and end apart: 67, of which 32 were waited for; matrix products, arithmetic and copies ran while one was open for 12% of the time, Pallas kernels for 34%

profile of v2, /device:TPU:9, one launch (start us, length us, event | category | flops | bytes accessed | tf_op | source)
XLA Modules:
  0.0 659.7 jit_solution(16641639130955775583)
XLA Ops:
  18.7 3.2 collective-permute-done.2.refs_5_
  21.9 16.2 %collective-permute-done.3.refs_6_ = bf16[208,640]{1,0:T(8,128)(2,1)S(1)} collective-permute-done((bf16[208,640]{1,0:T(8,128)(2,1)S(1)}, bf16[208,640]{1,0:T(8,128)(2,1)S(1)}, u32[]{:S(2)}, u32[]{:S(2)}) %collective-permute-start.3) | collective-permute-done | bytes 266272 | tf_op jit(solution)/shard_map/ppermute | solution.py:721
  51.8 9.5 %collective-permute-done.22 = bf16[216,1152]{1,0:T(8,128)(2,1)} collective-permute-done((bf16[216,1152]{1,0:T(8,128)(2,1)S(1)}, bf16[216,1152]{1,0:T(8,128)(2,1)}, u32[]{:S(2)}, u32[]{:S(2)}) %collective-permute-start.22) | collective-permute-done | bytes 497696 | tf_op jit(solution)/shard_map/ppermute | solution.py:718
  71.3 5.6 multiply_sine_fusion
  76.9 4.6 collective-permute-done.8.refs_10_
  81.5 5.7 collective-permute-done.9.refs_11_
  87.9 11.1 %shard_map.280 = (bf16[2048,1152]{1,0:T(8,128)(2,1)}, bf16[2048,256]{1,0:T(8,128)(2,1)}, bf16[2048,256]{1,0:T(8,128)(2,1)}, f32[2048,256]{1,0:T(8,128)}, f32[204...) custom-call(s32[9]{0:T(128)} %stack.161.meta_ref, ...), custom_call_target="tpu_custom_call" | custom-call | flops 48318384 | bytes 256491 | tf_op jit(solution)/shard_map/pallas_call | solution.py:83
  107.1 17.3 %shard_map.281 = (bf16[512,256]{1,0:T(8,128)(2,1)}, bf16[512,256]{1,0:T(8,128)(2,1)}, bf16[512,256]{1,0:T(8,128)(2,1)}, bf16[512,256]{1,0:T(8,128)(2,1)}, bf16[2048,2048]{1,0:T(8,128)(2,1)}) custom-call(s32[9]{0:T(128)} %stack.161.meta_ref, bf16[2048,256]{1,0:T(8,128)(2,1)} %get-tuple-element.107.q_ref, bf16[2048,256]{1,0:T(8,128)(2,1)} %get-tuple-element.108.mine_ref, ...), custom_call_target="tpu_custom_call" | custom-call | flops 85899344 | bytes 188743 | tf_op jit(solution)/shard_map/pallas_call | solution.py:83
  124.5 11.0 %all-gather.6.cloned.1.call-done = bf16[576,1728]{1,0:T(8,128)(2,1)} async-done(((bf16[144,1728]{1,0:T(8,128)(2,1)}), bf16[576,1728]{1,0:T(8,128)(2,1)}) %all-gather.6.cloned.1.call-update) | async-done | bytes 1990672 | tf_op jit(solution)/shard_map/all_gather | solution.py:726
  142.3 6.2 collective-permute-done.11.refs_3_
  150.4 6.8 %collective-permute-done.14.refs_3_ = bf16[512,256]{1,0:T(8,128)(2,1)S(1)} collective-permute-done((bf16[512,256]{1,0:T(8,128)(2,1)}, bf16[512,256]{1,0:T(8,128)(2,1)S(1)}, u32[]{:S(2)}, u32[]{:S(2)}) %collective-permute-start.14) | collective-permute-done | bytes 262176 | tf_op jit(solution)/shard_map/ppermute | solution.py:685
  158.3 7.1 %shard_map.282 = (bf16[512,1024]{1,0:T(8,128)(2,1)}, bf16[1024,1152]{1,0:T(8,128)(2,1)}, f32[512,1152]{1,0:T(8,128)}, f32[512,1152]{1,0:T(8,128)}, bf16[512,1152]{1,0:T(8,128)(2,1)}) custom-call(s32[1]{0:T(128)} %bitcast.1.me_ref, bf16[512,1152]{1,0:T(8,128)(2,1)} %x_ref.1, bf16[512,256]{1,0:T(8,128)(2,1)} %get-tuple-element.112.refs_0_, ...), custom_call_target="tpu_custom_call" | custom-call | flops 24159192 | bytes 186122 | tf_op jit(solution)/shard_map/pallas_call | solution.py:83
  166.5 26.3 %collective-permute-done.19.refs_5_ = bf16[4,144,1728]{2,1,0:T(8,128)(2,1)S(1)} collective-permute-done((bf16[4,144,1728]{2,1,0:T(8,128)(2,1)}, bf16[4,144,1728]{2,1,0:T(8,128)(2,1)S(1)}, u32[]{:S(2)}, u32[]{:S(2)}) %collective-permute-start.19) | collective-permute-done | bytes 1990688 | tf_op jit(solution)/shard_map/ppermute | solution.py:718
  195.1 16.8 %shard_map.283 = (bf16[1024,1728]{1,0:T(8,128)(2,1)}, bf16[1024,1728]{1,0:T(8,128)(2,1)}, bf16[1024,1728]{1,0:T(8,128)(2,1)}, bf16[1152,1728]{1,0:T(8,128)(2,1)}, bf16[1152,1728]{1,0:T(8,128)(2,1)}) custom-call(s32[1]{0:T(128)} %bitcast.meta_ref, bf16[512,1152]{1,0:T(8,128)(2,1)} %get-tuple-element.155.refs_0_, bf16[512,1152]{1,0:T(8,128)(2,1)} %copy-done.4, ...), custom_call_target="tpu_custom_call" | custom-call | flops 163074544 | bytes 371589 | tf_op jit(solution)/shard_map/pallas_call | solution.py:83
  216.5 16.1 %shard_map.284 = (bf16[1024,1728]{1,0:T(8,128)(2,1)}, bf16[1024,1728]{1,0:T(8,128)(2,1)}, bf16[1024,1728]{1,0:T(8,128)(2,1)}) custom-call(s32[1]{0:T(128)} %bitcast.meta_ref, bf16[512,1152]{1,0:T(8,128)(2,1)} %collective-permute-done.20.refs_0_.refs_2_, bf16[512,1152]{1,0:T(8,128)(2,1)} %copy-done.5, bf16[1152,1728]{1,0:T(8,128)(2,1)} %get-tuple-element.125.refs_2_.refs_5_, ...), custom_call_target="tpu_custom_call" | custom-call | flops 163074544 | bytes 212336 | tf_op jit(solution)/shard_map/pallas_call | solution.py:83
  232.7 9.5 %shard_map.285 = (bf16[512,1152]{1,0:T(8,128)(2,1)}, bf16[512,1152]{1,0:T(8,128)(2,1)}) custom-call(bf16[1024,1728]{1,0:T(8,128)(2,1)} %get-tuple-element.127.x_ref.refs_1_, bf16[1728,1152]{1,0:T(8,128)(2,1)} %all-gather.8.cloned.1.call-done.w_ref.refs_4_), custom_call_target="tpu_custom_call" | custom-call | flops 81537272 | bytes 47185 | tf_op jit(solution)/shard_map/pallas_call | solution.py:83
  242.5 9.8 %shard_map.286 = (bf16[512,1152]{1,0:T(8,128)(2,1)}, bf16[512,1152]{1,0:T(8,128)(2,1)}) custom-call(bf16[1024,1728]{1,0:T(8,128)(2,1)} %get-tuple-element.131.x_ref.refs_0_, bf16[1728,1152]{1,0:T(8,128)(2,1)} %all-gather.8.cloned.1.call-done.w_ref.refs_4_), custom_call_target="tpu_custom_call" | custom-call | flops 81537272 | bytes 47185 | tf_op jit(solution)/shard_map/pallas_call | solution.py:83
  253.4 3.7 shard_map.287
  257.2 27.4 %collective-permute-done.25.refs_2_ = bf16[512,1152]{1,0:T(8,128)(2,1)S(1)} collective-permute-done((bf16[512,1152]{1,0:T(8,128)(2,1)}, bf16[512,1152]{1,0:T(8,128)(2,1)S(1)}, u32[]{:S(2)}, u32[]{:S(2)}) %collective-permute-start.25) | collective-permute-done | bytes 1179680 | tf_op jit(solution)/shard_map/ppermute | solution.py:685
  285.6 5.9 shard_map.288
  296.4 26.2 %shard_map.289 = (bf16[1024,1728]{1,0:T(8,128)(2,1)}, bf16[1024,1728]{1,0:T(8,128)(2,1)}, bf16[512,1152]{1,0:T(8,128)(2,1)}, bf16[512,1152]{1,0:T(8,128)(2,1)}) custom-call(bf16[512,1152]{1,0:T(8,128)(2,1)} %get-tuple-element.136.refs_0_.refs_2_, bf16[512,1152]{1,0:T(8,128)(2,1)} %copy-done.7, bf16[1024,1728]{1,0:T(8,128)(2,1)} %get-tuple-element.137.refs_2_, ...), custom_call_target="tpu_custom_call" | custom-call | flops 244611808 | bytes 188743 | tf_op jit(solution)/shard_map/pallas_call | solution.py:83
  325.7 16.0 %shard_map.290 = (bf16[4,216,1152]{2,1,0:T(8,128)(2,1)}, bf16[4,216,1152]{2,1,0:T(8,128)(2,1)}) custom-call(s32[1]{0:T(128)} %bitcast.meta_ref, bf16[1024,1728]{1,0:T(8,128)(2,1)} %get-tuple-element.131.x_ref.refs_0_, bf16[1024,1728]{1,0:T(8,128)(2,1)} %get-tuple-element.127.x_ref.refs_1_, bf16[512,1152]{1,0:T(8,128)(2,1)} %get-tuple-element.136.refs_0_.refs_2_, ...), custom_call_target="tpu_custom_call" | custom-call | flops 163074544 | bytes 79626 | tf_op jit(solution)/shard_map/pallas_call | solution.py:83
  342.9 26.5 %shard_map.291 = (bf16[1024,1728]{1,0:T(8,128)(2,1)}, bf16[1024,1728]{1,0:T(8,128)(2,1)}, bf16[512,1152]{1,0:T(8,128)(2,1)}, bf16[512,1152]{1,0:T(8,128)(2,1)}) custom-call(bf16[512,1152]{1,0:T(8,128)(2,1)} %copy-done.6, bf16[512,1152]{1,0:T(8,128)(2,1)} %collective-permute-done.28.refs_5_.refs_1_, bf16[1024,1728]{1,0:T(8,128)(2,1)} %get-tuple-element.145.refs_2_, ...), custom_call_target="tpu_custom_call" | custom-call | flops 244611808 | bytes 188743 | tf_op jit(solution)/shard_map/pallas_call | solution.py:83
  370.2 3.4 collective-permute-done.29.refs_1_
  374.6 3.7 shard_map.292
  378.4 15.4 %shard_map.293 = (bf16[4,144,1728]{2,1,0:T(8,128)(2,1)}, bf16[4,144,1728]{2,1,0:T(8,128)(2,1)}) custom-call(s32[1]{0:T(128)} %bitcast.meta_ref, bf16[512,1152]{1,0:T(8,128)(2,1)} %get-tuple-element.155.refs_0_, bf16[512,1152]{1,0:T(8,128)(2,1)} %copy-done.4, bf16[512,1152]{1,0:T(8,128)(2,1)} %collective-permute-done.20.refs_0_.refs_2_, ...), custom_call_target="tpu_custom_call" | custom-call | flops 163074544 | bytes 79626 | tf_op jit(solution)/shard_map/pallas_call | solution.py:83
  393.8 4.4 shard_map.294
  398.6 15.4 %shard_map.295 = (bf16[4,144,1728]{2,1,0:T(8,128)(2,1)}, bf16[4,144,1728]{2,1,0:T(8,128)(2,1)}) custom-call(s32[1]{0:T(128)} %bitcast.meta_ref, bf16[512,1152]{1,0:T(8,128)(2,1)} %get-tuple-element.155.refs_0_, bf16[512,1152]{1,0:T(8,128)(2,1)} %copy-done.4, bf16[512,1152]{1,0:T(8,128)(2,1)} %collective-permute-done.20.refs_0_.refs_2_, ...), custom_call_target="tpu_custom_call" | custom-call | flops 163074544 | bytes 79626 | tf_op jit(solution)/shard_map/pallas_call | solution.py:83
  413.9 11.6 %collective-permute-done.32.c_ref = bf16[512,1152]{1,0:T(8,128)(2,1)} collective-permute-done((bf16[512,1152]{1,0:T(8,128)(2,1)S(1)}, bf16[512,1152]{1,0:T(8,128)(2,1)}, u32[]{:S(2)}, u32[]{:S(2)}) %collective-permute-start.32) | collective-permute-done | bytes 1179680 | tf_op jit(solution)/shard_map/ppermute | solution.py:685
  425.5 9.9 %shard_map.296 = (f32[512,1152]{1,0:T(8,128)}, bf16[512,1152]{1,0:T(8,128)(2,1)}, bf16[512,256]{1,0:T(8,128)(2,1)}, bf16[512,256]{1,0:T(8,128)(2,1)}, bf16[512,2...) custom-call(s32[1]{0:T(128)} %bitcast.1.me_ref, bf16[512,1152]{1,0:T(8,128)(2,1)} %get-tuple-element.159.a_ref, ...), custom_call_target="tpu_custom_call" | custom-call | flops 24159192 | bytes 91842 | tf_op jit(solution)/shard_map/pallas_call | solution.py:83
  438.7 6.5 collective-permute-done.34.refs_2_
  445.2 5.7 collective-permute-done.35.refs_3_
  450.9 4.4 shard_map.297
  455.4 19.0 %shard_map.298 = (f32[2048,256]{1,0:T(8,128)}, f32[2048,256]{1,0:T(8,128)}, bf16[2048,256]{1,0:T(8,128)(2,1)}) custom-call(s32[9]{0:T(128)} %stack.161.meta_ref, bf16[2048,256]{1,0:T(8,128)(2,1)} %get-tuple-element.107.q_ref, bf16[2048,256]{1,0:T(8,128)(2,1)} %get-tuple-element.108.mine_ref, bf16[2048,256]{1,0:T(8,128)(2,1)} %copy-done.11, ...), custom_call_target="tpu_custom_call" | custom-call | flops 171798688 | bytes 104857 | tf_op jit(solution)/shard_map/pallas_call | solution.py:83
  478.3 11.7 %shard_map.299 = (bf16[2048,512]{1,0:T(8,128)(2,1)}, f32[1,256]{1,0:T(1,128)}, f32[1,256]{1,0:T(1,128)}, bf16[512,1152]{1,0:T(8,128)(2,1)}, bf16[512,1152]{1,0:T...) custom-call(s32[1]{0:T(128)} %bitcast.2.core_ref, f32[2048,256]{1,0:T(8,128)} %get-tuple-element.170.refs_0_, ...), custom_call_target="tpu_custom_call" | custom-call | flops 48318384 | bytes 136355 | tf_op jit(solution)/shard_map/pallas_call | solution.py:83
  490.0 7.0 %convolution_convert_fusion.1 = bf16[1152,512]{1,0:T(8,128)(2,1)} fusion(bf16[2048,1152]{1,0:T(8,128)(2,1)} %get-tuple-element.182, bf16[2048,512]{1,0:T(8,128)(2,1)} %get-tuple-element.184), kind=kOutput, calls=%fused_computation.5 | convolution fusion | flops 2416508928 | bytes 7995392 | tf_op jit(solution)/shard_map/dot_general | solution.py:46
  501.4 20.8 %collective-permute-done.51.refs_1_ = bf16[4,144,1728]{2,1,0:T(8,128)(2,1)} collective-permute-done((bf16[4,144,1728]{2,1,0:T(8,128)(2,1)}, bf16[4,144,1728]{2,1,0:T(8,128)(2,1)}, u32[]{:S(2)}, u32[]{:S(2)}) %collective-permute-start.51) | collective-permute-done | bytes 1990688 | tf_op jit(solution)/shard_map/ppermute | solution.py:718
  523.2 4.5 shard_map.301
  537.3 9.0 %collective-permute-done.43 = bf16[8,32,1152]{2,1,0:T(8,128)(2,1)} collective-permute-done((bf16[8,32,1152]{2,1,0:T(8,128)(2,1)}, bf16[8,32,1152]{2,1,0:T(8,128)(2,1)}, u32[]{:S(2)}, u32[]{:S(2)}) %collective-permute-start.43) | collective-permute-done | bytes 589856 | tf_op jit(solution)/shard_map/ppermute | solution.py:685
  565.4 4.2 concatenate.209
  571.8 3.3 collective-permute-done.47.refs_1_
  575.1 3.9 shard_map.300
  583.1 5.6 collective-permute-done.40
  591.4 9.0 %collective-permute-done.49 = bf16[144,896]{1,0:T(8,128)(2,1)S(1)} collective-permute-done((bf16[144,896]{1,0:T(8,128)(2,1)S(1)}, bf16[144,896]{1,0:T(8,128)(2,1)S(1)}, u32[]{:S(2)}, u32[]{:S(2)}) %collective-permute-start.49) | collective-permute-done | bytes 258080 | tf_op jit(solution)/shard_map/ppermute | solution.py:721
  600.3 4.7 collective-permute-done.50
  613.9 4.7 fusion.2
  623.1 8.2 %collective-permute-done.59 = bf16[144,1728]{1,0:T(8,128)(2,1)S(1)} collective-permute-done((bf16[144,1728]{1,0:T(8,128)(2,1)S(1)}, bf16[144,1728]{1,0:T(8,128)(2,1)S(1)}, u32[]{:S(2)}, u32[]{:S(2)}) %collective-permute-start.59) | collective-permute-done | bytes 497696 | tf_op jit(solution)/shard_map/ppermute | solution.py:685
  646.0 4.2 concatenate.210
  (343 shorter events, 155.9 us)
Async XLA Ops:
  7.2 94.5 %all-gather.4.cloned.1.call-start = ((), (), s32[]{:S(2)}) async-start(), calls=%async_computation.3 | async-start | bytes 2580480 | tf_op jit(solution)/shard_map/all_gather | solution.py:726
  13.6 27.6 %collective-permute-start.1 = (bf16[512,1152]{1,0:T(8,128)(2,1)}, bf16[512,1152]{1,0:T(8,128)(2,1)S(1)}, u32[]{:S(2)}, u32[]{:S(2)}) collective-permute-start(bf16[512,1152]{1,0:T(8,128)(2,1)} %x_ref.1), channel_id=1, source_target_pairs={{0,2},{1,3},{2,0},{3,1},{4,6},{5,7},{6,4},{7,5},{8,10},{9,11},{10,... | collective-permute-start | bytes 3538952 | tf_op jit(solution)/shard_map/ppermute | solution.py:685
  16.2 21.9 %collective-permute-start.3 = (bf16[208,640]{1,0:T(8,128)(2,1)S(1)}, bf16[208,640]{1,0:T(8,128)(2,1)S(1)}, u32[]{:S(2)}, u32[]{:S(2)}) collective-permute-start(bf16[208,640]{1,0:T(8,128)(2,1)S(1)} %fusion.9.refs_4_), channel_id=1, source_target_pairs={{0,16},{4,20},{8,24},{12,28},{16,0},{20,4},{24,8},{28,12},{1,17},{... | collective-permute-start | bytes 798728 | tf_op jit(solution)/shard_map/ppermute | solution.py:721
  17.2 24.0 %collective-permute-start.4 = (bf16[208,640]{1,0:T(8,128)(2,1)S(1)}, bf16[208,640]{1,0:T(8,128)(2,1)S(1)}, u32[]{:S(2)}, u32[]{:S(2)}) collective-permute-start(bf16[208,640]{1,0:T(8,128)(2,1)S(1)} %fusion.9.refs_4_), channel_id=1, source_target_pairs={{0,24},{4,28},{8,0},{12,4},{16,8},{20,12},{24,16},{28,20},{1,25},{... | collective-permute-start | bytes 798728 | tf_op jit(solution)/shard_map/ppermute | solution.py:721
  44.7 90.8 %all-gather.6.cloned.1.call-start = ((), (), s32[]{:S(2)}) async-start(), calls=%async_computation.4 | async-start | bytes 2580480 | tf_op jit(solution)/shard_map/all_gather | solution.py:726
  47.8 184.8 %all-gather.8.cloned.1.call-start = ((), (), s32[]{:S(2)}) async-start(), calls=%async_computation.5 | async-start | bytes 4976640 | tf_op jit(solution)/shard_map/all_gather | solution.py:726
  49.2 12.1 %collective-permute-start.22 = (bf16[216,1152]{1,0:T(8,128)(2,1)S(1)}, bf16[216,1152]{1,0:T(8,128)(2,1)}, u32[]{:S(2)}, u32[]{:S(2)}) collective-permute-start(bf16[216,1152]{1,0:T(8,128)(2,1)S(1)} %dynamic-slice_convert_fusion), channel_id=1, source_target_pairs={{0,4},{4,0},{8,12},{12,8},{16,20},{20,16},{24,28},{28,24},{1,5},{5... | collective-permute-start | bytes 1493000 | tf_op jit(solution)/shard_map/ppermute | solution.py:718
  50.5 36.8 %collective-permute-start = (bf16[512,1152]{1,0:T(8,128)(2,1)S(1)}, bf16[512,1152]{1,0:T(8,128)(2,1)}, u32[]{:S(2)}, u32[]{:S(2)}) collective-permute-start(bf16[512,1152]{1,0:T(8,128)(2,1)S(1)} %copy-done.2), channel_id=1, source_target_pairs={{0,1},{1,0},{2,3},{3,2},{4,5},{5,4},{6,7},{7,6},{8,9},{9,8},{10,11... | collective-permute-start | bytes 3538952 | tf_op jit(solution)/shard_map/ppermute | solution.py:685
  51.7 35.5 %collective-permute-start.5 = (bf16[512,1152]{1,0:T(8,128)(2,1)S(1)}, bf16[512,1152]{1,0:T(8,128)(2,1)}, u32[]{:S(2)}, u32[]{:S(2)}) collective-permute-start(bf16[512,1152]{1,0:T(8,128)(2,1)S(1)} %collective-permute-done.1.refs_2_), channel_id=1, source_target_pairs={{0,1},{1,0},{2,3},{3,2},{4,5},{5,4},{6,7},{7,6},{8,9},{9,8},{10,11... | collective-permute-start | bytes 3538952 | tf_op jit(solution)/shard_map/ppermute | solution.py:685
  63.9 412.9 %reduce-scatter.10.cloned.1.call-start = ((), (), s32[]{:S(2)}) async-start(), calls=%async_computation.8 | async-start | bytes 2488320
  66.0 10.9 %collective-permute-start.7 = (bf16[208,640]{1,0:T(8,128)(2,1)S(1)}, bf16[208,640]{1,0:T(8,128)(2,1)S(1)}, u32[]{:S(2)}, u32[]{:S(2)}) collective-permute-start(bf16[208,640]{1,0:T(8,128)(2,1)S(1)} %copy-done.38), channel_id=1, source_target_pairs={{0,4},{4,0},{8,12},{12,8},{16,20},{20,16},{24,28},{28,24},{1,5},{5... | collective-permute-start | bytes 798728 | tf_op jit(solution)/shard_map/ppermute | solution.py:718
  66.3 15.2 %collective-permute-start.8 = (bf16[208,640]{1,0:T(8,128)(2,1)}, bf16[208,640]{1,0:T(8,128)(2,1)S(1)}, u32[]{:S(2)}, u32[]{:S(2)}) collective-permute-start(bf16[208,640]{1,0:T(8,128)(2,1)} %copy-done.39), channel_id=1, source_target_pairs={{0,4},{4,0},{8,12},{12,8},{16,20},{20,16},{24,28},{28,24},{1,5},{5... | collective-permute-start | bytes 798728 | tf_op jit(solution)/shard_map/ppermute | solution.py:718
  70.1 17.1 %collective-permute-start.9 = (bf16[208,640]{1,0:T(8,128)(2,1)}, bf16[208,640]{1,0:T(8,128)(2,1)S(1)}, u32[]{:S(2)}, u32[]{:S(2)}) collective-permute-start(bf16[208,640]{1,0:T(8,128)(2,1)} %copy-done.40), channel_id=1, source_target_pairs={{0,4},{4,0},{8,12},{12,8},{16,20},{20,16},{24,28},{28,24},{1,5},{5... | collective-permute-start | bytes 798728 | tf_op jit(solution)/shard_map/ppermute | solution.py:718
  101.7 46.8 %collective-permute-start.11 = (bf16[4,144,1728]{2,1,0:T(8,128)(2,1)}, bf16[4,144,1728]{2,1,0:T(8,128)(2,1)}, u32[]{:S(2)}, u32[]{:S(2)}) collective-permute-start(bf16[4,144,1728]{2,1,0:T(8,128)(2,1)} %bitcast.150), channel_id=1, source_target_pairs={{0,4},{4,0},{8,12},{12,8},{16,20},{20,16},{24,28},{28,24},{1,5},{5... | collective-permute-start | bytes 5971976 | tf_op jit(solution)/shard_map/ppermute | solution.py:718
  124.4 14.7 %collective-permute-start.16 = (bf16[256,1152]{1,0:T(8,128)(2,1)S(1)}, bf16[256,1152]{1,0:T(8,128)(2,1)S(1)}, u32[]{:S(2)}, u32[]{:S(2)}) collective-permute-start(bf16[256,1152]{1,0:T(8,128)(2,1)S(1)} %copy-done.32), channel_id=1, source_target_pairs={{0,2},{1,3},{2,0},{3,1},{4,6},{5,7},{6,4},{7,5},{8,10},{9,11},{10,... | collective-permute-start | bytes 1769480 | tf_op jit(solution)/shard_map/ppermute | solution.py:685
  135.5 57.3 %collective-permute-start.19 = (bf16[4,144,1728]{2,1,0:T(8,128)(2,1)}, bf16[4,144,1728]{2,1,0:T(8,128)(2,1)S(1)}, u32[]{:S(2)}, u32[]{:S(2)}) collective-permute-start(bf16[4,144,1728]{2,1,0:T(8,128)(2,1)} %bitcast.152), channel_id=1, source_target_pairs={{0,4},{4,0},{8,12},{12,8},{16,20},{20,16},{24,28},{28,24},{1,5},{5... | collective-permute-start | bytes 5971976 | tf_op jit(solution)/shard_map/ppermute | solution.py:718
  136.6 20.5 %collective-permute-start.15 = (bf16[256,1152]{1,0:T(8,128)(2,1)S(1)}, bf16[256,1152]{1,0:T(8,128)(2,1)S(1)}, u32[]{:S(2)}, u32[]{:S(2)}) collective-permute-start(bf16[256,1152]{1,0:T(8,128)(2,1)S(1)} %copy-done.32), channel_id=1, source_target_pairs={{0,1},{1,0},{2,3},{3,2},{4,5},{5,4},{6,7},{7,6},{8,9},{9,8},{10,11... | collective-permute-start | bytes 1769480 | tf_op jit(solution)/shard_map/ppermute | solution.py:685
  139.1 18.0 %collective-permute-start.17 = (bf16[256,1152]{1,0:T(8,128)(2,1)S(1)}, bf16[256,1152]{1,0:T(8,128)(2,1)S(1)}, u32[]{:S(2)}, u32[]{:S(2)}) collective-permute-start(bf16[256,1152]{1,0:T(8,128)(2,1)S(1)} %collective-permute-done.16.refs_6_), channel_id=1, source_target_pairs={{0,1},{1,0},{2,3},{3,2},{4,5},{5,4},{6,7},{7,6},{8,9},{9,8},{10,11... | collective-permute-start | bytes 1769480 | tf_op jit(solution)/shard_map/ppermute | solution.py:685
  148.5 8.6 %collective-permute-start.14 = (bf16[512,256]{1,0:T(8,128)(2,1)}, bf16[512,256]{1,0:T(8,128)(2,1)S(1)}, u32[]{:S(2)}, u32[]{:S(2)}) collective-permute-start(bf16[512,256]{1,0:T(8,128)(2,1)} %get-tuple-element.115), channel_id=1, source_target_pairs={{0,3},{1,2},{2,1},{3,0},{4,7},{5,6},{6,5},{7,4},{8,11},{9,10},{10,... | collective-permute-start | bytes 786440 | tf_op jit(solution)/shard_map/ppermute | solution.py:685
  165.4 27.4 %collective-permute-start.18 = (bf16[512,1152]{1,0:T(8,128)(2,1)}, bf16[512,1152]{1,0:T(8,128)(2,1)S(1)}, u32[]{:S(2)}, u32[]{:S(2)}) collective-permute-start(bf16[512,1152]{1,0:T(8,128)(2,1)} %get-tuple-element.155.refs_0_), channel_id=1, source_target_pairs={{0,1},{1,0},{2,3},{3,2},{4,5},{5,4},{6,7},{7,6},{8,9},{9,8},{10,11... | collective-permute-start | bytes 3538952 | tf_op jit(solution)/shard_map/ppermute | solution.py:685
  166.3 45.7 %collective-permute-start.20 = (bf16[512,1152]{1,0:T(8,128)(2,1)}, bf16[512,1152]{1,0:T(8,128)(2,1)}, u32[]{:S(2)}, u32[]{:S(2)}) collective-permute-start(bf16[512,1152]{1,0:T(8,128)(2,1)} %get-tuple-element.155.refs_0_), channel_id=1, source_target_pairs={{0,2},{1,3},{2,0},{3,1},{4,6},{5,7},{6,4},{7,5},{8,10},{9,11},{10,... | collective-permute-start | bytes 3538952 | tf_op jit(solution)/shard_map/ppermute | solution.py:685
  242.1 10.3 %collective-permute-start.24 = (bf16[512,1152]{1,0:T(8,128)(2,1)}, bf16[512,1152]{1,0:T(8,128)(2,1)S(1)}, u32[]{:S(2)}, u32[]{:S(2)}) collective-permute-start(bf16[512,1152]{1,0:T(8,128)(2,1)} %get-tuple-element.130), channel_id=1, source_target_pairs={{0,1},{1,0},{2,3},{3,2},{4,5},{5,4},{6,7},{7,6},{8,9},{9,8},{10,11... | collective-permute-start | bytes 3538952 | tf_op jit(solution)/shard_map/ppermute | solution.py:685
  257.2 27.4 %collective-permute-start.25 = (bf16[512,1152]{1,0:T(8,128)(2,1)}, bf16[512,1152]{1,0:T(8,128)(2,1)S(1)}, u32[]{:S(2)}, u32[]{:S(2)}) collective-permute-start(bf16[512,1152]{1,0:T(8,128)(2,1)} %shard_map.287), channel_id=1, source_target_pairs={{0,2},{1,3},{2,0},{3,1},{4,6},{5,7},{6,4},{7,5},{8,10},{9,11},{10,... | collective-permute-start | bytes 3538952 | tf_op jit(solution)/shard_map/ppermute | solution.py:685
  292.7 29.9 %collective-permute-start.27 = (bf16[512,1152]{1,0:T(8,128)(2,1)}, bf16[512,1152]{1,0:T(8,128)(2,1)S(1)}, u32[]{:S(2)}, u32[]{:S(2)}) collective-permute-start(bf16[512,1152]{1,0:T(8,128)(2,1)} %get-tuple-element.136.refs_0_.refs_2_), channel_id=1, source_target_pairs={{0,2},{1,3},{2,0},{3,1},{4,6},{5,7},{6,4},{7,5},{8,10},{9,11},{10,... | collective-permute-start | bytes 3538952 | tf_op jit(solution)/shard_map/ppermute | solution.py:685
  341.6 52.2 %collective-permute-start.31 = (bf16[4,216,1152]{2,1,0:T(8,128)(2,1)}, bf16[4,216,1152]{2,1,0:T(8,128)(2,1)}, u32[]{:S(2)}, u32[]{:S(2)}) collective-permute-start(bf16[4,216,1152]{2,1,0:T(8,128)(2,1)} %get-tuple-element.142), channel_id=1, source_target_pairs={{0,4},{4,0},{8,12},{12,8},{16,20},{20,16},{24,28},{28,24},{1,5},{5... | collective-permute-start | bytes 5971976 | tf_op jit(solution)/shard_map/ppermute | solution.py:718
  398.2 137.0 %reduce-scatter.6.cloned.1.call-start = ((), (), s32[]{:S(2)}) async-start(), calls=%async_computation.6 | async-start | bytes 2580480 | tf_op jit(solution)/shard_map/reduce_scatter | solution.py:770
  398.3 52.6 %collective-permute-start.36 = (bf16[4,144,1728]{2,1,0:T(8,128)(2,1)}, bf16[4,144,1728]{2,1,0:T(8,128)(2,1)}, u32[]{:S(2)}, u32[]{:S(2)}) collective-permute-start(bf16[4,144,1728]{2,1,0:T(8,128)(2,1)} %get-tuple-element.153), channel_id=1, source_target_pairs={{0,4},{4,0},{8,12},{12,8},{16,20},{20,16},{24,28},{28,24},{1,5},{5... | collective-permute-start | bytes 5971976 | tf_op jit(solution)/shard_map/ppermute | solution.py:718
  398.6 27.0 %collective-permute-start.32 = (bf16[512,1152]{1,0:T(8,128)(2,1)S(1)}, bf16[512,1152]{1,0:T(8,128)(2,1)}, u32[]{:S(2)}, u32[]{:S(2)}) collective-permute-start(bf16[512,1152]{1,0:T(8,128)(2,1)S(1)} %copy-done.18), channel_id=1, source_target_pairs={{0,2},{1,3},{2,0},{3,1},{4,6},{5,7},{6,4},{7,5},{8,10},{9,11},{10,... | collective-permute-start | bytes 3538952 | tf_op jit(solution)/shard_map/ppermute | solution.py:685
  437.0 13.8 %collective-permute-start.35 = (bf16[512,256]{1,0:T(8,128)(2,1)}, bf16[512,256]{1,0:T(8,128)(2,1)S(1)}, u32[]{:S(2)}, u32[]{:S(2)}) collective-permute-start(bf16[512,256]{1,0:T(8,128)(2,1)} %get-tuple-element.167), channel_id=1, source_target_pairs={{0,3},{1,2},{2,1},{3,0},{4,7},{5,6},{6,5},{7,4},{8,11},{9,10},{10,... | collective-permute-start | bytes 786440 | tf_op jit(solution)/shard_map/ppermute | solution.py:685
  455.3 153.8 %reduce-scatter.8.cloned.1.call-start = ((), (), s32[]{:S(2)}) async-start(), calls=%async_computation.7 | async-start | bytes 2580480 | tf_op jit(solution)/shard_map/reduce_scatter | solution.py:770
  475.5 46.6 %collective-permute-start.51 = (bf16[4,144,1728]{2,1,0:T(8,128)(2,1)}, bf16[4,144,1728]{2,1,0:T(8,128)(2,1)}, u32[]{:S(2)}, u32[]{:S(2)}) collective-permute-start(bf16[4,144,1728]{2,1,0:T(8,128)(2,1)} %get-tuple-element.158), channel_id=1, source_target_pairs={{0,4},{4,0},{8,12},{12,8},{16,20},{20,16},{24,28},{28,24},{1,5},{5... | collective-permute-start | bytes 5971976 | tf_op jit(solution)/shard_map/ppermute | solution.py:718
  499.7 28.8 %collective-permute-start.42 = (bf16[8,32,1152]{2,1,0:T(8,128)(2,1)}, bf16[8,32,1152]{2,1,0:T(8,128)(2,1)}, u32[]{:S(2)}, u32[]{:S(2)}) collective-permute-start(bf16[8,32,1152]{2,1,0:T(8,128)(2,1)} %get-tuple-element.220), channel_id=1, source_target_pairs={{0,1},{1,0},{2,3},{3,2},{4,5},{5,4},{6,7},{7,6},{8,9},{9,8},{10,11... | collective-permute-start | bytes 1769480 | tf_op jit(solution)/shard_map/ppermute | solution.py:685
  499.9 28.6 %collective-permute-start.45 = (bf16[216,1152]{1,0:T(8,128)(2,1)}, bf16[216,1152]{1,0:T(8,128)(2,1)}, u32[]{:S(2)}, u32[]{:S(2)}) collective-permute-start(bf16[216,1152]{1,0:T(8,128)(2,1)} %reduce-scatter.10.cloned.1.call-done), channel_id=1, source_target_pairs={{0,2},{1,3},{2,0},{3,1},{4,6},{5,7},{6,4},{7,5},{8,10},{9,11},{10,... | collective-permute-start | bytes 1493000 | tf_op jit(solution)/shard_map/ppermute | solution.py:685
  500.7 35.8 %collective-permute-start.41 = (bf16[8,32,1152]{2,1,0:T(8,128)(2,1)}, bf16[8,32,1152]{2,1,0:T(8,128)(2,1)S(1)}, u32[]{:S(2)}, u32[]{:S(2)}) collective-permute-start(bf16[8,32,1152]{2,1,0:T(8,128)(2,1)} %get-tuple-element.219), channel_id=1, source_target_pairs={{0,1},{1,0},{2,3},{3,2},{4,5},{5,4},{6,7},{7,6},{8,9},{9,8},{10,11... | collective-permute-start | bytes 1769480 | tf_op jit(solution)/shard_map/ppermute | solution.py:685
  501.3 56.9 %collective-permute-start.39 = (bf16[512,1152]{1,0:T(8,128)(2,1)}, bf16[512,1152]{1,0:T(8,128)(2,1)}, u32[]{:S(2)}, u32[]{:S(2)}) collective-permute-start(bf16[512,1152]{1,0:T(8,128)(2,1)} %get-tuple-element.181), channel_id=1, source_target_pairs={{0,1},{1,0},{2,3},{3,2},{4,5},{5,4},{6,7},{7,6},{8,9},{9,8},{10,11... | collective-permute-start | bytes 3538952 | tf_op jit(solution)/shard_map/ppermute | solution.py:685
  522.1 61.0 %collective-permute-start.38 = (bf16[512,1152]{1,0:T(8,128)(2,1)}, bf16[512,1152]{1,0:T(8,128)(2,1)}, u32[]{:S(2)}, u32[]{:S(2)}) collective-permute-start(bf16[512,1152]{1,0:T(8,128)(2,1)} %get-tuple-element.179), channel_id=1, source_target_pairs={{0,1},{1,0},{2,3},{3,2},{4,5},{5,4},{6,7},{7,6},{8,9},{9,8},{10,11... | collective-permute-start | bytes 3538952 | tf_op jit(solution)/shard_map/ppermute | solution.py:685
  531.1 15.2 %collective-permute-start.43 = (bf16[8,32,1152]{2,1,0:T(8,128)(2,1)}, bf16[8,32,1152]{2,1,0:T(8,128)(2,1)}, u32[]{:S(2)}, u32[]{:S(2)}) collective-permute-start(bf16[8,32,1152]{2,1,0:T(8,128)(2,1)} %fusion.3), channel_id=1, source_target_pairs={{0,2},{1,3},{2,0},{3,1},{4,6},{5,7},{6,4},{7,5},{8,10},{9,11},{10,... | collective-permute-start | bytes 1769480 | tf_op jit(solution)/shard_map/ppermute | solution.py:685
  535.2 22.2 %collective-permute-start.56 = (bf16[144,1728]{1,0:T(8,128)(2,1)}, bf16[144,1728]{1,0:T(8,128)(2,1)}, u32[]{:S(2)}, u32[]{:S(2)}) collective-permute-start(bf16[144,1728]{1,0:T(8,128)(2,1)} %reduce-scatter.6.cloned.1.call-done), channel_id=1, source_target_pairs={{0,2},{1,3},{2,0},{3,1},{4,6},{5,7},{6,4},{7,5},{8,10},{9,11},{10,... | collective-permute-start | bytes 1493000 | tf_op jit(solution)/shard_map/ppermute | solution.py:685
  551.7 23.3 %collective-permute-start.47 = (bf16[4,144,896]{2,1,0:T(8,128)(2,1)}, bf16[4,144,896]{2,1,0:T(8,128)(2,1)}, u32[]{:S(2)}, u32[]{:S(2)}) collective-permute-start(bf16[4,144,896]{2,1,0:T(8,128)(2,1)} %get-tuple-element.192), channel_id=1, source_target_pairs={{0,4},{4,0},{8,12},{12,8},{16,20},{20,16},{24,28},{28,24},{1,5},{5... | collective-permute-start | bytes 3096584 | tf_op jit(solution)/shard_map/ppermute | solution.py:718
  560.8 27.9 %collective-permute-start.40 = (bf16[512,1152]{1,0:T(8,128)(2,1)}, bf16[512,1152]{1,0:T(8,128)(2,1)}, u32[]{:S(2)}, u32[]{:S(2)}) collective-permute-start(bf16[512,1152]{1,0:T(8,128)(2,1)} %add_convert_fusion), channel_id=1, source_target_pairs={{0,2},{1,3},{2,0},{3,1},{4,6},{5,7},{6,4},{7,5},{8,10},{9,11},{10,... | collective-permute-start | bytes 3538952 | tf_op jit(solution)/shard_map/ppermute | solution.py:685
  580.2 11.1 %collective-permute-start.48 = (bf16[144,896]{1,0:T(8,128)(2,1)S(1)}, bf16[144,896]{1,0:T(8,128)(2,1)S(1)}, u32[]{:S(2)}, u32[]{:S(2)}) collective-permute-start(bf16[144,896]{1,0:T(8,128)(2,1)S(1)} %get-tuple-element.241), channel_id=1, source_target_pairs={{0,8},{4,12},{8,16},{12,20},{16,24},{20,28},{24,0},{28,4},{1,9},{5... | collective-permute-start | bytes 774152 | tf_op jit(solution)/shard_map/ppermute | solution.py:721
  580.4 19.9 %collective-permute-start.49 = (bf16[144,896]{1,0:T(8,128)(2,1)S(1)}, bf16[144,896]{1,0:T(8,128)(2,1)S(1)}, u32[]{:S(2)}, u32[]{:S(2)}) collective-permute-start(bf16[144,896]{1,0:T(8,128)(2,1)S(1)} %get-tuple-element.243), channel_id=1, source_target_pairs={{0,16},{4,20},{8,24},{12,28},{16,0},{20,4},{24,8},{28,12},{1,17},{... | collective-permute-start | bytes 774152 | tf_op jit(solution)/shard_map/ppermute | solution.py:721
  581.8 23.3 %collective-permute-start.50 = (bf16[144,896]{1,0:T(8,128)(2,1)S(1)}, bf16[144,896]{1,0:T(8,128)(2,1)S(1)}, u32[]{:S(2)}, u32[]{:S(2)}) collective-permute-start(bf16[144,896]{1,0:T(8,128)(2,1)S(1)} %get-tuple-element.242), channel_id=1, source_target_pairs={{0,24},{4,28},{8,0},{12,4},{16,8},{20,12},{24,16},{28,20},{1,25},{... | collective-permute-start | bytes 774152 | tf_op jit(solution)/shard_map/ppermute | solution.py:721
  618.7 12.5 %collective-permute-start.59 = (bf16[144,1728]{1,0:T(8,128)(2,1)S(1)}, bf16[144,1728]{1,0:T(8,128)(2,1)S(1)}, u32[]{:S(2)}, u32[]{:S(2)}) collective-permute-start(bf16[144,1728]{1,0:T(8,128)(2,1)S(1)} %copy-done.14), channel_id=1, source_target_pairs={{0,2},{1,3},{2,0},{3,1},{4,6},{5,7},{6,4},{7,5},{8,10},{9,11},{10,... | collective-permute-start | bytes 1493000 | tf_op jit(solution)/shard_map/ppermute | solution.py:685
  620.3 12.5 %collective-permute-start.52 = (bf16[144,896]{1,0:T(8,128)(2,1)S(1)}, bf16[144,896]{1,0:T(8,128)(2,1)S(1)}, u32[]{:S(2)}, u32[]{:S(2)}) collective-permute-start(bf16[144,896]{1,0:T(8,128)(2,1)S(1)} %pad_maximum_fusion.6), channel_id=1, source_target_pairs={{0,1},{1,0},{2,3},{3,2},{4,5},{5,4},{6,7},{7,6},{8,9},{9,8},{10,11... | collective-permute-start | bytes 774152 | tf_op jit(solution)/shard_map/ppermute | solution.py:685
  621.5 11.4 %collective-permute-start.54 = (bf16[144,896]{1,0:T(8,128)(2,1)S(1)}, bf16[144,896]{1,0:T(8,128)(2,1)S(1)}, u32[]{:S(2)}, u32[]{:S(2)}) collective-permute-start(bf16[144,896]{1,0:T(8,128)(2,1)S(1)} %collective-permute-done.53), channel_id=1, source_target_pairs={{0,1},{1,0},{2,3},{3,2},{4,5},{5,4},{6,7},{7,6},{8,9},{9,8},{10,11... | collective-permute-start | bytes 774152 | tf_op jit(solution)/shard_map/ppermute | solution.py:685
  622.7 19.7 %collective-permute-start.58 = (bf16[144,1728]{1,0:T(8,128)(2,1)S(1)}, bf16[144,1728]{1,0:T(8,128)(2,1)S(1)}, u32[]{:S(2)}, u32[]{:S(2)}) collective-permute-start(bf16[144,1728]{1,0:T(8,128)(2,1)S(1)} %copy-done.14), channel_id=1, source_target_pairs={{0,1},{1,0},{2,3},{3,2},{4,5},{5,4},{6,7},{7,6},{8,9},{9,8},{10,11... | collective-permute-start | bytes 1493000 | tf_op jit(solution)/shard_map/ppermute | solution.py:685
  631.2 11.2 %collective-permute-start.60 = (bf16[144,1728]{1,0:T(8,128)(2,1)S(1)}, bf16[144,1728]{1,0:T(8,128)(2,1)S(1)}, u32[]{:S(2)}, u32[]{:S(2)}) collective-permute-start(bf16[144,1728]{1,0:T(8,128)(2,1)S(1)} %collective-permute-done.59), channel_id=1, source_target_pairs={{0,1},{1,0},{2,3},{3,2},{4,5},{5,4},{6,7},{7,6},{8,9},{9,8},{10,11... | collective-permute-start | bytes 1493000 | tf_op jit(solution)/shard_map/ppermute | solution.py:685
  (79 other events, 638.7 us)
Sparse Core Ops, SparseCore 0:
  44.8 44.9 all-gather.3
  91.4 43.9 all-gather.5
  137.1 75.1 all-gather.7
  398.3 39.7 reduce-scatter.9
  455.5 41.5 reduce-scatter.5
  527.9 40.4 reduce-scatter.7

commit v3 on v2

--- a/solution.py
+++ b/solution.py
@@ -65,7 +65,7 @@
     return pl.BlockSpec(shape, lambda *at: (0,) * len(shape), pipeline_mode=pl.Buffered(1))
 
 
-def call(kernel, grid, in_specs, out_specs, outs, flops, limit=60, scratch=(), exps=0):
+def call(kernel, grid, in_specs, out_specs, outs, flops, limit=60, scratch=(), exps=0, same=None):
     shapes = [jax.ShapeDtypeStruct(s, d) for s, d in outs]
     size = sum(o.size * o.dtype.itemsize for o in shapes)
     made = pl.pallas_call(
@@ -75,6 +75,7 @@
         out_specs=out_specs,
         out_shape=shapes,
         scratch_shapes=list(scratch),
+        input_output_aliases=same or {},
         compiler_params=pltpu.CompilerParams(vmem_limit_bytes=limit * MIB),
         cost_estimate=pl.CostEstimate(
             flops=flops // 50, bytes_accessed=size // 50, transcendentals=exps // 50
@@ -115,6 +116,10 @@
 def add_half(first, second, steps):
     function = lambda a, b: (a.astype(f32) + b.astype(f32),)
     return fused(function, [first, second], [], [(first.shape, bf16)], steps)[0]
+
+
+def pair_sum(first, second):
+    return to_half(first.astype(f32) + second.astype(f32))
 
 
 def rms_back(values, gain, grad):
@@ -487,6 +492,33 @@
     )(meta, queries, mine, other, probs, *grads)
 
 
+def spread_kernel(owners, me_ref, *refs):
+    blocks, out_ref, all_ref = refs[:SEQ], refs[SEQ], refs[SEQ + 1]
+    for r, block in enumerate(blocks):
+        all_ref[jnp.bitwise_xor(me_ref[0], r)] = block[...].astype(f32)
+    part = blocks[0].shape[1] // owners
+    out_ref[...] = jnp.concatenate(
+        [all_ref[t][:, f * part : (f + 1) * part] for f in range(owners) for t in range(SEQ)],
+        axis=1,
+    )
+
+
+def spread_columns(me, blocks, owners):
+    rows, width = blocks[0].shape
+    steps = 3 if rows % 48 == 0 else 1
+    step = rows // steps
+    row = lambda w: pl.BlockSpec((step, w), lambda i: (i, 0))
+    return call(
+        partial(spread_kernel, owners),
+        (steps,),
+        [pl.BlockSpec(memory_space=pltpu.SMEM)] + [row(width)] * SEQ,
+        [row(SEQ * width)],
+        [((rows, SEQ * width), f32)],
+        flops=0,
+        scratch=[pltpu.VMEM((SEQ, step, width), f32)],
+    )(me, *blocks)[0]
+
+
 def pick_block(blocks, into_ref):
     for r, block in enumerate(blocks):
 
@@ -495,24 +527,7 @@
             into_ref[...] = block[...]
 
 
-def gate_up_kernel(count, pieces, meta_ref, *refs):
-    parts, outs = refs[count : count + 2 * pieces], refs[count + 2 * pieces :]
-    act_ref, value_ref, slope_ref = outs[:3]
-    x_ref = outs[-1]
-    gate_ref, up_ref = outs[3:5] if pieces == 2 else parts
-
-    if pieces == 2:
-
-        @pl.when(pl.program_id(0) == 0)
-        def _():
-            for w_ref, own in ((gate_ref, parts[:2]), (up_ref, parts[2:])):
-                for half, ref in enumerate(own):
-                    size = ref.shape[1]
-                    for z in range(ref.shape[0]):
-                        start = (2 * z + jnp.bitwise_xor(meta_ref[0], half)) * size
-                        w_ref[pl.ds(pl.multiple_of(start, 16), size), :] = ref[z]
-
-    pick_block(refs[:count], x_ref)
+def feed_rows(x_ref, gate_ref, up_ref, act_ref, value_ref, slope_ref):
     rows = x_ref[...]
     gate = mult(rows, gate_ref[...])
     upper = mult(rows, up_ref[...])
@@ -527,26 +542,74 @@
     slope_ref[...] = to_half(slope * upper)
 
 
-def gate_up(meta, blocks, gate_parts, up_parts):
+def gate_up_kernel(count, pieces, kept, meta_ref, *refs):
+    parts, outs = refs[count : count + 2 * pieces], refs[count + 2 * pieces + kept :]
+    act_ref, value_ref, slope_ref = outs[:3]
+    x_ref = outs[-1]
+    gate_ref, up_ref = outs[3:5] if pieces == 2 else parts
+
+    if pieces == 2:
+
+        @pl.when(pl.program_id(0) == 0)
+        def _():
+            for w_ref, own in ((gate_ref, parts[:2]), (up_ref, parts[2:])):
+                for half, ref in enumerate(own):
+                    size = ref.shape[1]
+                    for z in range(ref.shape[0]):
+                        start = (2 * z + jnp.bitwise_xor(meta_ref[0], half)) * size
+                        w_ref[pl.ds(pl.multiple_of(start, 16), size), :] = ref[z]
+
+    pick_block(refs[:count], x_ref)
+    feed_rows(x_ref, gate_ref, up_ref, act_ref, value_ref, slope_ref)
+
+
+def gate_up(meta, blocks, gate_parts, up_parts, first, saved):
     block, model = blocks[0].shape
     width = gate_parts[0].shape[-1]
-    total = block * len(blocks)
-    slab = pl.BlockSpec((block, width), lambda i: (i, 0))
+    total = block * SEQ
+    slab = pl.BlockSpec((block, width), lambda i: (i + first, 0))
     whole = pl.BlockSpec((model, width), lambda i: (0, 0))
     parts = [*gate_parts, *up_parts]
     made = len(parts) - 2
+    ins = 1 + len(blocks) + len(parts)
     out = call(
-        partial(gate_up_kernel, len(blocks), len(gate_parts)),
+        partial(gate_up_kernel, len(blocks), len(gate_parts), len(saved)),
         (len(blocks),),
-        [pl.BlockSpec(memory_space=pltpu.SMEM)] + [held(b.shape) for b in [*blocks, *parts]],
+        [pl.BlockSpec(memory_space=pltpu.SMEM)]
+        + [held(b.shape) for b in [*blocks, *parts]]
+        + [pl.BlockSpec(memory_space=pl.ANY)] * len(saved),
         [slab] * 3 + [whole] * made,
         [((total, width), bf16)] * 3 + [((model, width), bf16)] * made,
         flops=4 * total * model * width,
         exps=total * width,
         scratch=[pltpu.VMEM((block, model), bf16)],
         limit=62,
-    )(meta, *blocks, *parts)
+        same={ins + i: i for i in range(len(saved))},
+    )(meta, *blocks, *parts, *saved)
     return out if made else out + parts
+
+
+def feed_kernel(x_ref, gate_ref, up_ref, down_ref, *refs):
+    act_ref, value_ref, slope_ref, out_ref = refs[3:]
+    feed_rows(x_ref, gate_ref, up_ref, act_ref, value_ref, slope_ref)
+    out_ref[...] = to_half(mult(act_ref[...], down_ref[...]))
+
+
+def feed_first(rows, w_gate, w_up, w_down, saved):
+    block, model = rows.shape
+    width = w_gate.shape[1]
+    slab = pl.BlockSpec((block, width), lambda i: (0, 0))
+    return call(
+        feed_kernel,
+        (1,),
+        [held(v.shape) for v in [rows, w_gate, w_up, w_down]]
+        + [pl.BlockSpec(memory_space=pl.ANY)] * 3,
+        [slab] * 3 + [pl.BlockSpec((block, model), lambda i: (0, 0))],
+        [(v.shape, bf16) for v in saved] + [((block, model), bf16)],
+        flops=6 * block * model * width,
+        limit=62,
+        same={4: 0, 5: 1, 6: 2},
+    )(rows, w_gate, w_up, w_down, *saved)
 
 
 def down_kernel(x_ref, w_ref, *outs):
@@ -559,13 +622,13 @@
 
 
 def down(rows, w_down, count):
-    block = rows.shape[0] // count
+    block = rows.shape[0] // (count + 1)
     width, model = w_down.shape
     out = pl.BlockSpec((block, model), lambda i: (0, 0))
     return call(
         down_kernel,
         (count,),
-        [pl.BlockSpec((block, width), lambda i: (i, 0)), held(w_down.shape)],
+        [pl.BlockSpec((block, width), lambda i: (i + 1, 0)), held(w_down.shape)],
         [out] * count,
         [((block, model), bf16)] * count,
         flops=2 * count * block * model * width,
@@ -588,17 +651,18 @@
             ref[...] = out
 
 
-def back(blocks, value, slope, w_down, w_gate, w_up):
+def back(blocks, value, slope, w_down, w_gate, w_up, first):
     block, model = blocks[0].shape
     count = len(blocks)
     width = w_gate.shape[1]
+    ahead = pl.BlockSpec((block, width), lambda i: (i + first, 0))
     slab = pl.BlockSpec((block, width), lambda i: (i, 0))
     out = pl.BlockSpec((block, model), lambda i: (0, 0))
     return call(
         partial(back_kernel, count),
         (count,),
         [held(b.shape) for b in blocks]
-        + [slab, slab, held(w_down.shape), held(w_gate.shape), held(w_up.shape)],
+        + [ahead, ahead, held(w_down.shape), held(w_gate.shape), held(w_up.shape)],
         [slab, slab] + [out] * count,
         [((block * count, width), bf16)] * 2 + [((block, model), bf16)] * count,
         flops=6 * count * block * model * width,
@@ -758,10 +822,11 @@
         here = lax.dynamic_index_in_dim(view, self.low, 1, keepdims=False)
         return away, here
 
-    def product_halves(self, side, left, right, tile):
+    def product_halves(self, side, left, rights, tile):
         if (left[0].shape[1] // self.count) % 8 == 0:
-            return rows_product(side, left, [right], tile, self.count)
-        return self.halves(rows_product(side, left, [right], tile, self.count, False)[0])
+            return rows_product(side, left, rights, tile, self.count)
+        whole = rows_product(side, left, rights, tile, self.count, False)
+        return [half for value in whole for half in self.halves(value)]
 
     def fold(self, here, come):
         return add_half(here, come, here.shape[0])
@@ -884,7 +949,6 @@
         token_blocks, pieces, meta, cosine, sine, rows, short_rows, packed
     )
     gate_parts = owners.gather_wide(gate_own, queries)
-    g_input = gains[0]
     other_kv = swap_seq(mine_kv, 1)
     *heads, probs = attend(meta, queries, mine_kv, other_kv, code, low, high, scale, 256)
     up_parts = owners.gather_wide(up_own, probs)
@@ -899,21 +963,19 @@
         quarters = [w_out.transpose(1, 0, 2, 3).reshape(fsdp * out_rows, model)]
     heads[0] = after(heads[0], *gate_parts)
     heads16, w_out, attn, mixed, fed_own = mid(self_index, tokens, heads, quarters, gains, fsdp)
-    inputs32 = tokens.astype(f32)
 
     side = jnp.stack([owners.low]).astype(jnp.int32)
     fed_blocks = [fed_own, swap_seq(fed_own, 1), swap_seq(fed_own, 2)]
-    near_act, near_value, near_slope, w_gate, w_up = gate_up(
-        side, fed_blocks[:2], gate_parts, up_parts
-    )
-    fed_two = after(fed_blocks[2], near_act)
+    *saved, w_gate, w_up = gate_up(side, fed_blocks[1:2], gate_parts, up_parts, 1, [])
+    fed_two = after(fed_blocks[2], saved[0])
     fed_blocks = fed_blocks[:2] + [fed_two, swap_seq(fed_two, 1)]
-    far_act, far_value, far_slope, *_ = gate_up(side, fed_blocks[2:], [w_gate], [w_up])
-    far_share = down(far_act, w_down, 2)
-    near_act = after(near_act, *far_share)
-    share = down(near_act, w_down, 2) + far_share
-    share_pair = add_half(share[2], swap_seq(share[3], 1), 4)
-    shares = [share[0], swap_seq(share[1], 1), swap_seq(share_pair, 2)]
+    *saved, w_gate, w_up = gate_up(side, fed_blocks[2:], [w_gate], [w_up], 2, saved)
+    share_one, share_two, share_three = down(saved[0], w_down, 3)
+    share_one = swap_seq(share_one, 1)
+    share_pair = pair_sum(share_two, swap_seq(share_three, 1))
+    fed_first = after(fed_blocks[0], share_pair, share_one)
+    act16, value16, slope16, share = feed_first(fed_first, w_gate, w_up, w_down, saved)
+    shares = [share, share_one, swap_seq(share_pair, 2)]
 
     def feed_end(first, second, third, mixed, grad, gains):
         ffo = first.astype(f32) + second.astype(f32) + third.astype(f32)
@@ -932,24 +994,24 @@
 
     ffo_blocks = [ffo_own, swap_seq(ffo_own, 1), swap_seq(ffo_own, 2)]
     near_gate, near_up, *near_share = back(
-        ffo_blocks[:2], near_value, near_slope, w_down, w_gate, w_up
+        ffo_blocks[:2], value16, slope16, w_down, w_gate, w_up, 0
     )
     ffo_two = after(ffo_blocks[2], near_gate)
     ffo_blocks = ffo_blocks[:2] + [ffo_two, swap_seq(ffo_two, 1)]
-    away_down, here_down = owners.product_halves(side, [near_act, far_act], ffo_blocks, 256)
+    away_down, here_down = owners.product_halves(side, [act16], [ffo_blocks], 256)
     come_down = owners.swap(away_down)
     far_blocks = list(lax.optimization_barrier((away_down, *ffo_blocks[2:]))[1:])
-    far_gate, far_up, *far_share = back(far_blocks, far_value, far_slope, w_down, w_gate, w_up)
+    far_gate, far_up, *far_share = back(far_blocks, value16, slope16, w_down, w_gate, w_up, 2)
     pair = add_half(far_share[0], swap_seq(far_share[1], 1), 4)
     far_sum = swap_seq(pair, 2)
     near_one = swap_seq(near_share[1], 1)
     fed_left = [after(fed_blocks[0], pair, near_one)] + fed_blocks[1:]
-    away_gate, here_gate = owners.product_halves(side, fed_left, [near_gate, far_gate], 384)
+    away_gate, here_gate = owners.product_halves(side, fed_left, [[near_gate, far_gate]], 384)
     come_gate = owners.swap(away_gate)
     half_down = owners.fold(after(here_down, away_gate), come_down)
     grad_down = owners.scatter_row(half_down)
     fed_left = [after(fed_left[0], half_down)] + fed_left[1:]
-    away_up, here_up = owners.product_halves(side, fed_left, [near_up, far_up], 384)
+    away_up, here_up = owners.product_halves(side, fed_left, [[near_up, far_up]], 384)
     come_up = owners.swap(away_up)
     shares = [after(near_share[0], away_up), near_one, far_sum]
     grad_mixed, grad_attn16, *grad_heads, gain_mixed_part = mid_back(
@@ -976,18 +1038,23 @@
         head_gains,
         w_own,
     )
-    grad_normed = reduce_seq(normed_blocks)
-    grad_proj = to_half(inner_rows(normed16, after(grad_qkv16, normed_blocks[0])))
-    grad_out_share = to_half(inner_rows(heads16, after(grad_attn16, grad_proj)))
+    half_up = owners.fold(after(here_up, grad_qkv16), come_up)
+    grad_up = owners.scatter_row(half_up)
+    grad_out_share = to_half(inner_rows(heads16, after(grad_attn16, half_up)))
     grad_out_view = grad_out_share.reshape(fsdp, SEQ, out_part, model)
-    grad_out_part = reduce_seq(
-        [
-            lax.dynamic_index_in_dim(grad_out_view, me ^ r, 1, keepdims=False)
-            for r in range(SEQ)
-        ]
-    )
-    extra = out_part * model // rows
-    grad_out_part = to_half(grad_out_part).reshape(fsdp * rows, extra)
+    out_blocks = [
+        lax.dynamic_index_in_dim(grad_out_view, me ^ r, 1, keepdims=False) for r in range(SEQ)
+    ]
+    out_pair = pair_sum(out_blocks[2], swap_seq(out_blocks[3], 1))
+    out_one = pair_sum(out_blocks[0], swap_seq(out_blocks[1], 1))
+    out_two = swap_seq(out_pair, 2)
+    proj_left = after(normed16, out_pair, out_one)
+    away_proj, here_proj = owners.product_halves(side, [proj_left], [[grad_qkv16]], 384)
+    grad_out_part = pair_sum(out_one, after(out_two, away_proj))
+    normed_pair = pair_sum(normed_blocks[2], swap_seq(normed_blocks[3], 1))
+    normed_two = swap_seq(normed_pair, 2)
+    normed_one = swap_seq(normed_blocks[1], 1)
+    out_down = jnp.concatenate(natural(gather_seq(after(grad_down, away_proj)), me)).astype(f32)
 
     short = jnp.stack([gain_query_part[0], gain_key_part[0]], axis=1).reshape(fsdp, short_rows, 2)
     short = jnp.pad(short, ((0, 0), (0, rows - short_rows), (0, 0))).reshape(model, 2)
@@ -995,64 +1062,79 @@
         [jnp.stack([gain_mixed_part[0], gain_final_part[0]], axis=1), short], axis=1
     )
     gain_parts = jnp.pad(gain_parts, ((0, 0), (0, 128 - gain_parts.shape[1])))
-    half_up = owners.fold(after(here_up, grad_proj), come_up)
-    grad_up = owners.scatter_row(half_up)
-    downs = natural(gather_seq(grad_down), me)
-    out_down = jnp.concatenate(downs).astype(f32)
-    away_small, here_small = owners.halves(
-        jnp.concatenate([grad_proj, to_half(gain_parts), grad_out_part], axis=1)
-    )
-    half_small = owners.fold(here_small, owners.swap(after(away_small, out_down, grad_gate)))
+    away_gains, here_gains = owners.halves(to_half(gain_parts))
+    away_out, here_out = owners.halves(grad_out_part.reshape(fsdp * out_part, model))
+    wide = 2 * head_width + 128
+
+    def pile(proj, gains, out):
+        upper = jnp.concatenate([proj, gains], axis=2)
+        rest = jnp.pad(out[:, :, wide:], ((0, 0), (0, 0), (0, 2 * wide - model)))
+        return jnp.concatenate([upper, out[:, :, :wide], rest], axis=1)
+
+    away_small = pile(away_proj, away_gains, away_out)
+    here_small = pile(here_proj, here_gains, here_out)
+    come_small = owners.swap(after(away_small, grad_gate))
+    half_small = owners.fold(here_small, come_small)
     grad_small = owners.scatter_direct(half_small)
-    _, input_back = jax.vjp(lambda v: rms_scale(v, g_input), inputs32)
-    (grad_input_part,) = input_back(grad_normed)
-    grad_tokens = grad_mixed + grad_input_part
-
-    gates = natural(gather_seq(grad_gate), me)
-    ups = natural(gather_seq(grad_up), me)
-
-    def spread(blocks):
+
+    def input_end(first, second, third, values, grad, gains):
+        total = first.astype(f32) + second.astype(f32) + third.astype(f32)
+        return (grad + rms_back(values.astype(f32), gains[0:1], total)[0],)
+
+    (grad_tokens,) = fused(
+        input_end,
+        [normed_blocks[0], normed_one, normed_two, tokens, grad_mixed],
+        [gains],
+        [(tokens.shape, f32)],
+        4,
+    )
+
+    def spread(own):
+        blocks = gather_seq(own)
         if fsdp <= 8:
-            pieces = [
-                blocks[t][:, f * part : (f + 1) * part]
-                for f in range(fsdp)
-                for t in range(SEQ)
-            ]
-            return jnp.concatenate(pieces, axis=1).astype(f32)
-        stack = jnp.stack([b[:, : fsdp * part].reshape(rows, fsdp, part) for b in blocks], axis=2)
+            return spread_columns(self_index, blocks, fsdp)
+        stack = jnp.stack([b.reshape(rows, fsdp, part) for b in natural(blocks, me)], axis=2)
         return stack.reshape(rows, hidden).astype(f32)
 
-    out_gate = spread(gates)
-    out_up = spread(ups)
+    out_gate = spread(grad_gate)
+    out_up = spread(grad_up)
 
     feed_sum = jnp.sum(
         grad_gate.astype(f32) * gate_own.astype(f32)
         + grad_up.astype(f32) * up_own.astype(f32),
         axis=1,
     )
+    upper = grad_small[:rows]
     input_sum = jnp.sum(
-        grad_small[:, : 2 * head_width] * attn_own[:, : 2 * head_width].astype(f32), axis=1
+        upper[:, : 2 * head_width] * attn_own[:, : 2 * head_width].astype(f32), axis=1
     )
     tail = jnp.concatenate(
-        [grad_small[:, 2 * head_width : 2 * head_width + 4], jnp.stack([input_sum, feed_sum], axis=1)],
+        [upper[:, 2 * head_width : 2 * head_width + 4], jnp.stack([input_sum, feed_sum], axis=1)],
         axis=1,
     )
     tail = jnp.pad(tail, ((0, 0), (0, 128 - tail.shape[1])))
     small = gather_seq(
-        to_half(
-            jnp.concatenate(
-                [grad_small[:, : 2 * head_width], tail, grad_small[:, 2 * head_width + 128 :]], axis=1
-            )
+        jnp.concatenate(
+            [
+                to_half(jnp.concatenate([upper[:, : 2 * head_width], tail], axis=1)),
+                to_half(after(grad_small, out_up, out_gate, out_down, grad_tokens)[rows:]),
+            ]
         )
     )
-    outs = [b[:, 2 * head_width + 128 :].reshape(out_part, model) for b in natural(small, me)]
-    out_out = jnp.concatenate(outs).astype(f32)
+    lower = [b[rows:] for b in natural(small, me)]
+    out_out = jnp.concatenate(
+        [
+            jnp.concatenate([b[:out_part], b[out_part:, : model - wide]], axis=1)
+            for b in lower
+        ]
+    ).astype(f32)
+    small = [b[:rows] for b in small]
     out_query = jnp.concatenate([b[:, :head_width] for b in natural(small, me)], axis=1).astype(f32)
     kv = [b[:, head_width : 2 * head_width].astype(f32) for b in small]
     same, cross = kv[0] + kv[2], kv[1] + kv[3]
     out_key = jnp.where(core == 0, same, cross)
     out_value = jnp.where(core == 0, cross, same)
-    tails = sum(b[:, 2 * head_width : 2 * head_width + 128].astype(f32) for b in small)
+    tails = sum(b[:, 2 * head_width :].astype(f32) for b in small)
     own_gains = attn_own[:, 2 * head_width : 2 * head_width + 128].astype(f32)
     out_g_mixed = tails[:, 0]
     out_g_final = tails[:, 1]

time: 670 us -> 631 us (0.942)
  local copies, waits for them, and re-layouts: 55.4 us -> 31.5 us
  Pallas kernels: 258 us -> 280 us
  other arithmetic: 48.8 us -> 32.3 us
  waiting for transfers between devices: 226 us -> 214 us
    pallas_call x22 -> x25, Pallas kernels: 258 us -> 280 us  [call(): return lambda *operands: list(made(*operands))]
    concatenate x5 -> x1, local copies, waits for them, and re-layouts: 11 us -> 0.02 us  [body(): jnp.concatenate([upper[:, :2 * head_width], tail], axis=1)]
    slice x16 -> x17, local copies, waits for them, and re-layouts: 10.3 us -> 0.87 us  [the longest x2 0.68 us: pile(): rest = jnp.pad(out[:, :, wide:], ((0, 0), (0, 0), (0, 2 * wide - model)))]
    ppermute x6, waiting for transfers between devices: 36.2 us -> 27 us  [shift(): lax.ppermute(values, 'fsdp', [(i, (i + 2 * by) % self.count) for i in ran...]
    unnamed x120 -> x106, local copies, waits for them, and re-layouts: 13.2 us -> 14.8 us
  transfers between devices with their start and end apart: 67 -> 67, of which waited for: 32 -> 34; matrix products, arithmetic and copies ran while one was open for 12% -> 6% of each run, Pallas kernels for 34% -> 38%
where the time goes in v3:
time: 631 us; the launch traced here: 623 us
  Pallas kernels  280 us (44%)
  waiting for transfers between devices  214 us (34%)
  starting transfers between devices  47 us (7%)
  other arithmetic  32.3 us (5%)
  local copies, waits for them, and re-layouts  31.5 us (5%)
  between operations  15.1 us (2%)
    pallas_call x25, Pallas kernels, call(): return lambda *operands: list(made(*operands))  280 us
    ppermute x44, waiting for transfers between devices, swap_seq(): return lax.ppermute(values, 'seq', [(i, i ^ bits) for i in range(SEQ)])  101 us
    ppermute x11, waiting for transfers between devices, swap(): return lax.ppermute(values, 'fsdp', [(i, i ^ 1) for i in range(self.count)])  77.2 us
    ppermute x44, starting transfers between devices, swap_seq(): return lax.ppermute(values, 'seq', [(i, i ^ bits) for i in range(SEQ)])  30.6 us
    ppermute x6, waiting for transfers between devices, shift(): lax.ppermute(values, 'fsdp', [(i, (i + 2 * by) % self.count) for i in ran...  27 us
    unnamed x106, local copies, waits for them, and re-layouts  14.8 us
  transfers between devices with their start and end apart: 67, of which 34 were waited for; matrix products, arithmetic and copies ran while one was open for 6% of the time, Pallas kernels for 38%

profile of v3, /device:TPU:9, one launch (start us, length us, event | category | flops | bytes accessed | tf_op | source)
XLA Modules:
  0.0 623.2 jit_solution(11872626323705446229)
XLA Ops:
  18.1 3.2 collective-permute-done.2.refs_5_
  21.2 16.2 %collective-permute-done.3.refs_6_ = bf16[208,640]{1,0:T(8,128)(2,1)S(1)} collective-permute-done((bf16[208,640]{1,0:T(8,128)(2,1)S(1)}, bf16[208,640]{1,0:T(8,128)(2,1)S(1)}, u32[]{:S(2)}, u32[]{:S(2)}) %collective-permute-start.3) | collective-permute-done | bytes 266272 | tf_op jit(solution)/shard_map/ppermute | solution.py:785
  37.4 3.2 collective-permute-done.4.refs_7_
  52.0 10.7 %collective-permute-done.22 = bf16[216,1152]{1,0:T(8,128)(2,1)} collective-permute-done((bf16[216,1152]{1,0:T(8,128)(2,1)}, bf16[216,1152]{1,0:T(8,128)(2,1)}, u32[]{:S(2)}, u32[]{:S(2)}) %collective-permute-start.22) | collective-permute-done | bytes 497696 | tf_op jit(solution)/shard_map/ppermute | solution.py:782
  73.3 5.5 multiply_sine_fusion
  78.8 4.6 collective-permute-done.8.refs_10_
  83.5 5.7 collective-permute-done.9.refs_11_
  89.9 11.0 %shard_map.280 = (bf16[2048,1152]{1,0:T(8,128)(2,1)}, bf16[2048,256]{1,0:T(8,128)(2,1)}, bf16[2048,256]{1,0:T(8,128)(2,1)}, f32[2048,256]{1,0:T(8,128)}, f32[204...) custom-call(s32[9]{0:T(128)} %stack.140.meta_ref, ...), custom_call_target="tpu_custom_call" | custom-call | flops 48318384 | bytes 256491 | tf_op jit(solution)/shard_map/pallas_call | solution.py:84
  108.4 17.5 %shard_map.281 = (bf16[512,256]{1,0:T(8,128)(2,1)}, bf16[512,256]{1,0:T(8,128)(2,1)}, bf16[512,256]{1,0:T(8,128)(2,1)}, bf16[512,256]{1,0:T(8,128)(2,1)}, bf16[2048,2048]{1,0:T(8,128)(2,1)}) custom-call(s32[9]{0:T(128)} %stack.140.meta_ref, bf16[2048,256]{1,0:T(8,128)(2,1)} %get-tuple-element.115.q_ref, bf16[2048,256]{1,0:T(8,128)(2,1)} %get-tuple-element.116.mine_ref, ...), custom_call_target="tpu_custom_call" | custom-call | flops 85899344 | bytes 188743 | tf_op jit(solution)/shard_map/pallas_call | solution.py:84
  126.1 8.8 %all-gather.6.cloned.1.call-done = bf16[576,1728]{1,0:T(8,128)(2,1)} async-done(((bf16[144,1728]{1,0:T(8,128)(2,1)}), bf16[576,1728]{1,0:T(8,128)(2,1)}) %all-gather.6.cloned.1.call-update) | async-done | bytes 1990672 | tf_op jit(solution)/shard_map/all_gather | solution.py:790
  137.2 3.5 collective-permute-done.16.refs_6_
  143.9 6.0 collective-permute-done.11.refs_2_
  152.0 6.5 %collective-permute-done.14.refs_3_ = bf16[512,256]{1,0:T(8,128)(2,1)S(1)} collective-permute-done((bf16[512,256]{1,0:T(8,128)(2,1)}, bf16[512,256]{1,0:T(8,128)(2,1)S(1)}, u32[]{:S(2)}, u32[]{:S(2)}) %collective-permute-start.14) | collective-permute-done | bytes 262176 | tf_op jit(solution)/shard_map/ppermute | solution.py:749
  159.6 7.0 %shard_map.282 = (bf16[512,1024]{1,0:T(8,128)(2,1)}, bf16[1024,1152]{1,0:T(8,128)(2,1)}, f32[512,1152]{1,0:T(8,128)}, f32[512,1152]{1,0:T(8,128)}, bf16[512,1152]{1,0:T(8,128)(2,1)}) custom-call(s32[1]{0:T(128)} %bitcast.me_ref, bf16[512,1152]{1,0:T(8,128)(2,1)} %refs_3_.1, bf16[512,256]{1,0:T(8,128)(2,1)} %get-tuple-element.120.refs_0_, ...), custom_call_target="tpu_custom_call" | custom-call | flops 24159192 | bytes 186122 | tf_op jit(solution)/shard_map/pallas_call | solution.py:84
  167.5 26.7 %collective-permute-done.20.refs_4_ = bf16[4,144,1728]{2,1,0:T(8,128)(2,1)S(1)} collective-permute-done((bf16[4,144,1728]{2,1,0:T(8,128)(2,1)}, bf16[4,144,1728]{2,1,0:T(8,128)(2,1)S(1)}, u32[]{:S(2)}, u32[]{:S(2)}) %collective-permute-start.20) | collective-permute-done | bytes 1990688 | tf_op jit(solution)/shard_map/ppermute | solution.py:782
  196.5 11.0 %shard_map.283 = (bf16[2048,1728]{1,0:T(8,128)(2,1)}, bf16[2048,1728]{1,0:T(8,128)(2,1)}, bf16[2048,1728]{1,0:T(8,128)(2,1)}, bf16[1152,1728]{1,0:T(8,128)(2,1)}, bf16[1152,1728]{1,0:T(8,128)(2,1)}) custom-call(s32[1]{0:T(128)} %bitcast.29.meta_ref, bf16[512,1152]{1,0:T(8,128)(2,1)} %copy-done.2, bf16[4,144,1728]{2,1,0:T(8,128)(2,1)} %bitcast.145, ...), custom_call_target="tpu_custom_call" | custom-call | flops 326149088 | bytes 583925 | tf_op jit(solution)/shard_map/pallas_call | solution.py:84
  212.0 16.1 %shard_map.284 = (bf16[2048,1728]{1,0:T(8,128)(2,1)}, bf16[2048,1728]{1,0:T(8,128)(2,1)}, bf16[2048,1728]{1,0:T(8,128)(2,1)}) custom-call(s32[1]{0:T(128)} %bitcast.29.meta_ref, bf16[512,1152]{1,0:T(8,128)(2,1)} %collective-permute-done.18.refs_0_.refs_2_, bf16[512,1152]{1,0:T(8,128)(2,1)} %copy-done.3, ...), custom_call_target="tpu_custom_call", output_to_operand_aliasing={{0}: (5, {}), {1}: (6, {}), {2}: (7, {})} | custom-call | flops 326149088 | bytes 424673 | tf_op jit(solution)/shard_map/pallas_call | solution.py:84
  228.1 13.0 %shard_map.285 = (bf16[512,1152]{1,0:T(8,128)(2,1)}, bf16[512,1152]{1,0:T(8,128)(2,1)}, bf16[512,1152]{1,0:T(8,128)(2,1)}) custom-call(bf16[2048,1728]{1,0:T(8,128)(2,1)} %get-tuple-element.137.x_ref.refs_0_, bf16[1728,1152]{1,0:T(8,128)(2,1)} %all-gather.8.cloned.1.call-done.w_ref.down_ref.refs_4_), custom_call_target="tpu_custom_call" | custom-call | flops 122305904 | bytes 70778 | tf_op jit(solution)/shard_map/pallas_call | solution.py:84
  246.1 13.8 %shard_map.286 = (bf16[2048,1728]{1,0:T(8,128)(2,1)}, bf16[2048,1728]{1,0:T(8,128)(2,1)}, bf16[2048,1728]{1,0:T(8,128)(2,1)}, bf16[512,1152]{1,0:T(8,128)(2,1)}) custom-call(bf16[512,1152]{1,0:T(8,128)(2,1)} %get-tuple-element.166.x_ref.refs_0_, ...), custom_call_target="tpu_custom_call", output_to_operand_aliasing={{0}: (4, {}), {1}: (5, {}), {2}: (6, {})} | custom-call | flops 122305904 | bytes 448266 | tf_op jit(solution)/shard_map/pallas_call | solution.py:84
  259.8 13.5 %collective-permute-done.25.refs_2_ = bf16[512,1152]{1,0:T(8,128)(2,1)} collective-permute-done((bf16[512,1152]{1,0:T(8,128)(2,1)S(1)}, bf16[512,1152]{1,0:T(8,128)(2,1)}, u32[]{:S(2)}, u32[]{:S(2)}) %collective-permute-start.25) | collective-permute-done | bytes 1179680 | tf_op jit(solution)/shard_map/ppermute | solution.py:749
  273.3 5.9 shard_map.287
  284.2 26.4 %shard_map.288 = (bf16[1024,1728]{1,0:T(8,128)(2,1)}, bf16[1024,1728]{1,0:T(8,128)(2,1)}, bf16[512,1152]{1,0:T(8,128)(2,1)}, bf16[512,1152]{1,0:T(8,128)(2,1)}) custom-call(bf16[512,1152]{1,0:T(8,128)(2,1)} %get-tuple-element.148.refs_0_.refs_1_, bf16[512,1152]{1,0:T(8,128)(2,1)} %copy-done.6, bf16[2048,1728]{1,0:T(8,128)(2,1)} %get-tuple-element.149.refs_2_, ...), custom_call_target="tpu_custom_call" | custom-call | flops 244611808 | bytes 188743 | tf_op jit(solution)/shard_map/pallas_call | solution.py:84
  314.6 16.0 %shard_map.289 = (bf16[4,216,1152]{2,1,0:T(8,128)(2,1)}, bf16[4,216,1152]{2,1,0:T(8,128)(2,1)}) custom-call(s32[1]{0:T(128)} %bitcast.29.meta_ref, bf16[2048,1728]{1,0:T(8,128)(2,1)} %get-tuple-element.152.refs_0_, bf16[512,1152]{1,0:T(8,128)(2,1)} %get-tuple-element.148.refs_0_.refs_1_, bf16[512,1152]{1,0:T(8,128)(2,1)} %copy-done.6, ...), custom_call_target="tpu_custom_call" | custom-call | flops 163074544 | bytes 79626 | tf_op jit(solution)/shard_map/pallas_call | solution.py:84
  331.8 26.5 %shard_map.290 = (bf16[1024,1728]{1,0:T(8,128)(2,1)}, bf16[1024,1728]{1,0:T(8,128)(2,1)}, bf16[512,1152]{1,0:T(8,128)(2,1)}, bf16[512,1152]{1,0:T(8,128)(2,1)}) custom-call(bf16[512,1152]{1,0:T(8,128)(2,1)} %copy-done.5, bf16[512,1152]{1,0:T(8,128)(2,1)} %copy-done.7, bf16[2048,1728]{1,0:T(8,128)(2,1)} %get-tuple-element.149.refs_2_, ...), custom_call_target="tpu_custom_call" | custom-call | flops 244611808 | bytes 188743 | tf_op jit(solution)/shard_map/pallas_call | solution.py:84
  359.1 3.4 collective-permute-done.29.refs_1_
  363.5 3.7 shard_map.291
  367.2 15.3 %shard_map.292 = (bf16[4,144,1728]{2,1,0:T(8,128)(2,1)}, bf16[4,144,1728]{2,1,0:T(8,128)(2,1)}) custom-call(s32[1]{0:T(128)} %bitcast.29.meta_ref, bf16[512,1152]{1,0:T(8,128)(2,1)} %get-tuple-element.166.x_ref.refs_0_, bf16[512,1152]{1,0:T(8,128)(2,1)} %copy-done.2, bf16[512,1152]{1,0:T(8,128)(2,1)} %collective-permute-done.18.refs_0_.refs_2_, ...), custom_call_target="tpu_custom_call" | custom-call | flops 163074544 | bytes 79626 | tf_op jit(solution)/shard_map/pallas_call | solution.py:84
  382.6 4.2 shard_map.293
  388.1 15.7 %shard_map.294 = (bf16[4,144,1728]{2,1,0:T(8,128)(2,1)}, bf16[4,144,1728]{2,1,0:T(8,128)(2,1)}) custom-call(s32[1]{0:T(128)} %bitcast.29.meta_ref, bf16[512,1152]{1,0:T(8,128)(2,1)} %get-tuple-element.166.x_ref.refs_0_, bf16[512,1152]{1,0:T(8,128)(2,1)} %copy-done.2, bf16[512,1152]{1,0:T(8,128)(2,1)} %collective-permute-done.18.refs_0_.refs_2_, ...), custom_call_target="tpu_custom_call" | custom-call | flops 163074544 | bytes 79626 | tf_op jit(solution)/shard_map/pallas_call | solution.py:84
  403.8 11.5 %collective-permute-done.32.c_ref = bf16[512,1152]{1,0:T(8,128)(2,1)} collective-permute-done((bf16[512,1152]{1,0:T(8,128)(2,1)S(1)}, bf16[512,1152]{1,0:T(8,128)(2,1)}, u32[]{:S(2)}, u32[]{:S(2)}) %collective-permute-start.32) | collective-permute-done | bytes 1179680 | tf_op jit(solution)/shard_map/ppermute | solution.py:749
  415.4 9.9 %shard_map.295 = (f32[512,1152]{1,0:T(8,128)}, bf16[512,1152]{1,0:T(8,128)(2,1)}, bf16[512,256]{1,0:T(8,128)(2,1)}, bf16[512,256]{1,0:T(8,128)(2,1)}, bf16[512,2...) custom-call(s32[1]{0:T(128)} %bitcast.me_ref, bf16[512,1152]{1,0:T(8,128)(2,1)} %get-tuple-element.170.a_ref, ...), custom_call_target="tpu_custom_call" | custom-call | flops 24159192 | bytes 91842 | tf_op jit(solution)/shard_map/pallas_call | solution.py:84
  428.3 6.4 %collective-permute-done.34.refs_2_ = bf16[512,256]{1,0:T(8,128)(2,1)S(1)} collective-permute-done((bf16[512,256]{1,0:T(8,128)(2,1)}, bf16[512,256]{1,0:T(8,128)(2,1)S(1)}, u32[]{:S(2)}, u32[]{:S(2)}) %collective-permute-start.34) | collective-permute-done | bytes 262176 | tf_op jit(solution)/shard_map/ppermute | solution.py:749
  434.6 5.8 collective-permute-done.35.refs_3_
  440.4 4.4 shard_map.296
  445.3 19.0 %shard_map.297 = (f32[2048,256]{1,0:T(8,128)}, f32[2048,256]{1,0:T(8,128)}, bf16[2048,256]{1,0:T(8,128)(2,1)}) custom-call(s32[9]{0:T(128)} %stack.140.meta_ref, bf16[2048,256]{1,0:T(8,128)(2,1)} %get-tuple-element.115.q_ref, bf16[2048,256]{1,0:T(8,128)(2,1)} %get-tuple-element.116.mine_ref, bf16[2048,256]{1,0:T(8,128)(2,1)} %copy-done.10, ...), custom_call_target="tpu_custom_call" | custom-call | flops 171798688 | bytes 104857 | tf_op jit(solution)/shard_map/pallas_call | solution.py:84
  467.6 11.7 %shard_map.298 = (bf16[2048,512]{1,0:T(8,128)(2,1)}, f32[1,256]{1,0:T(1,128)}, f32[1,256]{1,0:T(1,128)}, bf16[512,1152]{1,0:T(8,128)(2,1)}, bf16[512,1152]{1,0:T...) custom-call(s32[1]{0:T(128)} %bitcast.1.core_ref, f32[2048,256]{1,0:T(8,128)} %get-tuple-element.180.refs_0_, ...), custom_call_target="tpu_custom_call" | custom-call | flops 48318384 | bytes 136355 | tf_op jit(solution)/shard_map/pallas_call | solution.py:84
  479.2 12.3 %collective-permute-done.41.refs_1_ = bf16[4,144,1728]{2,1,0:T(8,128)(2,1)S(1)} collective-permute-done((bf16[4,144,1728]{2,1,0:T(8,128)(2,1)}, bf16[4,144,1728]{2,1,0:T(8,128)(2,1)S(1)}, u32[]{:S(2)}, u32[]{:S(2)}) %collective-permute-start.41) | collective-permute-done | bytes 1990688 | tf_op jit(solution)/shard_map/ppermute | solution.py:782
  492.8 4.3 shard_map.300
  497.1 3.1 convolution_convert_fusion
  508.4 6.7 %shard_map.301 = (bf16[4,144,512]{2,1,0:T(8,128)(2,1)}, bf16[4,144,512]{2,1,0:T(8,128)(2,1)}) custom-call(s32[1]{0:T(128)} %bitcast.29.meta_ref, bf16[2048,1152]{1,0:T(8,128)(2,1)} %get-tuple-element.200.refs_0_, bf16[2048,512]{1,0:T(8,128)(2,1)} %get-tuple-element.197.refs_1_), custom_call_target="tpu_custom_call" | custom-call | flops 48318384 | bytes 23592 | tf_op jit(solution)/shard_map/pallas_call | solution.py:84
  519.5 14.4 %collective-permute-done.56 = bf16[216,1152]{1,0:T(8,128)(2,1)} collective-permute-done((bf16[216,1152]{1,0:T(8,128)(2,1)}, bf16[216,1152]{1,0:T(8,128)(2,1)}, u32[]{:S(2)}, u32[]{:S(2)}) %collective-permute-start.56) | collective-permute-done | bytes 497696 | tf_op jit(solution)/shard_map/ppermute | solution.py:749
  542.1 8.7 %collective-permute-done.53.refs_2_ = bf16[144,1728]{1,0:T(8,128)(2,1)} collective-permute-done((bf16[144,1728]{1,0:T(8,128)(2,1)}, bf16[144,1728]{1,0:T(8,128)(2,1)}, u32[]{:S(2)}, u32[]{:S(2)}) %collective-permute-start.53) | collective-permute-done | bytes 497696 | tf_op jit(solution)/shard_map/ppermute | solution.py:749
  554.6 8.1 %collective-permute-done.45.refs_1_ = bf16[4,208,640]{2,1,0:T(8,128)(2,1)} collective-permute-done((bf16[4,208,640]{2,1,0:T(8,128)(2,1)}, bf16[4,208,640]{2,1,0:T(8,128)(2,1)}, u32[]{:S(2)}, u32[]{:S(2)}) %collective-permute-start.45) | collective-permute-done | bytes 1064992 | tf_op jit(solution)/shard_map/ppermute | solution.py:782
  562.7 3.6 shard_map.302
  572.8 6.0 shard_map.304
  578.8 5.6 shard_map.299
  595.7 5.5 shard_map.303
  602.7 6.1 collective-permute-done.59
  (322 shorter events, 134.5 us)
Async XLA Ops:
  7.2 95.9 %all-gather.4.cloned.1.call-start = ((), (), s32[]{:S(2)}) async-start(), calls=%async_computation.3 | async-start | bytes 2580480 | tf_op jit(solution)/shard_map/all_gather | solution.py:790
  13.0 28.3 %collective-permute-start.1 = (bf16[512,1152]{1,0:T(8,128)(2,1)}, bf16[512,1152]{1,0:T(8,128)(2,1)S(1)}, u32[]{:S(2)}, u32[]{:S(2)}) collective-permute-start(bf16[512,1152]{1,0:T(8,128)(2,1)} %refs_3_.1), channel_id=1, source_target_pairs={{0,2},{1,3},{2,0},{3,1},{4,6},{5,7},{6,4},{7,5},{8,10},{9,11},{10,... | collective-permute-start | bytes 3538952 | tf_op jit(solution)/shard_map/ppermute | solution.py:749
  15.6 21.9 %collective-permute-start.3 = (bf16[208,640]{1,0:T(8,128)(2,1)S(1)}, bf16[208,640]{1,0:T(8,128)(2,1)S(1)}, u32[]{:S(2)}, u32[]{:S(2)}) collective-permute-start(bf16[208,640]{1,0:T(8,128)(2,1)S(1)} %fusion.9.refs_4_), channel_id=1, source_target_pairs={{0,16},{4,20},{8,24},{12,28},{16,0},{20,4},{24,8},{28,12},{1,17},{... | collective-permute-start | bytes 798728 | tf_op jit(solution)/shard_map/ppermute | solution.py:785
  16.6 24.0 %collective-permute-start.4 = (bf16[208,640]{1,0:T(8,128)(2,1)S(1)}, bf16[208,640]{1,0:T(8,128)(2,1)S(1)}, u32[]{:S(2)}, u32[]{:S(2)}) collective-permute-start(bf16[208,640]{1,0:T(8,128)(2,1)S(1)} %fusion.9.refs_4_), channel_id=1, source_target_pairs={{0,24},{4,28},{8,0},{12,4},{16,8},{20,12},{24,16},{28,20},{1,25},{... | collective-permute-start | bytes 798728 | tf_op jit(solution)/shard_map/ppermute | solution.py:785
  44.7 90.2 %all-gather.6.cloned.1.call-start = ((), (), s32[]{:S(2)}) async-start(), calls=%async_computation.4 | async-start | bytes 2580480 | tf_op jit(solution)/shard_map/all_gather | solution.py:790
  47.8 180.3 %all-gather.8.cloned.1.call-start = ((), (), s32[]{:S(2)}) async-start(), calls=%async_computation.5 | async-start | bytes 4976640 | tf_op jit(solution)/shard_map/all_gather | solution.py:790
  49.9 12.7 %collective-permute-start.22 = (bf16[216,1152]{1,0:T(8,128)(2,1)}, bf16[216,1152]{1,0:T(8,128)(2,1)}, u32[]{:S(2)}, u32[]{:S(2)}) collective-permute-start(bf16[216,1152]{1,0:T(8,128)(2,1)} %dynamic-slice_convert_fusion), channel_id=1, source_target_pairs={{0,4},{4,0},{8,12},{12,8},{16,20},{20,16},{24,28},{28,24},{1,5},{5... | collective-permute-start | bytes 1493000 | tf_op jit(solution)/shard_map/ppermute | solution.py:782
  51.1 38.0 %collective-permute-start = (bf16[512,1152]{1,0:T(8,128)(2,1)S(1)}, bf16[512,1152]{1,0:T(8,128)(2,1)}, u32[]{:S(2)}, u32[]{:S(2)}) collective-permute-start(bf16[512,1152]{1,0:T(8,128)(2,1)S(1)} %copy-done.4), channel_id=1, source_target_pairs={{0,1},{1,0},{2,3},{3,2},{4,5},{5,4},{6,7},{7,6},{8,9},{9,8},{10,11... | collective-permute-start | bytes 3538952 | tf_op jit(solution)/shard_map/ppermute | solution.py:749
  51.9 37.3 %collective-permute-start.5 = (bf16[512,1152]{1,0:T(8,128)(2,1)S(1)}, bf16[512,1152]{1,0:T(8,128)(2,1)}, u32[]{:S(2)}, u32[]{:S(2)}) collective-permute-start(bf16[512,1152]{1,0:T(8,128)(2,1)S(1)} %collective-permute-done.1.refs_2_), channel_id=1, source_target_pairs={{0,1},{1,0},{2,3},{3,2},{4,5},{5,4},{6,7},{7,6},{8,9},{9,8},{10,11... | collective-permute-start | bytes 3538952 | tf_op jit(solution)/shard_map/ppermute | solution.py:749
  65.3 399.7 %reduce-scatter.10.cloned.1.call-start = ((), (), s32[]{:S(2)}) async-start(), calls=%async_computation.8 | async-start | bytes 2488320
  67.4 11.5 %collective-permute-start.7 = (bf16[208,640]{1,0:T(8,128)(2,1)S(1)}, bf16[208,640]{1,0:T(8,128)(2,1)S(1)}, u32[]{:S(2)}, u32[]{:S(2)}) collective-permute-start(bf16[208,640]{1,0:T(8,128)(2,1)S(1)} %copy-done.32), channel_id=1, source_target_pairs={{0,4},{4,0},{8,12},{12,8},{16,20},{20,16},{24,28},{28,24},{1,5},{5... | collective-permute-start | bytes 798728 | tf_op jit(solution)/shard_map/ppermute | solution.py:782
  67.7 15.8 %collective-permute-start.8 = (bf16[208,640]{1,0:T(8,128)(2,1)S(1)}, bf16[208,640]{1,0:T(8,128)(2,1)S(1)}, u32[]{:S(2)}, u32[]{:S(2)}) collective-permute-start(bf16[208,640]{1,0:T(8,128)(2,1)S(1)} %copy-done.34), channel_id=1, source_target_pairs={{0,4},{4,0},{8,12},{12,8},{16,20},{20,16},{24,28},{28,24},{1,5},{5... | collective-permute-start | bytes 798728 | tf_op jit(solution)/shard_map/ppermute | solution.py:782
  72.1 17.1 %collective-permute-start.9 = (bf16[208,640]{1,0:T(8,128)(2,1)}, bf16[208,640]{1,0:T(8,128)(2,1)S(1)}, u32[]{:S(2)}, u32[]{:S(2)}) collective-permute-start(bf16[208,640]{1,0:T(8,128)(2,1)} %copy-done.35), channel_id=1, source_target_pairs={{0,4},{4,0},{8,12},{12,8},{16,20},{20,16},{24,28},{28,24},{1,5},{5... | collective-permute-start | bytes 798728 | tf_op jit(solution)/shard_map/ppermute | solution.py:782
  103.1 46.8 %collective-permute-start.11 = (bf16[4,144,1728]{2,1,0:T(8,128)(2,1)}, bf16[4,144,1728]{2,1,0:T(8,128)(2,1)}, u32[]{:S(2)}, u32[]{:S(2)}) collective-permute-start(bf16[4,144,1728]{2,1,0:T(8,128)(2,1)} %bitcast.144), channel_id=1, source_target_pairs={{0,4},{4,0},{8,12},{12,8},{16,20},{20,16},{24,28},{28,24},{1,5},{5... | collective-permute-start | bytes 5971976 | tf_op jit(solution)/shard_map/ppermute | solution.py:782
  126.0 14.7 %collective-permute-start.16 = (bf16[256,1152]{1,0:T(8,128)(2,1)S(1)}, bf16[256,1152]{1,0:T(8,128)(2,1)S(1)}, u32[]{:S(2)}, u32[]{:S(2)}) collective-permute-start(bf16[256,1152]{1,0:T(8,128)(2,1)S(1)} %copy-done.22), channel_id=1, source_target_pairs={{0,2},{1,3},{2,0},{3,1},{4,6},{5,7},{6,4},{7,5},{8,10},{9,11},{10,... | collective-permute-start | bytes 1769480 | tf_op jit(solution)/shard_map/ppermute | solution.py:749
  134.8 59.3 %collective-permute-start.20 = (bf16[4,144,1728]{2,1,0:T(8,128)(2,1)}, bf16[4,144,1728]{2,1,0:T(8,128)(2,1)S(1)}, u32[]{:S(2)}, u32[]{:S(2)}) collective-permute-start(bf16[4,144,1728]{2,1,0:T(8,128)(2,1)} %bitcast.146), channel_id=1, source_target_pairs={{0,4},{4,0},{8,12},{12,8},{16,20},{20,16},{24,28},{28,24},{1,5},{5... | collective-permute-start | bytes 5971976 | tf_op jit(solution)/shard_map/ppermute | solution.py:782
  136.0 22.5 %collective-permute-start.15 = (bf16[256,1152]{1,0:T(8,128)(2,1)S(1)}, bf16[256,1152]{1,0:T(8,128)(2,1)S(1)}, u32[]{:S(2)}, u32[]{:S(2)}) collective-permute-start(bf16[256,1152]{1,0:T(8,128)(2,1)S(1)} %copy-done.22), channel_id=1, source_target_pairs={{0,1},{1,0},{2,3},{3,2},{4,5},{5,4},{6,7},{7,6},{8,9},{9,8},{10,11... | collective-permute-start | bytes 1769480 | tf_op jit(solution)/shard_map/ppermute | solution.py:749
  140.7 17.8 %collective-permute-start.17 = (bf16[256,1152]{1,0:T(8,128)(2,1)S(1)}, bf16[256,1152]{1,0:T(8,128)(2,1)S(1)}, u32[]{:S(2)}, u32[]{:S(2)}) collective-permute-start(bf16[256,1152]{1,0:T(8,128)(2,1)S(1)} %collective-permute-done.16.refs_6_), channel_id=1, source_target_pairs={{0,1},{1,0},{2,3},{3,2},{4,5},{5,4},{6,7},{7,6},{8,9},{9,8},{10,11... | collective-permute-start | bytes 1769480 | tf_op jit(solution)/shard_map/ppermute | solution.py:749
  149.9 8.6 %collective-permute-start.14 = (bf16[512,256]{1,0:T(8,128)(2,1)}, bf16[512,256]{1,0:T(8,128)(2,1)S(1)}, u32[]{:S(2)}, u32[]{:S(2)}) collective-permute-start(bf16[512,256]{1,0:T(8,128)(2,1)} %get-tuple-element.123), channel_id=1, source_target_pairs={{0,3},{1,2},{2,1},{3,0},{4,7},{5,6},{6,5},{7,4},{8,11},{9,10},{10,... | collective-permute-start | bytes 786440 | tf_op jit(solution)/shard_map/ppermute | solution.py:749
  166.6 27.6 %collective-permute-start.19 = (bf16[512,1152]{1,0:T(8,128)(2,1)}, bf16[512,1152]{1,0:T(8,128)(2,1)S(1)}, u32[]{:S(2)}, u32[]{:S(2)}) collective-permute-start(bf16[512,1152]{1,0:T(8,128)(2,1)} %get-tuple-element.166.x_ref.refs_0_), channel_id=1, source_target_pairs={{0,1},{1,0},{2,3},{3,2},{4,5},{5,4},{6,7},{7,6},{8,9},{9,8},{10,11... | collective-permute-start | bytes 3538952 | tf_op jit(solution)/shard_map/ppermute | solution.py:749
  167.5 40.0 %collective-permute-start.18 = (bf16[512,1152]{1,0:T(8,128)(2,1)}, bf16[512,1152]{1,0:T(8,128)(2,1)}, u32[]{:S(2)}, u32[]{:S(2)}) collective-permute-start(bf16[512,1152]{1,0:T(8,128)(2,1)} %get-tuple-element.166.x_ref.refs_0_), channel_id=1, source_target_pairs={{0,2},{1,3},{2,0},{3,1},{4,6},{5,7},{6,4},{7,5},{8,10},{9,11},{10,... | collective-permute-start | bytes 3538952 | tf_op jit(solution)/shard_map/ppermute | solution.py:749
  246.0 27.4 %collective-permute-start.25 = (bf16[512,1152]{1,0:T(8,128)(2,1)S(1)}, bf16[512,1152]{1,0:T(8,128)(2,1)}, u32[]{:S(2)}, u32[]{:S(2)}) collective-permute-start(bf16[512,1152]{1,0:T(8,128)(2,1)S(1)} %add_convert_fusion.1), channel_id=1, source_target_pairs={{0,2},{1,3},{2,0},{3,1},{4,6},{5,7},{6,4},{7,5},{8,10},{9,11},{10,... | collective-permute-start | bytes 3538952 | tf_op jit(solution)/shard_map/ppermute | solution.py:749
  280.4 30.1 %collective-permute-start.27 = (bf16[512,1152]{1,0:T(8,128)(2,1)}, bf16[512,1152]{1,0:T(8,128)(2,1)S(1)}, u32[]{:S(2)}, u32[]{:S(2)}) collective-permute-start(bf16[512,1152]{1,0:T(8,128)(2,1)} %get-tuple-element.148.refs_0_.refs_1_), channel_id=1, source_target_pairs={{0,2},{1,3},{2,0},{3,1},{4,6},{5,7},{6,4},{7,5},{8,10},{9,11},{10,... | collective-permute-start | bytes 3538952 | tf_op jit(solution)/shard_map/ppermute | solution.py:749
  330.6 52.0 %collective-permute-start.31 = (bf16[4,216,1152]{2,1,0:T(8,128)(2,1)}, bf16[4,216,1152]{2,1,0:T(8,128)(2,1)}, u32[]{:S(2)}, u32[]{:S(2)}) collective-permute-start(bf16[4,216,1152]{2,1,0:T(8,128)(2,1)} %get-tuple-element.155), channel_id=1, source_target_pairs={{0,4},{4,0},{8,12},{12,8},{16,20},{20,16},{24,28},{28,24},{1,5},{5... | collective-permute-start | bytes 5971976 | tf_op jit(solution)/shard_map/ppermute | solution.py:782
  359.0 8.2 %collective-permute-start.30 = (bf16[512,1152]{1,0:T(8,128)(2,1)S(1)}, bf16[512,1152]{1,0:T(8,128)(2,1)}, u32[]{:S(2)}, u32[]{:S(2)}) collective-permute-start(bf16[512,1152]{1,0:T(8,128)(2,1)S(1)} %copy-done.50), channel_id=1, source_target_pairs={{0,1},{1,0},{2,3},{3,2},{4,5},{5,4},{6,7},{7,6},{8,9},{9,8},{10,11... | collective-permute-start | bytes 3538952 | tf_op jit(solution)/shard_map/ppermute | solution.py:749
  386.8 150.3 %reduce-scatter.6.cloned.1.call-start = ((), (), s32[]{:S(2)}) async-start(), calls=%async_computation.6 | async-start | bytes 2580480 | tf_op jit(solution)/shard_map/reduce_scatter | solution.py:835
  386.9 53.5 %collective-permute-start.36 = (bf16[4,144,1728]{2,1,0:T(8,128)(2,1)}, bf16[4,144,1728]{2,1,0:T(8,128)(2,1)}, u32[]{:S(2)}, u32[]{:S(2)}) collective-permute-start(bf16[4,144,1728]{2,1,0:T(8,128)(2,1)} %get-tuple-element.164), channel_id=1, source_target_pairs={{0,4},{4,0},{8,12},{12,8},{16,20},{20,16},{24,28},{28,24},{1,5},{5... | collective-permute-start | bytes 5971976 | tf_op jit(solution)/shard_map/ppermute | solution.py:782
  388.1 27.3 %collective-permute-start.32 = (bf16[512,1152]{1,0:T(8,128)(2,1)S(1)}, bf16[512,1152]{1,0:T(8,128)(2,1)}, u32[]{:S(2)}, u32[]{:S(2)}) collective-permute-start(bf16[512,1152]{1,0:T(8,128)(2,1)S(1)} %copy-done.18), channel_id=1, source_target_pairs={{0,2},{1,3},{2,0},{3,1},{4,6},{5,7},{6,4},{7,5},{8,10},{9,11},{10,... | collective-permute-start | bytes 3538952 | tf_op jit(solution)/shard_map/ppermute | solution.py:749
  426.5 13.9 %collective-permute-start.35 = (bf16[512,256]{1,0:T(8,128)(2,1)}, bf16[512,256]{1,0:T(8,128)(2,1)S(1)}, u32[]{:S(2)}, u32[]{:S(2)}) collective-permute-start(bf16[512,256]{1,0:T(8,128)(2,1)} %get-tuple-element.177), channel_id=1, source_target_pairs={{0,3},{1,2},{2,1},{3,0},{4,7},{5,6},{6,5},{7,4},{8,11},{9,10},{10,... | collective-permute-start | bytes 786440 | tf_op jit(solution)/shard_map/ppermute | solution.py:749
  444.9 121.4 %reduce-scatter.8.cloned.1.call-start = ((), (), s32[]{:S(2)}) async-start(), calls=%async_computation.7 | async-start | bytes 2580480 | tf_op jit(solution)/shard_map/reduce_scatter | solution.py:835
  444.9 46.6 %collective-permute-start.41 = (bf16[4,144,1728]{2,1,0:T(8,128)(2,1)}, bf16[4,144,1728]{2,1,0:T(8,128)(2,1)S(1)}, u32[]{:S(2)}, u32[]{:S(2)}) collective-permute-start(bf16[4,144,1728]{2,1,0:T(8,128)(2,1)} %get-tuple-element.169), channel_id=1, source_target_pairs={{0,4},{4,0},{8,12},{12,8},{16,20},{20,16},{24,28},{28,24},{1,5},{5... | collective-permute-start | bytes 5971976 | tf_op jit(solution)/shard_map/ppermute | solution.py:782
  508.4 26.7 %collective-permute-start.44 = (bf16[8,32,1152]{2,1,0:T(8,128)(2,1)}, bf16[8,32,1152]{2,1,0:T(8,128)(2,1)S(1)}, u32[]{:S(2)}, u32[]{:S(2)}) collective-permute-start(bf16[8,32,1152]{2,1,0:T(8,128)(2,1)} %get-tuple-element.234), channel_id=1, source_target_pairs={{0,2},{1,3},{2,0},{3,1},{4,6},{5,7},{6,4},{7,5},{8,10},{9,11},{10,... | collective-permute-start | bytes 1769480 | tf_op jit(solution)/shard_map/ppermute | solution.py:749
  515.1 18.8 %collective-permute-start.56 = (bf16[216,1152]{1,0:T(8,128)(2,1)}, bf16[216,1152]{1,0:T(8,128)(2,1)}, u32[]{:S(2)}, u32[]{:S(2)}) collective-permute-start(bf16[216,1152]{1,0:T(8,128)(2,1)} %reduce-scatter.10.cloned.1.call-done), channel_id=1, source_target_pairs={{0,2},{1,3},{2,0},{3,1},{4,6},{5,7},{6,4},{7,5},{8,10},{9,11},{10,... | collective-permute-start | bytes 1493000 | tf_op jit(solution)/shard_map/ppermute | solution.py:749
  516.9 20.5 %collective-permute-start.39 = (bf16[512,1152]{1,0:T(8,128)(2,1)}, bf16[512,1152]{1,0:T(8,128)(2,1)S(1)}, u32[]{:S(2)}, u32[]{:S(2)}) collective-permute-start(bf16[512,1152]{1,0:T(8,128)(2,1)} %get-tuple-element.191), channel_id=1, source_target_pairs={{0,1},{1,0},{2,3},{3,2},{4,5},{5,4},{6,7},{7,6},{8,9},{9,8},{10,11... | collective-permute-start | bytes 3538952 | tf_op jit(solution)/shard_map/ppermute | solution.py:749
  518.2 50.0 %collective-permute-start.38 = (bf16[512,1152]{1,0:T(8,128)(2,1)}, bf16[512,1152]{1,0:T(8,128)(2,1)}, u32[]{:S(2)}, u32[]{:S(2)}) collective-permute-start(bf16[512,1152]{1,0:T(8,128)(2,1)} %get-tuple-element.189), channel_id=1, source_target_pairs={{0,1},{1,0},{2,3},{3,2},{4,5},{5,4},{6,7},{7,6},{8,9},{9,8},{10,11... | collective-permute-start | bytes 3538952 | tf_op jit(solution)/shard_map/ppermute | solution.py:749
  519.0 19.7 %collective-permute-start.55 = (bf16[216,1152]{1,0:T(8,128)(2,1)}, bf16[216,1152]{1,0:T(8,128)(2,1)}, u32[]{:S(2)}, u32[]{:S(2)}) collective-permute-start(bf16[216,1152]{1,0:T(8,128)(2,1)} %reduce-scatter.10.cloned.1.call-done), channel_id=1, source_target_pairs={{0,1},{1,0},{2,3},{3,2},{4,5},{5,4},{6,7},{7,6},{8,9},{9,8},{10,11... | collective-permute-start | bytes 1493000 | tf_op jit(solution)/shard_map/ppermute | solution.py:749
  537.1 25.5 %collective-permute-start.45 = (bf16[4,208,640]{2,1,0:T(8,128)(2,1)}, bf16[4,208,640]{2,1,0:T(8,128)(2,1)}, u32[]{:S(2)}, u32[]{:S(2)}) collective-permute-start(bf16[4,208,640]{2,1,0:T(8,128)(2,1)} %fusion.5), channel_id=1, source_target_pairs={{0,4},{4,0},{8,12},{12,8},{16,20},{20,16},{24,28},{28,24},{1,5},{5... | collective-permute-start | bytes 3194888 | tf_op jit(solution)/shard_map/ppermute | solution.py:782
  537.4 13.4 %collective-permute-start.53 = (bf16[144,1728]{1,0:T(8,128)(2,1)}, bf16[144,1728]{1,0:T(8,128)(2,1)}, u32[]{:S(2)}, u32[]{:S(2)}) collective-permute-start(bf16[144,1728]{1,0:T(8,128)(2,1)} %reduce-scatter.6.cloned.1.call-done.refs_0_), channel_id=1, source_target_pairs={{0,2},{1,3},{2,0},{3,1},{4,6},{5,7},{6,4},{7,5},{8,10},{9,11},{10,... | collective-permute-start | bytes 1493000 | tf_op jit(solution)/shard_map/ppermute | solution.py:749
  538.7 40.1 %collective-permute-start.40 = (bf16[512,1152]{1,0:T(8,128)(2,1)}, bf16[512,1152]{1,0:T(8,128)(2,1)}, u32[]{:S(2)}, u32[]{:S(2)}) collective-permute-start(bf16[512,1152]{1,0:T(8,128)(2,1)} %add_convert_fusion), channel_id=1, source_target_pairs={{0,2},{1,3},{2,0},{3,1},{4,6},{5,7},{6,4},{7,5},{8,10},{9,11},{10,... | collective-permute-start | bytes 3538952 | tf_op jit(solution)/shard_map/ppermute | solution.py:749
  541.3 26.9 %collective-permute-start.52 = (bf16[144,1728]{1,0:T(8,128)(2,1)S(1)}, bf16[144,1728]{1,0:T(8,128)(2,1)S(1)}, u32[]{:S(2)}, u32[]{:S(2)}) collective-permute-start(bf16[144,1728]{1,0:T(8,128)(2,1)S(1)} %copy-done.11), channel_id=1, source_target_pairs={{0,1},{1,0},{2,3},{3,2},{4,5},{5,4},{6,7},{7,6},{8,9},{9,8},{10,11... | collective-permute-start | bytes 1493000 | tf_op jit(solution)/shard_map/ppermute | solution.py:749
  550.8 18.4 %collective-permute-start.54 = (bf16[144,1728]{1,0:T(8,128)(2,1)}, bf16[144,1728]{1,0:T(8,128)(2,1)}, u32[]{:S(2)}, u32[]{:S(2)}) collective-permute-start(bf16[144,1728]{1,0:T(8,128)(2,1)} %collective-permute-done.53.refs_2_), channel_id=1, source_target_pairs={{0,1},{1,0},{2,3},{3,2},{4,5},{5,4},{6,7},{7,6},{8,9},{9,8},{10,11... | collective-permute-start | bytes 1493000 | tf_op jit(solution)/shard_map/ppermute | solution.py:749
  566.3 20.8 %collective-permute-start.50 = (bf16[144,1728]{1,0:T(8,128)(2,1)}, bf16[144,1728]{1,0:T(8,128)(2,1)}, u32[]{:S(2)}, u32[]{:S(2)}) collective-permute-start(bf16[144,1728]{1,0:T(8,128)(2,1)} %reduce-scatter.8.cloned.1.call-done.refs_0_), channel_id=1, source_target_pairs={{0,2},{1,3},{2,0},{3,1},{4,6},{5,7},{6,4},{7,5},{8,10},{9,11},{10,... | collective-permute-start | bytes 1493000 | tf_op jit(solution)/shard_map/ppermute | solution.py:749
  568.2 20.0 %collective-permute-start.46 = (bf16[208,640]{1,0:T(8,128)(2,1)}, bf16[208,640]{1,0:T(8,128)(2,1)}, u32[]{:S(2)}, u32[]{:S(2)}) collective-permute-start(bf16[208,640]{1,0:T(8,128)(2,1)} %get-tuple-element.251), channel_id=1, source_target_pairs={{0,8},{4,12},{8,16},{12,20},{16,24},{20,28},{24,0},{28,4},{1,9},{5... | collective-permute-start | bytes 798728 | tf_op jit(solution)/shard_map/ppermute | solution.py:785
  568.2 22.0 %collective-permute-start.47 = (bf16[208,640]{1,0:T(8,128)(2,1)S(1)}, bf16[208,640]{1,0:T(8,128)(2,1)S(1)}, u32[]{:S(2)}, u32[]{:S(2)}) collective-permute-start(bf16[208,640]{1,0:T(8,128)(2,1)S(1)} %get-tuple-element.253), channel_id=1, source_target_pairs={{0,16},{4,20},{8,24},{12,28},{16,0},{20,4},{24,8},{28,12},{1,17},{... | collective-permute-start | bytes 798728 | tf_op jit(solution)/shard_map/ppermute | solution.py:785
  569.2 24.2 %collective-permute-start.48 = (bf16[208,640]{1,0:T(8,128)(2,1)S(1)}, bf16[208,640]{1,0:T(8,128)(2,1)}, u32[]{:S(2)}, u32[]{:S(2)}) collective-permute-start(bf16[208,640]{1,0:T(8,128)(2,1)S(1)} %get-tuple-element.252), channel_id=1, source_target_pairs={{0,24},{4,28},{8,0},{12,4},{16,8},{20,12},{24,16},{28,20},{1,25},{... | collective-permute-start | bytes 798728 | tf_op jit(solution)/shard_map/ppermute | solution.py:785
  584.4 11.3 %collective-permute-start.49 = (bf16[144,1728]{1,0:T(8,128)(2,1)S(1)}, bf16[144,1728]{1,0:T(8,128)(2,1)}, u32[]{:S(2)}, u32[]{:S(2)}) collective-permute-start(bf16[144,1728]{1,0:T(8,128)(2,1)S(1)} %copy-done.13), channel_id=1, source_target_pairs={{0,1},{1,0},{2,3},{3,2},{4,5},{5,4},{6,7},{7,6},{8,9},{9,8},{10,11... | collective-permute-start | bytes 1493000 | tf_op jit(solution)/shard_map/ppermute | solution.py:749
  587.1 8.6 %collective-permute-start.51 = (bf16[144,1728]{1,0:T(8,128)(2,1)}, bf16[144,1728]{1,0:T(8,128)(2,1)}, u32[]{:S(2)}, u32[]{:S(2)}) collective-permute-start(bf16[144,1728]{1,0:T(8,128)(2,1)} %collective-permute-done.50.refs_2_), channel_id=1, source_target_pairs={{0,1},{1,0},{2,3},{3,2},{4,5},{5,4},{6,7},{7,6},{8,9},{9,8},{10,11... | collective-permute-start | bytes 1493000 | tf_op jit(solution)/shard_map/ppermute | solution.py:749
  601.8 8.4 %collective-permute-start.58 = (bf16[208,640]{1,0:T(8,128)(2,1)S(1)}, bf16[208,640]{1,0:T(8,128)(2,1)S(1)}, u32[]{:S(2)}, u32[]{:S(2)}) collective-permute-start(bf16[208,640]{1,0:T(8,128)(2,1)S(1)} %get-tuple-element.267), channel_id=1, source_target_pairs={{0,1},{1,0},{2,3},{3,2},{4,5},{5,4},{6,7},{7,6},{8,9},{9,8},{10,11... | collective-permute-start | bytes 798728 | tf_op jit(solution)/shard_map/ppermute | solution.py:749
  (72 other events, 448.2 us)
Sparse Core Ops, SparseCore 0:
  44.8 44.3 all-gather.3
  90.8 43.9 all-gather.5
  137.0 75.1 all-gather.7
  387.0 38.6 reduce-scatter.9
  445.0 38.4 reduce-scatter.5
  502.6 38.8 reduce-scatter.7

commit v4 on v3

--- a/solution.py
+++ b/solution.py
@@ -810,9 +810,9 @@
         mine = after(self.gather_row(own), later).reshape(self.rows, size, width)
         return [mine, self.swap(mine)]
 
-    def gather_pair_first(self, own):
+    def gather_pair_first(self, own, later):
         size, width = own.shape
-        both = self.pair(own, self.swap(own), 0).reshape(2 * size, width)
+        both = self.pair(own, after(self.swap(own), later), 0).reshape(2 * size, width)
         return self.gather_row(both)
 
     def halves(self, whole):
@@ -952,7 +952,7 @@
     other_kv = swap_seq(mine_kv, 1)
     *heads, probs = attend(meta, queries, mine_kv, other_kv, code, low, high, scale, 256)
     up_parts = owners.gather_wide(up_own, probs)
-    w_down = owners.gather_pair_first(down_own)
+    w_down = owners.gather_pair_first(down_own, queries)
     heads = [heads[0]] + [swap_seq(heads[r], r) for r in range(1, SEQ)]
     self_index = jnp.stack([me]).astype(jnp.int32)
     if packed:
@@ -1054,7 +1054,6 @@
     normed_pair = pair_sum(normed_blocks[2], swap_seq(normed_blocks[3], 1))
     normed_two = swap_seq(normed_pair, 2)
     normed_one = swap_seq(normed_blocks[1], 1)
-    out_down = jnp.concatenate(natural(gather_seq(after(grad_down, away_proj)), me)).astype(f32)
 
     short = jnp.stack([gain_query_part[0], gain_key_part[0]], axis=1).reshape(fsdp, short_rows, 2)
     short = jnp.pad(short, ((0, 0), (0, rows - short_rows), (0, 0))).reshape(model, 2)
@@ -1074,6 +1073,8 @@
     away_small = pile(away_proj, away_gains, away_out)
     here_small = pile(here_proj, here_gains, here_out)
     come_small = owners.swap(after(away_small, grad_gate))
+    out_down = natural(gather_seq(after(grad_down, away_small)), me)
+    out_down = jnp.concatenate(out_down).astype(f32)
     half_small = owners.fold(here_small, come_small)
     grad_small = owners.scatter_direct(half_small)
 
@@ -1089,15 +1090,16 @@
         4,
     )
 
-    def spread(own):
+    def spread(own, *later):
         blocks = gather_seq(own)
+        if later:
+            blocks[0] = after(blocks[0], *later)
         if fsdp <= 8:
             return spread_columns(self_index, blocks, fsdp)
         stack = jnp.stack([b.reshape(rows, fsdp, part) for b in natural(blocks, me)], axis=2)
         return stack.reshape(rows, hidden).astype(f32)
 
     out_gate = spread(grad_gate)
-    out_up = spread(grad_up)
 
     feed_sum = jnp.sum(
         grad_gate.astype(f32) * gate_own.astype(f32)
@@ -1113,14 +1115,14 @@
         axis=1,
     )
     tail = jnp.pad(tail, ((0, 0), (0, 128 - tail.shape[1])))
-    small = gather_seq(
-        jnp.concatenate(
-            [
-                to_half(jnp.concatenate([upper[:, : 2 * head_width], tail], axis=1)),
-                to_half(after(grad_small, out_up, out_gate, out_down, grad_tokens)[rows:]),
-            ]
-        )
-    )
+    small = jnp.concatenate(
+        [
+            to_half(jnp.concatenate([upper[:, : 2 * head_width], tail], axis=1)),
+            to_half(after(grad_small, out_gate, out_down, grad_tokens)[rows:]),
+        ]
+    )
+    out_up = spread(grad_up, small)
+    small = gather_seq(small)
     lower = [b[rows:] for b in natural(small, me)]
     out_out = jnp.concatenate(
         [

time: 631 us -> 607 us (0.962)
  waiting for transfers between devices: 214 us -> 168 us
  starting transfers between devices: 47 us -> 66.3 us
    ppermute x11, waiting for transfers between devices: 77.2 us -> 29.8 us  [swap(): return lax.ppermute(values, 'fsdp', [(i, i ^ 1) for i in range(self.count)])]
    ppermute x44, starting transfers between devices: 30.6 us -> 46.4 us  [swap_seq(): return lax.ppermute(values, 'seq', [(i, i ^ bits) for i in range(SEQ)])]
    ppermute x44, waiting for transfers between devices: 101 us -> 91.9 us  [swap_seq(): return lax.ppermute(values, 'seq', [(i, i ^ bits) for i in range(SEQ)])]
    all_gather x3, waiting for transfers between devices: 8.76 us -> 17.8 us  [gather_row(): lax.all_gather(values, 'fsdp', axis=0, tiled=True, axis_index_groups=self...]
    unnamed x106 -> x108, local copies, waits for them, and re-layouts: 14.8 us -> 16 us
  transfers between devices with their start and end apart: 67 -> 67, of which waited for: 34 -> 32; matrix products, arithmetic and copies ran while one was open for 6% -> 8% of each run, Pallas kernels for 38% -> 39%
where the time goes in v4:
time: 607 us; the launch traced here: 600 us
  Pallas kernels  280 us (46%)
  waiting for transfers between devices  168 us (28%)
  starting transfers between devices  66.3 us (11%)
  other arithmetic  35.3 us (6%)
  local copies, waits for them, and re-layouts  32.9 us (5%)
  between operations  15.1 us (2%)
    pallas_call x25, Pallas kernels, call(): return lambda *operands: list(made(*operands))  280 us
    ppermute x44, waiting for transfers between devices, swap_seq(): return lax.ppermute(values, 'seq', [(i, i ^ bits) for i in range(SEQ)])  91.9 us
    ppermute x44, starting transfers between devices, swap_seq(): return lax.ppermute(values, 'seq', [(i, i ^ bits) for i in range(SEQ)])  46.4 us
    ppermute x11, waiting for transfers between devices, swap(): return lax.ppermute(values, 'fsdp', [(i, i ^ 1) for i in range(self.count)])  29.8 us
    ppermute x6, waiting for transfers between devices, shift(): lax.ppermute(values, 'fsdp', [(i, (i + 2 * by) % self.count) for i in ran...  28 us
    all_gather x3, waiting for transfers between devices, gather_row(): lax.all_gather(values, 'fsdp', axis=0, tiled=True, axis_index_groups=self...  17.8 us
    unnamed x108, local copies, waits for them, and re-layouts  16 us
  transfers between devices with their start and end apart: 67, of which 32 were waited for; matrix products, arithmetic and copies ran while one was open for 8% of the time, Pallas kernels for 39%

profile of v4, /device:TPU:9, one launch (start us, length us, event | category | flops | bytes accessed | tf_op | source)
XLA Modules:
  0.0 600.4 jit_solution(4900913721017573078)
XLA Ops:
  18.1 3.2 collective-permute-done.2.refs_5_
  21.2 16.2 %collective-permute-done.3.refs_6_ = bf16[208,640]{1,0:T(8,128)(2,1)S(1)} collective-permute-done((bf16[208,640]{1,0:T(8,128)(2,1)S(1)}, bf16[208,640]{1,0:T(8,128)(2,1)S(1)}, u32[]{:S(2)}, u32[]{:S(2)}) %collective-permute-start.3) | collective-permute-done | bytes 266272 | tf_op jit(solution)/shard_map/ppermute | solution.py:785
  37.4 3.2 collective-permute-done.4.refs_7_
  57.1 4.6 collective-permute-done.7.refs_9_
  63.0 5.6 multiply_sine_fusion
  68.6 4.5 collective-permute-done.9.refs_11_
  73.7 11.1 %shard_map.280 = (bf16[2048,1152]{1,0:T(8,128)(2,1)}, bf16[2048,256]{1,0:T(8,128)(2,1)}, bf16[2048,256]{1,0:T(8,128)(2,1)}, f32[2048,256]{1,0:T(8,128)}, f32[204...) custom-call(s32[9]{0:T(128)} %stack.140.meta_ref, ...), custom_call_target="tpu_custom_call" | custom-call | flops 48318384 | bytes 256491 | tf_op jit(solution)/shard_map/pallas_call | solution.py:84
  98.3 17.5 %shard_map.281 = (bf16[512,256]{1,0:T(8,128)(2,1)}, bf16[512,256]{1,0:T(8,128)(2,1)}, bf16[512,256]{1,0:T(8,128)(2,1)}, bf16[512,256]{1,0:T(8,128)(2,1)}, bf16[2048,2048]{1,0:T(8,128)(2,1)}) custom-call(s32[9]{0:T(128)} %stack.140.meta_ref, bf16[2048,256]{1,0:T(8,128)(2,1)} %get-tuple-element.117.q_ref, bf16[2048,256]{1,0:T(8,128)(2,1)} %get-tuple-element.118.mine_ref, ...), custom_call_target="tpu_custom_call" | custom-call | flops 85899344 | bytes 188743 | tf_op jit(solution)/shard_map/pallas_call | solution.py:84
  117.1 17.8 %all-gather.6.cloned.1.call-done = bf16[576,1728]{1,0:T(8,128)(2,1)} async-done(((bf16[144,1728]{1,0:T(8,128)(2,1)}), bf16[576,1728]{1,0:T(8,128)(2,1)}) %all-gather.6.cloned.1.call-update) | async-done | bytes 1990672 | tf_op jit(solution)/shard_map/all_gather | solution.py:790
  141.9 5.7 collective-permute-done.13.refs_2_
  147.6 6.4 %collective-permute-done.14.refs_3_ = bf16[512,256]{1,0:T(8,128)(2,1)S(1)} collective-permute-done((bf16[512,256]{1,0:T(8,128)(2,1)}, bf16[512,256]{1,0:T(8,128)(2,1)S(1)}, u32[]{:S(2)}, u32[]{:S(2)}) %collective-permute-start.14) | collective-permute-done | bytes 262176 | tf_op jit(solution)/shard_map/ppermute | solution.py:749
  155.1 7.0 %shard_map.282 = (bf16[512,1024]{1,0:T(8,128)(2,1)}, bf16[1024,1152]{1,0:T(8,128)(2,1)}, f32[512,1152]{1,0:T(8,128)}, f32[512,1152]{1,0:T(8,128)}, bf16[512,1152]{1,0:T(8,128)(2,1)}) custom-call(s32[1]{0:T(128)} %bitcast.me_ref, bf16[512,1152]{1,0:T(8,128)(2,1)} %refs_3_.1, bf16[512,256]{1,0:T(8,128)(2,1)} %get-tuple-element.122.refs_0_, ...), custom_call_target="tpu_custom_call" | custom-call | flops 24159192 | bytes 186122 | tf_op jit(solution)/shard_map/pallas_call | solution.py:84
  163.3 17.8 %collective-permute-done.20.refs_4_ = bf16[4,144,1728]{2,1,0:T(8,128)(2,1)S(1)} collective-permute-done((bf16[4,144,1728]{2,1,0:T(8,128)(2,1)}, bf16[4,144,1728]{2,1,0:T(8,128)(2,1)S(1)}, u32[]{:S(2)}, u32[]{:S(2)}) %collective-permute-start.20) | collective-permute-done | bytes 1990688 | tf_op jit(solution)/shard_map/ppermute | solution.py:782
  183.4 11.0 %shard_map.283 = (bf16[2048,1728]{1,0:T(8,128)(2,1)}, bf16[2048,1728]{1,0:T(8,128)(2,1)}, bf16[2048,1728]{1,0:T(8,128)(2,1)}, bf16[1152,1728]{1,0:T(8,128)(2,1)}, bf16[1152,1728]{1,0:T(8,128)(2,1)}) custom-call(s32[1]{0:T(128)} %bitcast.29.meta_ref, bf16[512,1152]{1,0:T(8,128)(2,1)} %copy-done.2, bf16[4,144,1728]{2,1,0:T(8,128)(2,1)} %bitcast.145, ...), custom_call_target="tpu_custom_call" | custom-call | flops 326149088 | bytes 583925 | tf_op jit(solution)/shard_map/pallas_call | solution.py:84
  199.8 16.4 %shard_map.284 = (bf16[2048,1728]{1,0:T(8,128)(2,1)}, bf16[2048,1728]{1,0:T(8,128)(2,1)}, bf16[2048,1728]{1,0:T(8,128)(2,1)}) custom-call(s32[1]{0:T(128)} %bitcast.29.meta_ref, bf16[512,1152]{1,0:T(8,128)(2,1)} %collective-permute-done.18.refs_0_.refs_2_, bf16[512,1152]{1,0:T(8,128)(2,1)} %copy-done.3, ...), custom_call_target="tpu_custom_call", output_to_operand_aliasing={{0}: (5, {}), {1}: (6, {}), {2}: (7, {})} | custom-call | flops 326149088 | bytes 424673 | tf_op jit(solution)/shard_map/pallas_call | solution.py:84
  216.2 13.0 %shard_map.285 = (bf16[512,1152]{1,0:T(8,128)(2,1)}, bf16[512,1152]{1,0:T(8,128)(2,1)}, bf16[512,1152]{1,0:T(8,128)(2,1)}) custom-call(bf16[2048,1728]{1,0:T(8,128)(2,1)} %get-tuple-element.139.x_ref.refs_0_, bf16[1728,1152]{1,0:T(8,128)(2,1)} %all-gather.8.cloned.1.call-done.w_ref.down_ref.refs_4_), custom_call_target="tpu_custom_call" | custom-call | flops 122305904 | bytes 70778 | tf_op jit(solution)/shard_map/pallas_call | solution.py:84
  235.4 13.8 %shard_map.286 = (bf16[2048,1728]{1,0:T(8,128)(2,1)}, bf16[2048,1728]{1,0:T(8,128)(2,1)}, bf16[2048,1728]{1,0:T(8,128)(2,1)}, bf16[512,1152]{1,0:T(8,128)(2,1)}) custom-call(bf16[512,1152]{1,0:T(8,128)(2,1)} %get-tuple-element.169.x_ref.refs_0_, ...), custom_call_target="tpu_custom_call", output_to_operand_aliasing={{0}: (4, {}), {1}: (5, {}), {2}: (6, {})} | custom-call | flops 122305904 | bytes 448266 | tf_op jit(solution)/shard_map/pallas_call | solution.py:84
  249.2 12.3 %collective-permute-done.25.refs_2_ = bf16[512,1152]{1,0:T(8,128)(2,1)} collective-permute-done((bf16[512,1152]{1,0:T(8,128)(2,1)S(1)}, bf16[512,1152]{1,0:T(8,128)(2,1)}, u32[]{:S(2)}, u32[]{:S(2)}) %collective-permute-start.25) | collective-permute-done | bytes 1179680 | tf_op jit(solution)/shard_map/ppermute | solution.py:749
  261.5 5.9 shard_map.287
  272.3 26.4 %shard_map.288 = (bf16[1024,1728]{1,0:T(8,128)(2,1)}, bf16[1024,1728]{1,0:T(8,128)(2,1)}, bf16[512,1152]{1,0:T(8,128)(2,1)}, bf16[512,1152]{1,0:T(8,128)(2,1)}) custom-call(bf16[512,1152]{1,0:T(8,128)(2,1)} %get-tuple-element.151.refs_0_.refs_1_, bf16[512,1152]{1,0:T(8,128)(2,1)} %copy-done.6, bf16[2048,1728]{1,0:T(8,128)(2,1)} %get-tuple-element.152.refs_2_, ...), custom_call_target="tpu_custom_call" | custom-call | flops 244611808 | bytes 188743 | tf_op jit(solution)/shard_map/pallas_call | solution.py:84
  302.7 16.0 %shard_map.289 = (bf16[4,216,1152]{2,1,0:T(8,128)(2,1)}, bf16[4,216,1152]{2,1,0:T(8,128)(2,1)}) custom-call(s32[1]{0:T(128)} %bitcast.29.meta_ref, bf16[2048,1728]{1,0:T(8,128)(2,1)} %get-tuple-element.155.refs_0_, bf16[512,1152]{1,0:T(8,128)(2,1)} %get-tuple-element.151.refs_0_.refs_1_, bf16[512,1152]{1,0:T(8,128)(2,1)} %copy-done.6, ...), custom_call_target="tpu_custom_call" | custom-call | flops 163074544 | bytes 79626 | tf_op jit(solution)/shard_map/pallas_call | solution.py:84
  319.9 26.5 %shard_map.290 = (bf16[1024,1728]{1,0:T(8,128)(2,1)}, bf16[1024,1728]{1,0:T(8,128)(2,1)}, bf16[512,1152]{1,0:T(8,128)(2,1)}, bf16[512,1152]{1,0:T(8,128)(2,1)}) custom-call(bf16[512,1152]{1,0:T(8,128)(2,1)} %copy-done.5, bf16[512,1152]{1,0:T(8,128)(2,1)} %copy-done.7, bf16[2048,1728]{1,0:T(8,128)(2,1)} %get-tuple-element.152.refs_2_, ...), custom_call_target="tpu_custom_call" | custom-call | flops 244611808 | bytes 188743 | tf_op jit(solution)/shard_map/pallas_call | solution.py:84
  347.3 3.4 collective-permute-done.29.refs_1_
  351.7 3.7 shard_map.291
  355.4 15.4 %shard_map.292 = (bf16[4,144,1728]{2,1,0:T(8,128)(2,1)}, bf16[4,144,1728]{2,1,0:T(8,128)(2,1)}) custom-call(s32[1]{0:T(128)} %bitcast.29.meta_ref, bf16[512,1152]{1,0:T(8,128)(2,1)} %get-tuple-element.169.x_ref.refs_0_, bf16[512,1152]{1,0:T(8,128)(2,1)} %copy-done.2, bf16[512,1152]{1,0:T(8,128)(2,1)} %collective-permute-done.18.refs_0_.refs_2_, ...), custom_call_target="tpu_custom_call" | custom-call | flops 163074544 | bytes 79626 | tf_op jit(solution)/shard_map/pallas_call | solution.py:84
  370.8 4.2 shard_map.293
  376.6 15.4 %shard_map.294 = (bf16[4,144,1728]{2,1,0:T(8,128)(2,1)}, bf16[4,144,1728]{2,1,0:T(8,128)(2,1)}) custom-call(s32[1]{0:T(128)} %bitcast.29.meta_ref, bf16[512,1152]{1,0:T(8,128)(2,1)} %get-tuple-element.169.x_ref.refs_0_, bf16[512,1152]{1,0:T(8,128)(2,1)} %copy-done.2, bf16[512,1152]{1,0:T(8,128)(2,1)} %collective-permute-done.18.refs_0_.refs_2_, ...), custom_call_target="tpu_custom_call" | custom-call | flops 163074544 | bytes 79626 | tf_op jit(solution)/shard_map/pallas_call | solution.py:84
  393.2 9.4 %collective-permute-done.32.c_ref = bf16[512,1152]{1,0:T(8,128)(2,1)} collective-permute-done((bf16[512,1152]{1,0:T(8,128)(2,1)}, bf16[512,1152]{1,0:T(8,128)(2,1)}, u32[]{:S(2)}, u32[]{:S(2)}) %collective-permute-start.32) | collective-permute-done | bytes 1179680 | tf_op jit(solution)/shard_map/ppermute | solution.py:749
  402.6 9.9 %shard_map.295 = (f32[512,1152]{1,0:T(8,128)}, bf16[512,1152]{1,0:T(8,128)(2,1)}, bf16[512,256]{1,0:T(8,128)(2,1)}, bf16[512,256]{1,0:T(8,128)(2,1)}, bf16[512,2...) custom-call(s32[1]{0:T(128)} %bitcast.me_ref, bf16[512,1152]{1,0:T(8,128)(2,1)} %get-tuple-element.173.a_ref, ...), custom_call_target="tpu_custom_call" | custom-call | flops 24159192 | bytes 91842 | tf_op jit(solution)/shard_map/pallas_call | solution.py:84
  415.7 6.5 %collective-permute-done.34.refs_2_ = bf16[512,256]{1,0:T(8,128)(2,1)S(1)} collective-permute-done((bf16[512,256]{1,0:T(8,128)(2,1)}, bf16[512,256]{1,0:T(8,128)(2,1)S(1)}, u32[]{:S(2)}, u32[]{:S(2)}) %collective-permute-start.34) | collective-permute-done | bytes 262176 | tf_op jit(solution)/shard_map/ppermute | solution.py:749
  422.2 6.0 collective-permute-done.35.refs_3_
  428.2 4.4 shard_map.296
  432.7 19.1 %shard_map.297 = (f32[2048,256]{1,0:T(8,128)}, f32[2048,256]{1,0:T(8,128)}, bf16[2048,256]{1,0:T(8,128)(2,1)}) custom-call(s32[9]{0:T(128)} %stack.140.meta_ref, bf16[2048,256]{1,0:T(8,128)(2,1)} %get-tuple-element.117.q_ref, bf16[2048,256]{1,0:T(8,128)(2,1)} %get-tuple-element.118.mine_ref, bf16[2048,256]{1,0:T(8,128)(2,1)} %copy-done.11, ...), custom_call_target="tpu_custom_call" | custom-call | flops 171798688 | bytes 104857 | tf_op jit(solution)/shard_map/pallas_call | solution.py:84
  454.9 11.8 %shard_map.298 = (bf16[2048,512]{1,0:T(8,128)(2,1)}, f32[1,256]{1,0:T(1,128)}, f32[1,256]{1,0:T(1,128)}, bf16[512,1152]{1,0:T(8,128)(2,1)}, bf16[512,1152]{1,0:T...) custom-call(s32[1]{0:T(128)} %bitcast.1.core_ref, f32[2048,256]{1,0:T(8,128)} %get-tuple-element.183.refs_0_, ...), custom_call_target="tpu_custom_call" | custom-call | flops 48318384 | bytes 136355 | tf_op jit(solution)/shard_map/pallas_call | solution.py:84
  468.0 4.3 shard_map.300
  472.3 3.1 convolution_convert_fusion
  482.9 6.6 %shard_map.301 = (bf16[4,144,512]{2,1,0:T(8,128)(2,1)}, bf16[4,144,512]{2,1,0:T(8,128)(2,1)}) custom-call(s32[1]{0:T(128)} %bitcast.29.meta_ref, bf16[2048,1152]{1,0:T(8,128)(2,1)} %get-tuple-element.203.refs_0_, bf16[2048,512]{1,0:T(8,128)(2,1)} %get-tuple-element.200.refs_1_), custom_call_target="tpu_custom_call" | custom-call | flops 48318384 | bytes 23592 | tf_op jit(solution)/shard_map/pallas_call | solution.py:84
  489.6 5.0 collective-permute-done.44
  502.5 6.5 %collective-permute-done.53 = bf16[216,1152]{1,0:T(8,128)(2,1)} collective-permute-done((bf16[216,1152]{1,0:T(8,128)(2,1)}, bf16[216,1152]{1,0:T(8,128)(2,1)}, u32[]{:S(2)}, u32[]{:S(2)}) %collective-permute-start.53) | collective-permute-done | bytes 497696 | tf_op jit(solution)/shard_map/ppermute | solution.py:749
  509.1 3.7 collective-permute-start.54
  520.1 3.7 collective-permute-start.49
  526.0 3.7 shard_map.302
  537.7 6.0 shard_map.303
  546.4 5.5 shard_map.299
  551.9 3.1 collective-permute-done.47
  568.1 4.2 collective-permute-start.57
  572.4 6.8 %collective-permute-done.59.refs_2_ = bf16[144,1728]{1,0:T(8,128)(2,1)S(1)} collective-permute-done((bf16[144,1728]{1,0:T(8,128)(2,1)S(1)}, bf16[144,1728]{1,0:T(8,128)(2,1)S(1)}, u32[]{:S(2)}, u32[]{:S(2)}) %collective-permute-start.59) | collective-permute-done | bytes 497696 | tf_op jit(solution)/shard_map/ppermute | solution.py:749
  587.9 5.5 shard_map.304
  (324 shorter events, 146.8 us)
Async XLA Ops:
  7.2 83.6 %all-gather.4.cloned.1.call-start = ((), (), s32[]{:S(2)}) async-start(), calls=%async_computation.3 | async-start | bytes 2580480 | tf_op jit(solution)/shard_map/all_gather | solution.py:790
  13.0 27.6 %collective-permute-start.1 = (bf16[512,1152]{1,0:T(8,128)(2,1)}, bf16[512,1152]{1,0:T(8,128)(2,1)S(1)}, u32[]{:S(2)}, u32[]{:S(2)}) collective-permute-start(bf16[512,1152]{1,0:T(8,128)(2,1)} %refs_3_.1), channel_id=1, source_target_pairs={{0,2},{1,3},{2,0},{3,1},{4,6},{5,7},{6,4},{7,5},{8,10},{9,11},{10,... | collective-permute-start | bytes 3538952 | tf_op jit(solution)/shard_map/ppermute | solution.py:749
  15.6 21.9 %collective-permute-start.3 = (bf16[208,640]{1,0:T(8,128)(2,1)S(1)}, bf16[208,640]{1,0:T(8,128)(2,1)S(1)}, u32[]{:S(2)}, u32[]{:S(2)}) collective-permute-start(bf16[208,640]{1,0:T(8,128)(2,1)S(1)} %fusion.9.refs_4_), channel_id=1, source_target_pairs={{0,16},{4,20},{8,24},{12,28},{16,0},{20,4},{24,8},{28,12},{1,17},{... | collective-permute-start | bytes 798728 | tf_op jit(solution)/shard_map/ppermute | solution.py:785
  16.6 24.0 %collective-permute-start.4 = (bf16[208,640]{1,0:T(8,128)(2,1)S(1)}, bf16[208,640]{1,0:T(8,128)(2,1)S(1)}, u32[]{:S(2)}, u32[]{:S(2)}) collective-permute-start(bf16[208,640]{1,0:T(8,128)(2,1)S(1)} %fusion.9.refs_4_), channel_id=1, source_target_pairs={{0,24},{4,28},{8,0},{12,4},{16,8},{20,12},{24,16},{28,20},{1,25},{... | collective-permute-start | bytes 798728 | tf_op jit(solution)/shard_map/ppermute | solution.py:785
  44.1 90.8 %all-gather.6.cloned.1.call-start = ((), (), s32[]{:S(2)}) async-start(), calls=%async_computation.4 | async-start | bytes 2580480 | tf_op jit(solution)/shard_map/all_gather | solution.py:790
  47.2 169.0 %all-gather.8.cloned.1.call-start = ((), (), s32[]{:S(2)}) async-start(), calls=%async_computation.5 | async-start | bytes 4976640 | tf_op jit(solution)/shard_map/all_gather | solution.py:790
  47.3 25.8 %collective-permute-start = (bf16[512,1152]{1,0:T(8,128)(2,1)S(1)}, bf16[512,1152]{1,0:T(8,128)(2,1)}, u32[]{:S(2)}, u32[]{:S(2)}) collective-permute-start(bf16[512,1152]{1,0:T(8,128)(2,1)S(1)} %copy-done.4), channel_id=1, source_target_pairs={{0,1},{1,0},{2,3},{3,2},{4,5},{5,4},{6,7},{7,6},{8,9},{9,8},{10,11... | collective-permute-start | bytes 3538952 | tf_op jit(solution)/shard_map/ppermute | solution.py:749
  48.3 24.8 %collective-permute-start.5 = (bf16[512,1152]{1,0:T(8,128)(2,1)S(1)}, bf16[512,1152]{1,0:T(8,128)(2,1)}, u32[]{:S(2)}, u32[]{:S(2)}) collective-permute-start(bf16[512,1152]{1,0:T(8,128)(2,1)S(1)} %collective-permute-done.1.refs_2_), channel_id=1, source_target_pairs={{0,1},{1,0},{2,3},{3,2},{4,5},{5,4},{6,7},{7,6},{8,9},{9,8},{10,11... | collective-permute-start | bytes 3538952 | tf_op jit(solution)/shard_map/ppermute | solution.py:749
  49.7 12.0 %collective-permute-start.7 = (bf16[208,640]{1,0:T(8,128)(2,1)}, bf16[208,640]{1,0:T(8,128)(2,1)}, u32[]{:S(2)}, u32[]{:S(2)}) collective-permute-start(bf16[208,640]{1,0:T(8,128)(2,1)} %copy-done.34), channel_id=1, source_target_pairs={{0,4},{4,0},{8,12},{12,8},{16,20},{20,16},{24,28},{28,24},{1,5},{5... | collective-permute-start | bytes 798728 | tf_op jit(solution)/shard_map/ppermute | solution.py:782
  50.7 17.9 %collective-permute-start.8 = (bf16[208,640]{1,0:T(8,128)(2,1)}, bf16[208,640]{1,0:T(8,128)(2,1)S(1)}, u32[]{:S(2)}, u32[]{:S(2)}) collective-permute-start(bf16[208,640]{1,0:T(8,128)(2,1)} %copy-done.35), channel_id=1, source_target_pairs={{0,4},{4,0},{8,12},{12,8},{16,20},{20,16},{24,28},{28,24},{1,5},{5... | collective-permute-start | bytes 798728 | tf_op jit(solution)/shard_map/ppermute | solution.py:782
  55.9 17.1 %collective-permute-start.9 = (bf16[208,640]{1,0:T(8,128)(2,1)}, bf16[208,640]{1,0:T(8,128)(2,1)S(1)}, u32[]{:S(2)}, u32[]{:S(2)}) collective-permute-start(bf16[208,640]{1,0:T(8,128)(2,1)} %copy-done.36), channel_id=1, source_target_pairs={{0,4},{4,0},{8,12},{12,8},{16,20},{20,16},{24,28},{28,24},{1,5},{5... | collective-permute-start | bytes 798728 | tf_op jit(solution)/shard_map/ppermute | solution.py:782
  61.7 23.1 %collective-permute-start.22 = (bf16[216,1152]{1,0:T(8,128)(2,1)S(1)}, bf16[216,1152]{1,0:T(8,128)(2,1)S(1)}, u32[]{:S(2)}, u32[]{:S(2)}) collective-permute-start(bf16[216,1152]{1,0:T(8,128)(2,1)S(1)} %dynamic-slice_convert_fusion), channel_id=1, source_target_pairs={{0,4},{4,0},{8,12},{12,8},{16,20},{20,16},{24,28},{28,24},{1,5},{5... | collective-permute-start | bytes 1493000 | tf_op jit(solution)/shard_map/ppermute | solution.py:782
  88.2 363.8 %reduce-scatter.10.cloned.1.call-start = ((), (), s32[]{:S(2)}) async-start(), calls=%async_computation.8 | async-start | bytes 2488320
  90.8 50.2 %collective-permute-start.11 = (bf16[4,144,1728]{2,1,0:T(8,128)(2,1)}, bf16[4,144,1728]{2,1,0:T(8,128)(2,1)}, u32[]{:S(2)}, u32[]{:S(2)}) collective-permute-start(bf16[4,144,1728]{2,1,0:T(8,128)(2,1)} %bitcast.144), channel_id=1, source_target_pairs={{0,4},{4,0},{8,12},{12,8},{16,20},{20,16},{24,28},{28,24},{1,5},{5... | collective-permute-start | bytes 5971976 | tf_op jit(solution)/shard_map/ppermute | solution.py:782
  115.8 21.5 %collective-permute-start.16 = (bf16[256,1152]{1,0:T(8,128)(2,1)S(1)}, bf16[256,1152]{1,0:T(8,128)(2,1)S(1)}, u32[]{:S(2)}, u32[]{:S(2)}) collective-permute-start(bf16[256,1152]{1,0:T(8,128)(2,1)S(1)} %copy-done.24), channel_id=1, source_target_pairs={{0,2},{1,3},{2,0},{3,1},{4,6},{5,7},{6,4},{7,5},{8,10},{9,11},{10,... | collective-permute-start | bytes 1769480 | tf_op jit(solution)/shard_map/ppermute | solution.py:749
  134.9 46.2 %collective-permute-start.20 = (bf16[4,144,1728]{2,1,0:T(8,128)(2,1)}, bf16[4,144,1728]{2,1,0:T(8,128)(2,1)S(1)}, u32[]{:S(2)}, u32[]{:S(2)}) collective-permute-start(bf16[4,144,1728]{2,1,0:T(8,128)(2,1)} %bitcast.146), channel_id=1, source_target_pairs={{0,4},{4,0},{8,12},{12,8},{16,20},{20,16},{24,28},{28,24},{1,5},{5... | collective-permute-start | bytes 5971976 | tf_op jit(solution)/shard_map/ppermute | solution.py:782
  136.1 17.9 %collective-permute-start.15 = (bf16[256,1152]{1,0:T(8,128)(2,1)S(1)}, bf16[256,1152]{1,0:T(8,128)(2,1)S(1)}, u32[]{:S(2)}, u32[]{:S(2)}) collective-permute-start(bf16[256,1152]{1,0:T(8,128)(2,1)S(1)} %copy-done.24), channel_id=1, source_target_pairs={{0,1},{1,0},{2,3},{3,2},{4,5},{5,4},{6,7},{7,6},{8,9},{9,8},{10,11... | collective-permute-start | bytes 1769480 | tf_op jit(solution)/shard_map/ppermute | solution.py:749
  137.3 16.8 %collective-permute-start.17 = (bf16[256,1152]{1,0:T(8,128)(2,1)S(1)}, bf16[256,1152]{1,0:T(8,128)(2,1)S(1)}, u32[]{:S(2)}, u32[]{:S(2)}) collective-permute-start(bf16[256,1152]{1,0:T(8,128)(2,1)S(1)} %collective-permute-done.16.refs_6_), channel_id=1, source_target_pairs={{0,1},{1,0},{2,3},{3,2},{4,5},{5,4},{6,7},{7,6},{8,9},{9,8},{10,11... | collective-permute-start | bytes 1769480 | tf_op jit(solution)/shard_map/ppermute | solution.py:749
  141.1 13.0 %collective-permute-start.14 = (bf16[512,256]{1,0:T(8,128)(2,1)}, bf16[512,256]{1,0:T(8,128)(2,1)S(1)}, u32[]{:S(2)}, u32[]{:S(2)}) collective-permute-start(bf16[512,256]{1,0:T(8,128)(2,1)} %get-tuple-element.125), channel_id=1, source_target_pairs={{0,3},{1,2},{2,1},{3,0},{4,7},{5,6},{6,5},{7,4},{8,11},{9,10},{10,... | collective-permute-start | bytes 786440 | tf_op jit(solution)/shard_map/ppermute | solution.py:749
  162.1 19.0 %collective-permute-start.19 = (bf16[512,1152]{1,0:T(8,128)(2,1)}, bf16[512,1152]{1,0:T(8,128)(2,1)S(1)}, u32[]{:S(2)}, u32[]{:S(2)}) collective-permute-start(bf16[512,1152]{1,0:T(8,128)(2,1)} %get-tuple-element.169.x_ref.refs_0_), channel_id=1, source_target_pairs={{0,1},{1,0},{2,3},{3,2},{4,5},{5,4},{6,7},{7,6},{8,9},{9,8},{10,11... | collective-permute-start | bytes 3538952 | tf_op jit(solution)/shard_map/ppermute | solution.py:749
  162.1 32.3 %collective-permute-start.18 = (bf16[512,1152]{1,0:T(8,128)(2,1)}, bf16[512,1152]{1,0:T(8,128)(2,1)}, u32[]{:S(2)}, u32[]{:S(2)}) collective-permute-start(bf16[512,1152]{1,0:T(8,128)(2,1)} %get-tuple-element.169.x_ref.refs_0_), channel_id=1, source_target_pairs={{0,2},{1,3},{2,0},{3,1},{4,6},{5,7},{6,4},{7,5},{8,10},{9,11},{10,... | collective-permute-start | bytes 3538952 | tf_op jit(solution)/shard_map/ppermute | solution.py:749
  234.2 27.4 %collective-permute-start.25 = (bf16[512,1152]{1,0:T(8,128)(2,1)S(1)}, bf16[512,1152]{1,0:T(8,128)(2,1)}, u32[]{:S(2)}, u32[]{:S(2)}) collective-permute-start(bf16[512,1152]{1,0:T(8,128)(2,1)S(1)} %add_convert_fusion.1), channel_id=1, source_target_pairs={{0,2},{1,3},{2,0},{3,1},{4,6},{5,7},{6,4},{7,5},{8,10},{9,11},{10,... | collective-permute-start | bytes 3538952 | tf_op jit(solution)/shard_map/ppermute | solution.py:749
  268.6 30.2 %collective-permute-start.27 = (bf16[512,1152]{1,0:T(8,128)(2,1)}, bf16[512,1152]{1,0:T(8,128)(2,1)S(1)}, u32[]{:S(2)}, u32[]{:S(2)}) collective-permute-start(bf16[512,1152]{1,0:T(8,128)(2,1)} %get-tuple-element.151.refs_0_.refs_1_), channel_id=1, source_target_pairs={{0,2},{1,3},{2,0},{3,1},{4,6},{5,7},{6,4},{7,5},{8,10},{9,11},{10,... | collective-permute-start | bytes 3538952 | tf_op jit(solution)/shard_map/ppermute | solution.py:749
  318.7 52.1 %collective-permute-start.31 = (bf16[4,216,1152]{2,1,0:T(8,128)(2,1)}, bf16[4,216,1152]{2,1,0:T(8,128)(2,1)}, u32[]{:S(2)}, u32[]{:S(2)}) collective-permute-start(bf16[4,216,1152]{2,1,0:T(8,128)(2,1)} %get-tuple-element.158), channel_id=1, source_target_pairs={{0,4},{4,0},{8,12},{12,8},{16,20},{20,16},{24,28},{28,24},{1,5},{5... | collective-permute-start | bytes 5971976 | tf_op jit(solution)/shard_map/ppermute | solution.py:782
  375.0 125.9 %reduce-scatter.6.cloned.1.call-start = ((), (), s32[]{:S(2)}) async-start(), calls=%async_computation.6 | async-start | bytes 2580480 | tf_op jit(solution)/shard_map/reduce_scatter | solution.py:835
  375.1 53.1 %collective-permute-start.36 = (bf16[4,144,1728]{2,1,0:T(8,128)(2,1)}, bf16[4,144,1728]{2,1,0:T(8,128)(2,1)}, u32[]{:S(2)}, u32[]{:S(2)}) collective-permute-start(bf16[4,144,1728]{2,1,0:T(8,128)(2,1)} %get-tuple-element.167), channel_id=1, source_target_pairs={{0,4},{4,0},{8,12},{12,8},{16,20},{20,16},{24,28},{28,24},{1,5},{5... | collective-permute-start | bytes 5971976 | tf_op jit(solution)/shard_map/ppermute | solution.py:782
  375.4 27.2 %collective-permute-start.32 = (bf16[512,1152]{1,0:T(8,128)(2,1)}, bf16[512,1152]{1,0:T(8,128)(2,1)}, u32[]{:S(2)}, u32[]{:S(2)}) collective-permute-start(bf16[512,1152]{1,0:T(8,128)(2,1)} %shard_map.291), channel_id=1, source_target_pairs={{0,2},{1,3},{2,0},{3,1},{4,6},{5,7},{6,4},{7,5},{8,10},{9,11},{10,... | collective-permute-start | bytes 3538952 | tf_op jit(solution)/shard_map/ppermute | solution.py:749
  391.9 74.7 %collective-permute-start.41 = (bf16[4,144,1728]{2,1,0:T(8,128)(2,1)}, bf16[4,144,1728]{2,1,0:T(8,128)(2,1)S(1)}, u32[]{:S(2)}, u32[]{:S(2)}) collective-permute-start(bf16[4,144,1728]{2,1,0:T(8,128)(2,1)} %get-tuple-element.172), channel_id=1, source_target_pairs={{0,4},{4,0},{8,12},{12,8},{16,20},{20,16},{24,28},{28,24},{1,5},{5... | collective-permute-start | bytes 5971976 | tf_op jit(solution)/shard_map/ppermute | solution.py:782
  415.3 12.9 %collective-permute-start.35 = (bf16[512,256]{1,0:T(8,128)(2,1)}, bf16[512,256]{1,0:T(8,128)(2,1)S(1)}, u32[]{:S(2)}, u32[]{:S(2)}) collective-permute-start(bf16[512,256]{1,0:T(8,128)(2,1)} %get-tuple-element.180), channel_id=1, source_target_pairs={{0,3},{1,2},{2,1},{3,0},{4,7},{5,6},{6,5},{7,4},{8,11},{9,10},{10,... | collective-permute-start | bytes 786440 | tf_op jit(solution)/shard_map/ppermute | solution.py:749
  432.7 127.0 %reduce-scatter.8.cloned.1.call-start = ((), (), s32[]{:S(2)}) async-start(), calls=%async_computation.7 | async-start | bytes 2580480 | tf_op jit(solution)/shard_map/reduce_scatter | solution.py:835
  479.6 15.0 %collective-permute-start.44 = (bf16[8,32,1152]{2,1,0:T(8,128)(2,1)}, bf16[8,32,1152]{2,1,0:T(8,128)(2,1)}, u32[]{:S(2)}, u32[]{:S(2)}) collective-permute-start(bf16[8,32,1152]{2,1,0:T(8,128)(2,1)} %get-tuple-element.238), channel_id=1, source_target_pairs={{0,2},{1,3},{2,0},{3,1},{4,6},{5,7},{6,4},{7,5},{8,10},{9,11},{10,... | collective-permute-start | bytes 1769480 | tf_op jit(solution)/shard_map/ppermute | solution.py:749
  481.5 20.8 %collective-permute-start.39 = (bf16[512,1152]{1,0:T(8,128)(2,1)}, bf16[512,1152]{1,0:T(8,128)(2,1)S(1)}, u32[]{:S(2)}, u32[]{:S(2)}) collective-permute-start(bf16[512,1152]{1,0:T(8,128)(2,1)} %get-tuple-element.194), channel_id=1, source_target_pairs={{0,1},{1,0},{2,3},{3,2},{4,5},{5,4},{6,7},{7,6},{8,9},{9,8},{10,11... | collective-permute-start | bytes 3538952 | tf_op jit(solution)/shard_map/ppermute | solution.py:749
  497.0 12.1 %collective-permute-start.53 = (bf16[216,1152]{1,0:T(8,128)(2,1)}, bf16[216,1152]{1,0:T(8,128)(2,1)}, u32[]{:S(2)}, u32[]{:S(2)}) collective-permute-start(bf16[216,1152]{1,0:T(8,128)(2,1)} %reduce-scatter.10.cloned.1.call-done), channel_id=1, source_target_pairs={{0,2},{1,3},{2,0},{3,1},{4,6},{5,7},{6,4},{7,5},{8,10},{9,11},{10,... | collective-permute-start | bytes 1493000 | tf_op jit(solution)/shard_map/ppermute | solution.py:749
  498.2 45.4 %collective-permute-start.38 = (bf16[512,1152]{1,0:T(8,128)(2,1)}, bf16[512,1152]{1,0:T(8,128)(2,1)}, u32[]{:S(2)}, u32[]{:S(2)}) collective-permute-start(bf16[512,1152]{1,0:T(8,128)(2,1)} %get-tuple-element.192), channel_id=1, source_target_pairs={{0,1},{1,0},{2,3},{3,2},{4,5},{5,4},{6,7},{7,6},{8,9},{9,8},{10,11... | collective-permute-start | bytes 3538952 | tf_op jit(solution)/shard_map/ppermute | solution.py:749
  501.0 13.1 %collective-permute-start.52 = (bf16[216,1152]{1,0:T(8,128)(2,1)}, bf16[216,1152]{1,0:T(8,128)(2,1)}, u32[]{:S(2)}, u32[]{:S(2)}) collective-permute-start(bf16[216,1152]{1,0:T(8,128)(2,1)} %reduce-scatter.10.cloned.1.call-done), channel_id=1, source_target_pairs={{0,1},{1,0},{2,3},{3,2},{4,5},{5,4},{6,7},{7,6},{8,9},{9,8},{10,11... | collective-permute-start | bytes 1493000 | tf_op jit(solution)/shard_map/ppermute | solution.py:749
  501.0 25.0 %collective-permute-start.45 = (bf16[4,208,640]{2,1,0:T(8,128)(2,1)}, bf16[4,208,640]{2,1,0:T(8,128)(2,1)}, u32[]{:S(2)}, u32[]{:S(2)}) collective-permute-start(bf16[4,208,640]{2,1,0:T(8,128)(2,1)} %fusion.5), channel_id=1, source_target_pairs={{0,4},{4,0},{8,12},{12,8},{16,20},{20,16},{24,28},{28,24},{1,5},{5... | collective-permute-start | bytes 3194888 | tf_op jit(solution)/shard_map/ppermute | solution.py:782
  502.3 17.8 %collective-permute-start.50 = (bf16[144,1728]{1,0:T(8,128)(2,1)}, bf16[144,1728]{1,0:T(8,128)(2,1)}, u32[]{:S(2)}, u32[]{:S(2)}) collective-permute-start(bf16[144,1728]{1,0:T(8,128)(2,1)} %reduce-scatter.6.cloned.1.call-done.refs_0_), channel_id=1, source_target_pairs={{0,2},{1,3},{2,0},{3,1},{4,6},{5,7},{6,4},{7,5},{8,10},{9,11},{10,... | collective-permute-start | bytes 1493000 | tf_op jit(solution)/shard_map/ppermute | solution.py:749
  509.1 14.7 %collective-permute-start.54 = (bf16[216,1152]{1,0:T(8,128)(2,1)}, bf16[216,1152]{1,0:T(8,128)(2,1)S(1)}, u32[]{:S(2)}, u32[]{:S(2)}) collective-permute-start(bf16[216,1152]{1,0:T(8,128)(2,1)} %collective-permute-done.53), channel_id=1, source_target_pairs={{0,1},{1,0},{2,3},{3,2},{4,5},{5,4},{6,7},{7,6},{8,9},{9,8},{10,11... | collective-permute-start | bytes 1493000 | tf_op jit(solution)/shard_map/ppermute | solution.py:749
  514.0 31.3 %collective-permute-start.40 = (bf16[512,1152]{1,0:T(8,128)(2,1)}, bf16[512,1152]{1,0:T(8,128)(2,1)S(1)}, u32[]{:S(2)}, u32[]{:S(2)}) collective-permute-start(bf16[512,1152]{1,0:T(8,128)(2,1)} %add_convert_fusion), channel_id=1, source_target_pairs={{0,2},{1,3},{2,0},{3,1},{4,6},{5,7},{6,4},{7,5},{8,10},{9,11},{10,... | collective-permute-start | bytes 3538952 | tf_op jit(solution)/shard_map/ppermute | solution.py:749
  520.1 13.0 %collective-permute-start.49 = (bf16[144,1728]{1,0:T(8,128)(2,1)S(1)}, bf16[144,1728]{1,0:T(8,128)(2,1)}, u32[]{:S(2)}, u32[]{:S(2)}) collective-permute-start(bf16[144,1728]{1,0:T(8,128)(2,1)S(1)} %copy-done.12), channel_id=1, source_target_pairs={{0,1},{1,0},{2,3},{3,2},{4,5},{5,4},{6,7},{7,6},{8,9},{9,8},{10,11... | collective-permute-start | bytes 1493000 | tf_op jit(solution)/shard_map/ppermute | solution.py:749
  523.8 11.7 %collective-permute-start.51 = (bf16[144,1728]{1,0:T(8,128)(2,1)}, bf16[144,1728]{1,0:T(8,128)(2,1)}, u32[]{:S(2)}, u32[]{:S(2)}) collective-permute-start(bf16[144,1728]{1,0:T(8,128)(2,1)} %collective-permute-done.50.refs_2_), channel_id=1, source_target_pairs={{0,1},{1,0},{2,3},{3,2},{4,5},{5,4},{6,7},{7,6},{8,9},{9,8},{10,11... | collective-permute-start | bytes 1493000 | tf_op jit(solution)/shard_map/ppermute | solution.py:749
  531.7 20.2 %collective-permute-start.46 = (bf16[208,640]{1,0:T(8,128)(2,1)}, bf16[208,640]{1,0:T(8,128)(2,1)}, u32[]{:S(2)}, u32[]{:S(2)}) collective-permute-start(bf16[208,640]{1,0:T(8,128)(2,1)} %get-tuple-element.255), channel_id=1, source_target_pairs={{0,8},{4,12},{8,16},{12,20},{16,24},{20,28},{24,0},{28,4},{1,9},{5... | collective-permute-start | bytes 798728 | tf_op jit(solution)/shard_map/ppermute | solution.py:785
  533.1 21.8 %collective-permute-start.47 = (bf16[208,640]{1,0:T(8,128)(2,1)}, bf16[208,640]{1,0:T(8,128)(2,1)S(1)}, u32[]{:S(2)}, u32[]{:S(2)}) collective-permute-start(bf16[208,640]{1,0:T(8,128)(2,1)} %get-tuple-element.257), channel_id=1, source_target_pairs={{0,16},{4,20},{8,24},{12,28},{16,0},{20,4},{24,8},{28,12},{1,17},{... | collective-permute-start | bytes 798728 | tf_op jit(solution)/shard_map/ppermute | solution.py:785
  535.5 22.6 %collective-permute-start.48 = (bf16[208,640]{1,0:T(8,128)(2,1)}, bf16[208,640]{1,0:T(8,128)(2,1)}, u32[]{:S(2)}, u32[]{:S(2)}) collective-permute-start(bf16[208,640]{1,0:T(8,128)(2,1)} %get-tuple-element.256), channel_id=1, source_target_pairs={{0,24},{4,28},{8,0},{12,4},{16,8},{20,12},{24,16},{28,20},{1,25},{... | collective-permute-start | bytes 798728 | tf_op jit(solution)/shard_map/ppermute | solution.py:785
  562.6 9.7 %collective-permute-start.55 = (bf16[208,640]{1,0:T(8,128)(2,1)S(1)}, bf16[208,640]{1,0:T(8,128)(2,1)S(1)}, u32[]{:S(2)}, u32[]{:S(2)}) collective-permute-start(bf16[208,640]{1,0:T(8,128)(2,1)S(1)} %get-tuple-element.271), channel_id=1, source_target_pairs={{0,1},{1,0},{2,3},{3,2},{4,5},{5,4},{6,7},{7,6},{8,9},{9,8},{10,11... | collective-permute-start | bytes 798728 | tf_op jit(solution)/shard_map/ppermute | solution.py:749
  564.3 14.9 %collective-permute-start.59 = (bf16[144,1728]{1,0:T(8,128)(2,1)S(1)}, bf16[144,1728]{1,0:T(8,128)(2,1)S(1)}, u32[]{:S(2)}, u32[]{:S(2)}) collective-permute-start(bf16[144,1728]{1,0:T(8,128)(2,1)S(1)} %copy-done.14), channel_id=1, source_target_pairs={{0,2},{1,3},{2,0},{3,1},{4,6},{5,7},{6,4},{7,5},{8,10},{9,11},{10,... | collective-permute-start | bytes 1493000 | tf_op jit(solution)/shard_map/ppermute | solution.py:749
  564.9 21.3 %collective-permute-start.58 = (bf16[144,1728]{1,0:T(8,128)(2,1)S(1)}, bf16[144,1728]{1,0:T(8,128)(2,1)S(1)}, u32[]{:S(2)}, u32[]{:S(2)}) collective-permute-start(bf16[144,1728]{1,0:T(8,128)(2,1)S(1)} %copy-done.14), channel_id=1, source_target_pairs={{0,1},{1,0},{2,3},{3,2},{4,5},{5,4},{6,7},{7,6},{8,9},{9,8},{10,11... | collective-permute-start | bytes 1493000 | tf_op jit(solution)/shard_map/ppermute | solution.py:749
  568.1 13.4 %collective-permute-start.57 = (bf16[208,640]{1,0:T(8,128)(2,1)S(1)}, bf16[208,640]{1,0:T(8,128)(2,1)S(1)}, u32[]{:S(2)}, u32[]{:S(2)}) collective-permute-start(bf16[208,640]{1,0:T(8,128)(2,1)S(1)} %collective-permute-done.56), channel_id=1, source_target_pairs={{0,1},{1,0},{2,3},{3,2},{4,5},{5,4},{6,7},{7,6},{8,9},{9,8},{10,11... | collective-permute-start | bytes 798728 | tf_op jit(solution)/shard_map/ppermute | solution.py:749
  (73 other events, 464.3 us)
Sparse Core Ops, SparseCore 0:
  44.3 44.9 all-gather.3
  90.9 43.9 all-gather.5
  137.1 75.1 all-gather.7
  375.1 41.0 reduce-scatter.9
  432.8 41.7 reduce-scatter.5
  481.3 41.0 reduce-scatter.7

commit v5 on v4

--- a/solution.py
+++ b/solution.py
@@ -829,7 +829,7 @@
         return [half for value in whole for half in self.halves(value)]
 
     def fold(self, here, come):
-        return add_half(here, come, here.shape[0])
+        return add_half(here, come, 2 if here.shape[0] % 2 == 0 else 1)
 
     def scatter_row(self, half):
         return lax.psum_scatter(
@@ -988,7 +988,7 @@
         [*shares, mixed, cotangent],
         [gains],
         [(tokens.shape, bf16), (tokens.shape, bf16)],
-        4,
+        2,
         [(1, model)],
     )
 
@@ -1002,7 +1002,7 @@
     come_down = owners.swap(away_down)
     far_blocks = list(lax.optimization_barrier((away_down, *ffo_blocks[2:]))[1:])
     far_gate, far_up, *far_share = back(far_blocks, value16, slope16, w_down, w_gate, w_up, 2)
-    pair = add_half(far_share[0], swap_seq(far_share[1], 1), 4)
+    pair = add_half(far_share[0], swap_seq(far_share[1], 1), 2)
     far_sum = swap_seq(pair, 2)
     near_one = swap_seq(near_share[1], 1)
     fed_left = [after(fed_blocks[0], pair, near_one)] + fed_blocks[1:]
@@ -1015,7 +1015,7 @@
     come_up = owners.swap(away_up)
     shares = [after(near_share[0], away_up), near_one, far_sum]
     grad_mixed, grad_attn16, *grad_heads, gain_mixed_part = mid_back(
-        self_index, shares, cotangent, mixed, attn, w_out, gains, 4
+        self_index, shares, cotangent, mixed, attn, w_out, gains, 2
     )
     grad_heads = [grad_heads[0]] + [swap_seq(grad_heads[r], r) for r in range(1, SEQ)]
 
@@ -1023,7 +1023,7 @@
     grad_gate = owners.scatter_row(half_gate)
     grad_heads[0] = after(grad_heads[0], half_gate)
     grad_queries, keep_kv, send_kv = attend_back(
-        meta, queries, mine_kv, other_kv, probs, grad_heads, scale, 256
+        meta, queries, mine_kv, other_kv, probs, grad_heads, scale, 512
     )
     come_kv = swap_seq(send_kv, 1)
     grad_qkv16, gain_query_part, gain_key_part, *normed_blocks = project_back(

time: 607 us -> 601 us (level)
  Pallas kernels: 280 us -> 271 us
    pallas_call x25, Pallas kernels: 280 us -> 271 us  [call(): return lambda *operands: list(made(*operands))]
  transfers between devices with their start and end apart: 67 -> 67, of which waited for: 32 -> 33; matrix products, arithmetic and copies ran while one was open for 8% -> 8% of each run, Pallas kernels for 39% -> 38%
where the time goes in v5:
time: 601 us; the launch traced here: 596 us
  Pallas kernels  271 us (45%)
  waiting for transfers between devices  171 us (28%)
  starting transfers between devices  66.6 us (11%)
  other arithmetic  35.4 us (6%)
  local copies, waits for them, and re-layouts  32.9 us (5%)
  between operations  15.1 us (3%)
    pallas_call x25, Pallas kernels, call(): return lambda *operands: list(made(*operands))  271 us
    ppermute x44, waiting for transfers between devices, swap_seq(): return lax.ppermute(values, 'seq', [(i, i ^ bits) for i in range(SEQ)])  93.5 us
    ppermute x44, starting transfers between devices, swap_seq(): return lax.ppermute(values, 'seq', [(i, i ^ bits) for i in range(SEQ)])  47.8 us
    ppermute x11, waiting for transfers between devices, swap(): return lax.ppermute(values, 'fsdp', [(i, i ^ 1) for i in range(self.count)])  32.9 us
    ppermute x6, waiting for transfers between devices, shift(): lax.ppermute(values, 'fsdp', [(i, (i + 2 * by) % self.count) for i in ran...  27.1 us
    all_gather x3, waiting for transfers between devices, gather_row(): lax.all_gather(values, 'fsdp', axis=0, tiled=True, axis_index_groups=self...  17.8 us
    unnamed x108, local copies, waits for them, and re-layouts  16 us
  transfers between devices with their start and end apart: 67, of which 33 were waited for; matrix products, arithmetic and copies ran while one was open for 8% of the time, Pallas kernels for 38%

profile of v5, /device:TPU:9, one launch (start us, length us, event | category | flops | bytes accessed | tf_op | source)
XLA Modules:
  0.0 595.8 jit_solution(16909120241531621814)
XLA Ops:
  18.1 3.2 collective-permute-done.2.refs_5_
  21.2 16.2 %collective-permute-done.3.refs_6_ = bf16[208,640]{1,0:T(8,128)(2,1)S(1)} collective-permute-done((bf16[208,640]{1,0:T(8,128)(2,1)S(1)}, bf16[208,640]{1,0:T(8,128)(2,1)S(1)}, u32[]{:S(2)}, u32[]{:S(2)}) %collective-permute-start.3) | collective-permute-done | bytes 266272 | tf_op jit(solution)/shard_map/ppermute | solution.py:785
  37.4 3.2 collective-permute-done.4.refs_7_
  57.1 4.6 collective-permute-done.7.refs_9_
  63.0 5.6 multiply_sine_fusion
  68.6 4.5 collective-permute-done.9.refs_11_
  73.7 11.1 %shard_map.280 = (bf16[2048,1152]{1,0:T(8,128)(2,1)}, bf16[2048,256]{1,0:T(8,128)(2,1)}, bf16[2048,256]{1,0:T(8,128)(2,1)}, f32[2048,256]{1,0:T(8,128)}, f32[204...) custom-call(s32[9]{0:T(128)} %stack.140.meta_ref, ...), custom_call_target="tpu_custom_call" | custom-call | flops 48318384 | bytes 256491 | tf_op jit(solution)/shard_map/pallas_call | solution.py:84
  98.3 17.5 %shard_map.281 = (bf16[512,256]{1,0:T(8,128)(2,1)}, bf16[512,256]{1,0:T(8,128)(2,1)}, bf16[512,256]{1,0:T(8,128)(2,1)}, bf16[512,256]{1,0:T(8,128)(2,1)}, bf16[2048,2048]{1,0:T(8,128)(2,1)}) custom-call(s32[9]{0:T(128)} %stack.140.meta_ref, bf16[2048,256]{1,0:T(8,128)(2,1)} %get-tuple-element.117.q_ref, bf16[2048,256]{1,0:T(8,128)(2,1)} %get-tuple-element.118.mine_ref, ...), custom_call_target="tpu_custom_call" | custom-call | flops 85899344 | bytes 188743 | tf_op jit(solution)/shard_map/pallas_call | solution.py:84
  117.1 17.8 %all-gather.6.cloned.1.call-done = bf16[576,1728]{1,0:T(8,128)(2,1)} async-done(((bf16[144,1728]{1,0:T(8,128)(2,1)}), bf16[576,1728]{1,0:T(8,128)(2,1)}) %all-gather.6.cloned.1.call-update) | async-done | bytes 1990672 | tf_op jit(solution)/shard_map/all_gather | solution.py:790
  141.9 5.7 collective-permute-done.13.refs_2_
  147.6 6.4 %collective-permute-done.14.refs_3_ = bf16[512,256]{1,0:T(8,128)(2,1)S(1)} collective-permute-done((bf16[512,256]{1,0:T(8,128)(2,1)}, bf16[512,256]{1,0:T(8,128)(2,1)S(1)}, u32[]{:S(2)}, u32[]{:S(2)}) %collective-permute-start.14) | collective-permute-done | bytes 262176 | tf_op jit(solution)/shard_map/ppermute | solution.py:749
  155.1 7.0 %shard_map.282 = (bf16[512,1024]{1,0:T(8,128)(2,1)}, bf16[1024,1152]{1,0:T(8,128)(2,1)}, f32[512,1152]{1,0:T(8,128)}, f32[512,1152]{1,0:T(8,128)}, bf16[512,1152]{1,0:T(8,128)(2,1)}) custom-call(s32[1]{0:T(128)} %bitcast.me_ref, bf16[512,1152]{1,0:T(8,128)(2,1)} %refs_3_.1, bf16[512,256]{1,0:T(8,128)(2,1)} %get-tuple-element.122.refs_0_, ...), custom_call_target="tpu_custom_call" | custom-call | flops 24159192 | bytes 186122 | tf_op jit(solution)/shard_map/pallas_call | solution.py:84
  163.3 17.8 %collective-permute-done.20.refs_4_ = bf16[4,144,1728]{2,1,0:T(8,128)(2,1)S(1)} collective-permute-done((bf16[4,144,1728]{2,1,0:T(8,128)(2,1)}, bf16[4,144,1728]{2,1,0:T(8,128)(2,1)S(1)}, u32[]{:S(2)}, u32[]{:S(2)}) %collective-permute-start.20) | collective-permute-done | bytes 1990688 | tf_op jit(solution)/shard_map/ppermute | solution.py:782
  183.4 11.0 %shard_map.283 = (bf16[2048,1728]{1,0:T(8,128)(2,1)}, bf16[2048,1728]{1,0:T(8,128)(2,1)}, bf16[2048,1728]{1,0:T(8,128)(2,1)}, bf16[1152,1728]{1,0:T(8,128)(2,1)}, bf16[1152,1728]{1,0:T(8,128)(2,1)}) custom-call(s32[1]{0:T(128)} %bitcast.29.meta_ref, bf16[512,1152]{1,0:T(8,128)(2,1)} %copy-done.2, bf16[4,144,1728]{2,1,0:T(8,128)(2,1)} %bitcast.145, ...), custom_call_target="tpu_custom_call" | custom-call | flops 326149088 | bytes 583925 | tf_op jit(solution)/shard_map/pallas_call | solution.py:84
  199.8 16.4 %shard_map.284 = (bf16[2048,1728]{1,0:T(8,128)(2,1)}, bf16[2048,1728]{1,0:T(8,128)(2,1)}, bf16[2048,1728]{1,0:T(8,128)(2,1)}) custom-call(s32[1]{0:T(128)} %bitcast.29.meta_ref, bf16[512,1152]{1,0:T(8,128)(2,1)} %collective-permute-done.18.refs_0_.refs_2_, bf16[512,1152]{1,0:T(8,128)(2,1)} %copy-done.3, ...), custom_call_target="tpu_custom_call", output_to_operand_aliasing={{0}: (5, {}), {1}: (6, {}), {2}: (7, {})} | custom-call | flops 326149088 | bytes 424673 | tf_op jit(solution)/shard_map/pallas_call | solution.py:84
  216.2 13.0 %shard_map.285 = (bf16[512,1152]{1,0:T(8,128)(2,1)}, bf16[512,1152]{1,0:T(8,128)(2,1)}, bf16[512,1152]{1,0:T(8,128)(2,1)}) custom-call(bf16[2048,1728]{1,0:T(8,128)(2,1)} %get-tuple-element.139.x_ref.refs_0_, bf16[1728,1152]{1,0:T(8,128)(2,1)} %all-gather.8.cloned.1.call-done.w_ref.down_ref.refs_4_), custom_call_target="tpu_custom_call" | custom-call | flops 122305904 | bytes 70778 | tf_op jit(solution)/shard_map/pallas_call | solution.py:84
  235.5 13.8 %shard_map.286 = (bf16[2048,1728]{1,0:T(8,128)(2,1)}, bf16[2048,1728]{1,0:T(8,128)(2,1)}, bf16[2048,1728]{1,0:T(8,128)(2,1)}, bf16[512,1152]{1,0:T(8,128)(2,1)}) custom-call(bf16[512,1152]{1,0:T(8,128)(2,1)} %get-tuple-element.169.x_ref.refs_0_, ...), custom_call_target="tpu_custom_call", output_to_operand_aliasing={{0}: (4, {}), {1}: (5, {}), {2}: (6, {})} | custom-call | flops 122305904 | bytes 448266 | tf_op jit(solution)/shard_map/pallas_call | solution.py:84
  249.3 12.3 %collective-permute-done.25.refs_2_ = bf16[512,1152]{1,0:T(8,128)(2,1)} collective-permute-done((bf16[512,1152]{1,0:T(8,128)(2,1)S(1)}, bf16[512,1152]{1,0:T(8,128)(2,1)}, u32[]{:S(2)}, u32[]{:S(2)}) %collective-permute-start.25) | collective-permute-done | bytes 1179680 | tf_op jit(solution)/shard_map/ppermute | solution.py:749
  261.6 5.3 shard_map.287
  271.8 26.4 %shard_map.288 = (bf16[1024,1728]{1,0:T(8,128)(2,1)}, bf16[1024,1728]{1,0:T(8,128)(2,1)}, bf16[512,1152]{1,0:T(8,128)(2,1)}, bf16[512,1152]{1,0:T(8,128)(2,1)}) custom-call(bf16[512,1152]{1,0:T(8,128)(2,1)} %get-tuple-element.151.refs_0_.refs_1_, bf16[512,1152]{1,0:T(8,128)(2,1)} %copy-done.6, bf16[2048,1728]{1,0:T(8,128)(2,1)} %get-tuple-element.152.refs_2_, ...), custom_call_target="tpu_custom_call" | custom-call | flops 244611808 | bytes 188743 | tf_op jit(solution)/shard_map/pallas_call | solution.py:84
  302.2 16.0 %shard_map.289 = (bf16[4,216,1152]{2,1,0:T(8,128)(2,1)}, bf16[4,216,1152]{2,1,0:T(8,128)(2,1)}) custom-call(s32[1]{0:T(128)} %bitcast.29.meta_ref, bf16[2048,1728]{1,0:T(8,128)(2,1)} %get-tuple-element.155.refs_0_, bf16[512,1152]{1,0:T(8,128)(2,1)} %get-tuple-element.151.refs_0_.refs_1_, bf16[512,1152]{1,0:T(8,128)(2,1)} %copy-done.6, ...), custom_call_target="tpu_custom_call" | custom-call | flops 163074544 | bytes 79626 | tf_op jit(solution)/shard_map/pallas_call | solution.py:84
  319.5 26.5 %shard_map.290 = (bf16[1024,1728]{1,0:T(8,128)(2,1)}, bf16[1024,1728]{1,0:T(8,128)(2,1)}, bf16[512,1152]{1,0:T(8,128)(2,1)}, bf16[512,1152]{1,0:T(8,128)(2,1)}) custom-call(bf16[512,1152]{1,0:T(8,128)(2,1)} %copy-done.5, bf16[512,1152]{1,0:T(8,128)(2,1)} %copy-done.7, bf16[2048,1728]{1,0:T(8,128)(2,1)} %get-tuple-element.152.refs_2_, ...), custom_call_target="tpu_custom_call" | custom-call | flops 244611808 | bytes 188743 | tf_op jit(solution)/shard_map/pallas_call | solution.py:84
  346.8 3.4 collective-permute-done.29.refs_1_
  353.8 15.4 %shard_map.292 = (bf16[4,144,1728]{2,1,0:T(8,128)(2,1)}, bf16[4,144,1728]{2,1,0:T(8,128)(2,1)}) custom-call(s32[1]{0:T(128)} %bitcast.29.meta_ref, bf16[512,1152]{1,0:T(8,128)(2,1)} %get-tuple-element.169.x_ref.refs_0_, bf16[512,1152]{1,0:T(8,128)(2,1)} %copy-done.2, bf16[512,1152]{1,0:T(8,128)(2,1)} %collective-permute-done.18.refs_0_.refs_2_, ...), custom_call_target="tpu_custom_call" | custom-call | flops 163074544 | bytes 79626 | tf_op jit(solution)/shard_map/pallas_call | solution.py:84
  369.2 3.3 shard_map.293
  374.0 15.4 %shard_map.294 = (bf16[4,144,1728]{2,1,0:T(8,128)(2,1)}, bf16[4,144,1728]{2,1,0:T(8,128)(2,1)}) custom-call(s32[1]{0:T(128)} %bitcast.29.meta_ref, bf16[512,1152]{1,0:T(8,128)(2,1)} %get-tuple-element.169.x_ref.refs_0_, bf16[512,1152]{1,0:T(8,128)(2,1)} %copy-done.2, bf16[512,1152]{1,0:T(8,128)(2,1)} %collective-permute-done.18.refs_0_.refs_2_, ...), custom_call_target="tpu_custom_call" | custom-call | flops 163074544 | bytes 79626 | tf_op jit(solution)/shard_map/pallas_call | solution.py:84
  390.6 9.4 %collective-permute-done.32.c_ref = bf16[512,1152]{1,0:T(8,128)(2,1)} collective-permute-done((bf16[512,1152]{1,0:T(8,128)(2,1)}, bf16[512,1152]{1,0:T(8,128)(2,1)}, u32[]{:S(2)}, u32[]{:S(2)}) %collective-permute-start.32) | collective-permute-done | bytes 1179680 | tf_op jit(solution)/shard_map/ppermute | solution.py:749
  400.0 8.8 %shard_map.295 = (f32[512,1152]{1,0:T(8,128)}, bf16[512,1152]{1,0:T(8,128)(2,1)}, bf16[512,256]{1,0:T(8,128)(2,1)}, bf16[512,256]{1,0:T(8,128)(2,1)}, bf16[512,2...) custom-call(s32[1]{0:T(128)} %bitcast.me_ref, bf16[512,1152]{1,0:T(8,128)(2,1)} %get-tuple-element.173.a_ref, ...), custom_call_target="tpu_custom_call" | custom-call | flops 24159192 | bytes 91842 | tf_op jit(solution)/shard_map/pallas_call | solution.py:84
  412.1 6.5 %collective-permute-done.34.refs_2_ = bf16[512,256]{1,0:T(8,128)(2,1)S(1)} collective-permute-done((bf16[512,256]{1,0:T(8,128)(2,1)}, bf16[512,256]{1,0:T(8,128)(2,1)S(1)}, u32[]{:S(2)}, u32[]{:S(2)}) %collective-permute-start.34) | collective-permute-done | bytes 262176 | tf_op jit(solution)/shard_map/ppermute | solution.py:749
  418.6 6.0 %collective-permute-done.35.refs_3_ = bf16[512,256]{1,0:T(8,128)(2,1)S(1)} collective-permute-done((bf16[512,256]{1,0:T(8,128)(2,1)}, bf16[512,256]{1,0:T(8,128)(2,1)S(1)}, u32[]{:S(2)}, u32[]{:S(2)}) %collective-permute-start.35) | collective-permute-done | bytes 262176 | tf_op jit(solution)/shard_map/ppermute | solution.py:749
  424.5 3.5 shard_map.296
  428.1 17.2 %shard_map.297 = (f32[2048,256]{1,0:T(8,128)}, f32[2048,256]{1,0:T(8,128)}, bf16[2048,256]{1,0:T(8,128)(2,1)}) custom-call(s32[9]{0:T(128)} %stack.140.meta_ref, bf16[2048,256]{1,0:T(8,128)(2,1)} %get-tuple-element.117.q_ref, bf16[2048,256]{1,0:T(8,128)(2,1)} %get-tuple-element.118.mine_ref, bf16[2048,256]{1,0:T(8,128)(2,1)} %copy-done.11, ...), custom_call_target="tpu_custom_call" | custom-call | flops 171798688 | bytes 104857 | tf_op jit(solution)/shard_map/pallas_call | solution.py:84
  445.5 2.9 collective-permute-done.37.refs_2_
  448.4 11.7 %shard_map.298 = (bf16[2048,512]{1,0:T(8,128)(2,1)}, f32[1,256]{1,0:T(1,128)}, f32[1,256]{1,0:T(1,128)}, bf16[512,1152]{1,0:T(8,128)(2,1)}, bf16[512,1152]{1,0:T...) custom-call(s32[1]{0:T(128)} %bitcast.1.core_ref, f32[2048,256]{1,0:T(8,128)} %get-tuple-element.183.refs_0_, ...), custom_call_target="tpu_custom_call" | custom-call | flops 48318384 | bytes 136355 | tf_op jit(solution)/shard_map/pallas_call | solution.py:84
  460.2 3.1 collective-permute-done.41.refs_1_
  464.6 3.3 shard_map.300
  468.0 3.1 convolution_convert_fusion
  479.4 6.8 %shard_map.301 = (bf16[4,144,512]{2,1,0:T(8,128)(2,1)}, bf16[4,144,512]{2,1,0:T(8,128)(2,1)}) custom-call(s32[1]{0:T(128)} %bitcast.29.meta_ref, bf16[2048,1152]{1,0:T(8,128)(2,1)} %get-tuple-element.203.refs_0_, bf16[2048,512]{1,0:T(8,128)(2,1)} %get-tuple-element.200.refs_1_), custom_call_target="tpu_custom_call" | custom-call | flops 48318384 | bytes 23592 | tf_op jit(solution)/shard_map/pallas_call | solution.py:84
  486.3 4.6 collective-permute-done.44
  497.9 7.3 %collective-permute-done.53 = bf16[216,1152]{1,0:T(8,128)(2,1)} collective-permute-done((bf16[216,1152]{1,0:T(8,128)(2,1)}, bf16[216,1152]{1,0:T(8,128)(2,1)}, u32[]{:S(2)}, u32[]{:S(2)}) %collective-permute-start.53) | collective-permute-done | bytes 497696 | tf_op jit(solution)/shard_map/ppermute | solution.py:749
  505.3 3.9 collective-permute-start.54
  516.3 3.9 collective-permute-start.49
  533.0 5.5 shard_map.303
  538.5 3.0 collective-permute-done.40.refs_2_
  542.6 5.5 shard_map.299
  563.4 4.2 collective-permute-start.57
  567.7 6.8 %collective-permute-done.59.refs_2_ = bf16[144,1728]{1,0:T(8,128)(2,1)S(1)} collective-permute-done((bf16[144,1728]{1,0:T(8,128)(2,1)S(1)}, bf16[144,1728]{1,0:T(8,128)(2,1)S(1)}, u32[]{:S(2)}, u32[]{:S(2)}) %collective-permute-start.59) | collective-permute-done | bytes 497696 | tf_op jit(solution)/shard_map/ppermute | solution.py:749
  583.2 5.5 shard_map.304
  (324 shorter events, 149.3 us)
Async XLA Ops:
  7.2 83.6 %all-gather.4.cloned.1.call-start = ((), (), s32[]{:S(2)}) async-start(), calls=%async_computation.3 | async-start | bytes 2580480 | tf_op jit(solution)/shard_map/all_gather | solution.py:790
  13.0 27.6 %collective-permute-start.1 = (bf16[512,1152]{1,0:T(8,128)(2,1)}, bf16[512,1152]{1,0:T(8,128)(2,1)S(1)}, u32[]{:S(2)}, u32[]{:S(2)}) collective-permute-start(bf16[512,1152]{1,0:T(8,128)(2,1)} %refs_3_.1), channel_id=1, source_target_pairs={{0,2},{1,3},{2,0},{3,1},{4,6},{5,7},{6,4},{7,5},{8,10},{9,11},{10,... | collective-permute-start | bytes 3538952 | tf_op jit(solution)/shard_map/ppermute | solution.py:749
  15.6 21.9 %collective-permute-start.3 = (bf16[208,640]{1,0:T(8,128)(2,1)S(1)}, bf16[208,640]{1,0:T(8,128)(2,1)S(1)}, u32[]{:S(2)}, u32[]{:S(2)}) collective-permute-start(bf16[208,640]{1,0:T(8,128)(2,1)S(1)} %fusion.9.refs_4_), channel_id=1, source_target_pairs={{0,16},{4,20},{8,24},{12,28},{16,0},{20,4},{24,8},{28,12},{1,17},{... | collective-permute-start | bytes 798728 | tf_op jit(solution)/shard_map/ppermute | solution.py:785
  16.6 24.0 %collective-permute-start.4 = (bf16[208,640]{1,0:T(8,128)(2,1)S(1)}, bf16[208,640]{1,0:T(8,128)(2,1)S(1)}, u32[]{:S(2)}, u32[]{:S(2)}) collective-permute-start(bf16[208,640]{1,0:T(8,128)(2,1)S(1)} %fusion.9.refs_4_), channel_id=1, source_target_pairs={{0,24},{4,28},{8,0},{12,4},{16,8},{20,12},{24,16},{28,20},{1,25},{... | collective-permute-start | bytes 798728 | tf_op jit(solution)/shard_map/ppermute | solution.py:785
  44.1 90.8 %all-gather.6.cloned.1.call-start = ((), (), s32[]{:S(2)}) async-start(), calls=%async_computation.4 | async-start | bytes 2580480 | tf_op jit(solution)/shard_map/all_gather | solution.py:790
  47.2 169.0 %all-gather.8.cloned.1.call-start = ((), (), s32[]{:S(2)}) async-start(), calls=%async_computation.5 | async-start | bytes 4976640 | tf_op jit(solution)/shard_map/all_gather | solution.py:790
  47.3 25.8 %collective-permute-start = (bf16[512,1152]{1,0:T(8,128)(2,1)S(1)}, bf16[512,1152]{1,0:T(8,128)(2,1)}, u32[]{:S(2)}, u32[]{:S(2)}) collective-permute-start(bf16[512,1152]{1,0:T(8,128)(2,1)S(1)} %copy-done.4), channel_id=1, source_target_pairs={{0,1},{1,0},{2,3},{3,2},{4,5},{5,4},{6,7},{7,6},{8,9},{9,8},{10,11... | collective-permute-start | bytes 3538952 | tf_op jit(solution)/shard_map/ppermute | solution.py:749
  48.3 24.8 %collective-permute-start.5 = (bf16[512,1152]{1,0:T(8,128)(2,1)S(1)}, bf16[512,1152]{1,0:T(8,128)(2,1)}, u32[]{:S(2)}, u32[]{:S(2)}) collective-permute-start(bf16[512,1152]{1,0:T(8,128)(2,1)S(1)} %collective-permute-done.1.refs_2_), channel_id=1, source_target_pairs={{0,1},{1,0},{2,3},{3,2},{4,5},{5,4},{6,7},{7,6},{8,9},{9,8},{10,11... | collective-permute-start | bytes 3538952 | tf_op jit(solution)/shard_map/ppermute | solution.py:749
  49.7 12.0 %collective-permute-start.7 = (bf16[208,640]{1,0:T(8,128)(2,1)}, bf16[208,640]{1,0:T(8,128)(2,1)}, u32[]{:S(2)}, u32[]{:S(2)}) collective-permute-start(bf16[208,640]{1,0:T(8,128)(2,1)} %copy-done.34), channel_id=1, source_target_pairs={{0,4},{4,0},{8,12},{12,8},{16,20},{20,16},{24,28},{28,24},{1,5},{5... | collective-permute-start | bytes 798728 | tf_op jit(solution)/shard_map/ppermute | solution.py:782
  50.7 17.9 %collective-permute-start.8 = (bf16[208,640]{1,0:T(8,128)(2,1)}, bf16[208,640]{1,0:T(8,128)(2,1)S(1)}, u32[]{:S(2)}, u32[]{:S(2)}) collective-permute-start(bf16[208,640]{1,0:T(8,128)(2,1)} %copy-done.35), channel_id=1, source_target_pairs={{0,4},{4,0},{8,12},{12,8},{16,20},{20,16},{24,28},{28,24},{1,5},{5... | collective-permute-start | bytes 798728 | tf_op jit(solution)/shard_map/ppermute | solution.py:782
  55.9 17.1 %collective-permute-start.9 = (bf16[208,640]{1,0:T(8,128)(2,1)}, bf16[208,640]{1,0:T(8,128)(2,1)S(1)}, u32[]{:S(2)}, u32[]{:S(2)}) collective-permute-start(bf16[208,640]{1,0:T(8,128)(2,1)} %copy-done.36), channel_id=1, source_target_pairs={{0,4},{4,0},{8,12},{12,8},{16,20},{20,16},{24,28},{28,24},{1,5},{5... | collective-permute-start | bytes 798728 | tf_op jit(solution)/shard_map/ppermute | solution.py:782
  61.7 23.1 %collective-permute-start.22 = (bf16[216,1152]{1,0:T(8,128)(2,1)S(1)}, bf16[216,1152]{1,0:T(8,128)(2,1)S(1)}, u32[]{:S(2)}, u32[]{:S(2)}) collective-permute-start(bf16[216,1152]{1,0:T(8,128)(2,1)S(1)} %dynamic-slice_convert_fusion), channel_id=1, source_target_pairs={{0,4},{4,0},{8,12},{12,8},{16,20},{20,16},{24,28},{28,24},{1,5},{5... | collective-permute-start | bytes 1493000 | tf_op jit(solution)/shard_map/ppermute | solution.py:782
  88.2 357.3 %reduce-scatter.10.cloned.1.call-start = ((), (), s32[]{:S(2)}) async-start(), calls=%async_computation.8 | async-start | bytes 2488320
  90.8 50.3 %collective-permute-start.11 = (bf16[4,144,1728]{2,1,0:T(8,128)(2,1)}, bf16[4,144,1728]{2,1,0:T(8,128)(2,1)}, u32[]{:S(2)}, u32[]{:S(2)}) collective-permute-start(bf16[4,144,1728]{2,1,0:T(8,128)(2,1)} %bitcast.144), channel_id=1, source_target_pairs={{0,4},{4,0},{8,12},{12,8},{16,20},{20,16},{24,28},{28,24},{1,5},{5... | collective-permute-start | bytes 5971976 | tf_op jit(solution)/shard_map/ppermute | solution.py:782
  115.8 21.5 %collective-permute-start.16 = (bf16[256,1152]{1,0:T(8,128)(2,1)S(1)}, bf16[256,1152]{1,0:T(8,128)(2,1)S(1)}, u32[]{:S(2)}, u32[]{:S(2)}) collective-permute-start(bf16[256,1152]{1,0:T(8,128)(2,1)S(1)} %copy-done.24), channel_id=1, source_target_pairs={{0,2},{1,3},{2,0},{3,1},{4,6},{5,7},{6,4},{7,5},{8,10},{9,11},{10,... | collective-permute-start | bytes 1769480 | tf_op jit(solution)/shard_map/ppermute | solution.py:749
  134.9 46.2 %collective-permute-start.20 = (bf16[4,144,1728]{2,1,0:T(8,128)(2,1)}, bf16[4,144,1728]{2,1,0:T(8,128)(2,1)S(1)}, u32[]{:S(2)}, u32[]{:S(2)}) collective-permute-start(bf16[4,144,1728]{2,1,0:T(8,128)(2,1)} %bitcast.146), channel_id=1, source_target_pairs={{0,4},{4,0},{8,12},{12,8},{16,20},{20,16},{24,28},{28,24},{1,5},{5... | collective-permute-start | bytes 5971976 | tf_op jit(solution)/shard_map/ppermute | solution.py:782
  136.1 17.9 %collective-permute-start.15 = (bf16[256,1152]{1,0:T(8,128)(2,1)S(1)}, bf16[256,1152]{1,0:T(8,128)(2,1)S(1)}, u32[]{:S(2)}, u32[]{:S(2)}) collective-permute-start(bf16[256,1152]{1,0:T(8,128)(2,1)S(1)} %copy-done.24), channel_id=1, source_target_pairs={{0,1},{1,0},{2,3},{3,2},{4,5},{5,4},{6,7},{7,6},{8,9},{9,8},{10,11... | collective-permute-start | bytes 1769480 | tf_op jit(solution)/shard_map/ppermute | solution.py:749
  137.3 16.8 %collective-permute-start.17 = (bf16[256,1152]{1,0:T(8,128)(2,1)S(1)}, bf16[256,1152]{1,0:T(8,128)(2,1)S(1)}, u32[]{:S(2)}, u32[]{:S(2)}) collective-permute-start(bf16[256,1152]{1,0:T(8,128)(2,1)S(1)} %collective-permute-done.16.refs_6_), channel_id=1, source_target_pairs={{0,1},{1,0},{2,3},{3,2},{4,5},{5,4},{6,7},{7,6},{8,9},{9,8},{10,11... | collective-permute-start | bytes 1769480 | tf_op jit(solution)/shard_map/ppermute | solution.py:749
  141.1 13.0 %collective-permute-start.14 = (bf16[512,256]{1,0:T(8,128)(2,1)}, bf16[512,256]{1,0:T(8,128)(2,1)S(1)}, u32[]{:S(2)}, u32[]{:S(2)}) collective-permute-start(bf16[512,256]{1,0:T(8,128)(2,1)} %get-tuple-element.125), channel_id=1, source_target_pairs={{0,3},{1,2},{2,1},{3,0},{4,7},{5,6},{6,5},{7,4},{8,11},{9,10},{10,... | collective-permute-start | bytes 786440 | tf_op jit(solution)/shard_map/ppermute | solution.py:749
  162.1 18.9 %collective-permute-start.19 = (bf16[512,1152]{1,0:T(8,128)(2,1)}, bf16[512,1152]{1,0:T(8,128)(2,1)S(1)}, u32[]{:S(2)}, u32[]{:S(2)}) collective-permute-start(bf16[512,1152]{1,0:T(8,128)(2,1)} %get-tuple-element.169.x_ref.refs_0_), channel_id=1, source_target_pairs={{0,1},{1,0},{2,3},{3,2},{4,5},{5,4},{6,7},{7,6},{8,9},{9,8},{10,11... | collective-permute-start | bytes 3538952 | tf_op jit(solution)/shard_map/ppermute | solution.py:749
  162.1 32.3 %collective-permute-start.18 = (bf16[512,1152]{1,0:T(8,128)(2,1)}, bf16[512,1152]{1,0:T(8,128)(2,1)}, u32[]{:S(2)}, u32[]{:S(2)}) collective-permute-start(bf16[512,1152]{1,0:T(8,128)(2,1)} %get-tuple-element.169.x_ref.refs_0_), channel_id=1, source_target_pairs={{0,2},{1,3},{2,0},{3,1},{4,6},{5,7},{6,4},{7,5},{8,10},{9,11},{10,... | collective-permute-start | bytes 3538952 | tf_op jit(solution)/shard_map/ppermute | solution.py:749
  234.2 27.4 %collective-permute-start.25 = (bf16[512,1152]{1,0:T(8,128)(2,1)S(1)}, bf16[512,1152]{1,0:T(8,128)(2,1)}, u32[]{:S(2)}, u32[]{:S(2)}) collective-permute-start(bf16[512,1152]{1,0:T(8,128)(2,1)S(1)} %add_convert_fusion.1), channel_id=1, source_target_pairs={{0,2},{1,3},{2,0},{3,1},{4,6},{5,7},{6,4},{7,5},{8,10},{9,11},{10,... | collective-permute-start | bytes 3538952 | tf_op jit(solution)/shard_map/ppermute | solution.py:749
  268.1 30.2 %collective-permute-start.27 = (bf16[512,1152]{1,0:T(8,128)(2,1)}, bf16[512,1152]{1,0:T(8,128)(2,1)S(1)}, u32[]{:S(2)}, u32[]{:S(2)}) collective-permute-start(bf16[512,1152]{1,0:T(8,128)(2,1)} %get-tuple-element.151.refs_0_.refs_1_), channel_id=1, source_target_pairs={{0,2},{1,3},{2,0},{3,1},{4,6},{5,7},{6,4},{7,5},{8,10},{9,11},{10,... | collective-permute-start | bytes 3538952 | tf_op jit(solution)/shard_map/ppermute | solution.py:749
  318.2 51.0 %collective-permute-start.31 = (bf16[4,216,1152]{2,1,0:T(8,128)(2,1)}, bf16[4,216,1152]{2,1,0:T(8,128)(2,1)}, u32[]{:S(2)}, u32[]{:S(2)}) collective-permute-start(bf16[4,216,1152]{2,1,0:T(8,128)(2,1)} %get-tuple-element.158), channel_id=1, source_target_pairs={{0,4},{4,0},{8,12},{12,8},{16,20},{20,16},{24,28},{28,24},{1,5},{5... | collective-permute-start | bytes 5971976 | tf_op jit(solution)/shard_map/ppermute | solution.py:782
  372.5 124.9 %reduce-scatter.6.cloned.1.call-start = ((), (), s32[]{:S(2)}) async-start(), calls=%async_computation.6 | async-start | bytes 2580480 | tf_op jit(solution)/shard_map/reduce_scatter | solution.py:835
  372.5 52.0 %collective-permute-start.36 = (bf16[4,144,1728]{2,1,0:T(8,128)(2,1)}, bf16[4,144,1728]{2,1,0:T(8,128)(2,1)}, u32[]{:S(2)}, u32[]{:S(2)}) collective-permute-start(bf16[4,144,1728]{2,1,0:T(8,128)(2,1)} %get-tuple-element.167), channel_id=1, source_target_pairs={{0,4},{4,0},{8,12},{12,8},{16,20},{20,16},{24,28},{28,24},{1,5},{5... | collective-permute-start | bytes 5971976 | tf_op jit(solution)/shard_map/ppermute | solution.py:782
  372.8 27.2 %collective-permute-start.32 = (bf16[512,1152]{1,0:T(8,128)(2,1)}, bf16[512,1152]{1,0:T(8,128)(2,1)}, u32[]{:S(2)}, u32[]{:S(2)}) collective-permute-start(bf16[512,1152]{1,0:T(8,128)(2,1)} %shard_map.291), channel_id=1, source_target_pairs={{0,2},{1,3},{2,0},{3,1},{4,6},{5,7},{6,4},{7,5},{8,10},{9,11},{10,... | collective-permute-start | bytes 3538952 | tf_op jit(solution)/shard_map/ppermute | solution.py:749
  389.4 73.9 %collective-permute-start.41 = (bf16[4,144,1728]{2,1,0:T(8,128)(2,1)}, bf16[4,144,1728]{2,1,0:T(8,128)(2,1)S(1)}, u32[]{:S(2)}, u32[]{:S(2)}) collective-permute-start(bf16[4,144,1728]{2,1,0:T(8,128)(2,1)} %get-tuple-element.172), channel_id=1, source_target_pairs={{0,4},{4,0},{8,12},{12,8},{16,20},{20,16},{24,28},{28,24},{1,5},{5... | collective-permute-start | bytes 5971976 | tf_op jit(solution)/shard_map/ppermute | solution.py:782
  411.6 12.9 %collective-permute-start.35 = (bf16[512,256]{1,0:T(8,128)(2,1)}, bf16[512,256]{1,0:T(8,128)(2,1)S(1)}, u32[]{:S(2)}, u32[]{:S(2)}) collective-permute-start(bf16[512,256]{1,0:T(8,128)(2,1)} %get-tuple-element.180), channel_id=1, source_target_pairs={{0,3},{1,2},{2,1},{3,0},{4,7},{5,6},{6,5},{7,4},{8,11},{9,10},{10,... | collective-permute-start | bytes 786440 | tf_op jit(solution)/shard_map/ppermute | solution.py:749
  428.1 127.0 %reduce-scatter.8.cloned.1.call-start = ((), (), s32[]{:S(2)}) async-start(), calls=%async_computation.7 | async-start | bytes 2580480 | tf_op jit(solution)/shard_map/reduce_scatter | solution.py:835
  476.1 14.8 %collective-permute-start.44 = (bf16[8,32,1152]{2,1,0:T(8,128)(2,1)}, bf16[8,32,1152]{2,1,0:T(8,128)(2,1)}, u32[]{:S(2)}, u32[]{:S(2)}) collective-permute-start(bf16[8,32,1152]{2,1,0:T(8,128)(2,1)} %get-tuple-element.238), channel_id=1, source_target_pairs={{0,2},{1,3},{2,0},{3,1},{4,6},{5,7},{6,4},{7,5},{8,10},{9,11},{10,... | collective-permute-start | bytes 1769480 | tf_op jit(solution)/shard_map/ppermute | solution.py:749
  477.9 19.8 %collective-permute-start.39 = (bf16[512,1152]{1,0:T(8,128)(2,1)}, bf16[512,1152]{1,0:T(8,128)(2,1)S(1)}, u32[]{:S(2)}, u32[]{:S(2)}) collective-permute-start(bf16[512,1152]{1,0:T(8,128)(2,1)} %get-tuple-element.194), channel_id=1, source_target_pairs={{0,1},{1,0},{2,3},{3,2},{4,5},{5,4},{6,7},{7,6},{8,9},{9,8},{10,11... | collective-permute-start | bytes 3538952 | tf_op jit(solution)/shard_map/ppermute | solution.py:749
  493.3 11.9 %collective-permute-start.53 = (bf16[216,1152]{1,0:T(8,128)(2,1)}, bf16[216,1152]{1,0:T(8,128)(2,1)}, u32[]{:S(2)}, u32[]{:S(2)}) collective-permute-start(bf16[216,1152]{1,0:T(8,128)(2,1)} %reduce-scatter.10.cloned.1.call-done), channel_id=1, source_target_pairs={{0,2},{1,3},{2,0},{3,1},{4,6},{5,7},{6,4},{7,5},{8,10},{9,11},{10,... | collective-permute-start | bytes 1493000 | tf_op jit(solution)/shard_map/ppermute | solution.py:749
  494.5 44.0 %collective-permute-start.38 = (bf16[512,1152]{1,0:T(8,128)(2,1)}, bf16[512,1152]{1,0:T(8,128)(2,1)}, u32[]{:S(2)}, u32[]{:S(2)}) collective-permute-start(bf16[512,1152]{1,0:T(8,128)(2,1)} %get-tuple-element.192), channel_id=1, source_target_pairs={{0,1},{1,0},{2,3},{3,2},{4,5},{5,4},{6,7},{7,6},{8,9},{9,8},{10,11... | collective-permute-start | bytes 3538952 | tf_op jit(solution)/shard_map/ppermute | solution.py:749
  497.4 13.1 %collective-permute-start.52 = (bf16[216,1152]{1,0:T(8,128)(2,1)}, bf16[216,1152]{1,0:T(8,128)(2,1)}, u32[]{:S(2)}, u32[]{:S(2)}) collective-permute-start(bf16[216,1152]{1,0:T(8,128)(2,1)} %reduce-scatter.10.cloned.1.call-done), channel_id=1, source_target_pairs={{0,1},{1,0},{2,3},{3,2},{4,5},{5,4},{6,7},{7,6},{8,9},{9,8},{10,11... | collective-permute-start | bytes 1493000 | tf_op jit(solution)/shard_map/ppermute | solution.py:749
  497.4 25.0 %collective-permute-start.45 = (bf16[4,208,640]{2,1,0:T(8,128)(2,1)}, bf16[4,208,640]{2,1,0:T(8,128)(2,1)}, u32[]{:S(2)}, u32[]{:S(2)}) collective-permute-start(bf16[4,208,640]{2,1,0:T(8,128)(2,1)} %fusion.5), channel_id=1, source_target_pairs={{0,4},{4,0},{8,12},{12,8},{16,20},{20,16},{24,28},{28,24},{1,5},{5... | collective-permute-start | bytes 3194888 | tf_op jit(solution)/shard_map/ppermute | solution.py:782
  497.7 18.7 %collective-permute-start.50 = (bf16[144,1728]{1,0:T(8,128)(2,1)}, bf16[144,1728]{1,0:T(8,128)(2,1)}, u32[]{:S(2)}, u32[]{:S(2)}) collective-permute-start(bf16[144,1728]{1,0:T(8,128)(2,1)} %reduce-scatter.6.cloned.1.call-done.refs_0_), channel_id=1, source_target_pairs={{0,2},{1,3},{2,0},{3,1},{4,6},{5,7},{6,4},{7,5},{8,10},{9,11},{10,... | collective-permute-start | bytes 1493000 | tf_op jit(solution)/shard_map/ppermute | solution.py:749
  505.3 14.9 %collective-permute-start.54 = (bf16[216,1152]{1,0:T(8,128)(2,1)}, bf16[216,1152]{1,0:T(8,128)(2,1)S(1)}, u32[]{:S(2)}, u32[]{:S(2)}) collective-permute-start(bf16[216,1152]{1,0:T(8,128)(2,1)} %collective-permute-done.53), channel_id=1, source_target_pairs={{0,1},{1,0},{2,3},{3,2},{4,5},{5,4},{6,7},{7,6},{8,9},{9,8},{10,11... | collective-permute-start | bytes 1493000 | tf_op jit(solution)/shard_map/ppermute | solution.py:749
  510.5 31.1 %collective-permute-start.40 = (bf16[512,1152]{1,0:T(8,128)(2,1)}, bf16[512,1152]{1,0:T(8,128)(2,1)S(1)}, u32[]{:S(2)}, u32[]{:S(2)}) collective-permute-start(bf16[512,1152]{1,0:T(8,128)(2,1)} %add_convert_fusion), channel_id=1, source_target_pairs={{0,2},{1,3},{2,0},{3,1},{4,6},{5,7},{6,4},{7,5},{8,10},{9,11},{10,... | collective-permute-start | bytes 3538952 | tf_op jit(solution)/shard_map/ppermute | solution.py:749
  516.3 12.2 %collective-permute-start.49 = (bf16[144,1728]{1,0:T(8,128)(2,1)S(1)}, bf16[144,1728]{1,0:T(8,128)(2,1)}, u32[]{:S(2)}, u32[]{:S(2)}) collective-permute-start(bf16[144,1728]{1,0:T(8,128)(2,1)S(1)} %copy-done.12), channel_id=1, source_target_pairs={{0,1},{1,0},{2,3},{3,2},{4,5},{5,4},{6,7},{7,6},{8,9},{9,8},{10,11... | collective-permute-start | bytes 1493000 | tf_op jit(solution)/shard_map/ppermute | solution.py:749
  520.2 10.6 %collective-permute-start.51 = (bf16[144,1728]{1,0:T(8,128)(2,1)}, bf16[144,1728]{1,0:T(8,128)(2,1)}, u32[]{:S(2)}, u32[]{:S(2)}) collective-permute-start(bf16[144,1728]{1,0:T(8,128)(2,1)} %collective-permute-done.50.refs_2_), channel_id=1, source_target_pairs={{0,1},{1,0},{2,3},{3,2},{4,5},{5,4},{6,7},{7,6},{8,9},{9,8},{10,11... | collective-permute-start | bytes 1493000 | tf_op jit(solution)/shard_map/ppermute | solution.py:749
  527.1 21.0 %collective-permute-start.46 = (bf16[208,640]{1,0:T(8,128)(2,1)}, bf16[208,640]{1,0:T(8,128)(2,1)}, u32[]{:S(2)}, u32[]{:S(2)}) collective-permute-start(bf16[208,640]{1,0:T(8,128)(2,1)} %get-tuple-element.255), channel_id=1, source_target_pairs={{0,8},{4,12},{8,16},{12,20},{16,24},{20,28},{24,0},{28,4},{1,9},{5... | collective-permute-start | bytes 798728 | tf_op jit(solution)/shard_map/ppermute | solution.py:785
  528.5 21.8 %collective-permute-start.47 = (bf16[208,640]{1,0:T(8,128)(2,1)}, bf16[208,640]{1,0:T(8,128)(2,1)S(1)}, u32[]{:S(2)}, u32[]{:S(2)}) collective-permute-start(bf16[208,640]{1,0:T(8,128)(2,1)} %get-tuple-element.257), channel_id=1, source_target_pairs={{0,16},{4,20},{8,24},{12,28},{16,0},{20,4},{24,8},{28,12},{1,17},{... | collective-permute-start | bytes 798728 | tf_op jit(solution)/shard_map/ppermute | solution.py:785
  530.8 22.6 %collective-permute-start.48 = (bf16[208,640]{1,0:T(8,128)(2,1)}, bf16[208,640]{1,0:T(8,128)(2,1)}, u32[]{:S(2)}, u32[]{:S(2)}) collective-permute-start(bf16[208,640]{1,0:T(8,128)(2,1)} %get-tuple-element.256), channel_id=1, source_target_pairs={{0,24},{4,28},{8,0},{12,4},{16,8},{20,12},{24,16},{28,20},{1,25},{... | collective-permute-start | bytes 798728 | tf_op jit(solution)/shard_map/ppermute | solution.py:785
  557.9 9.7 %collective-permute-start.55 = (bf16[208,640]{1,0:T(8,128)(2,1)S(1)}, bf16[208,640]{1,0:T(8,128)(2,1)S(1)}, u32[]{:S(2)}, u32[]{:S(2)}) collective-permute-start(bf16[208,640]{1,0:T(8,128)(2,1)S(1)} %get-tuple-element.271), channel_id=1, source_target_pairs={{0,1},{1,0},{2,3},{3,2},{4,5},{5,4},{6,7},{7,6},{8,9},{9,8},{10,11... | collective-permute-start | bytes 798728 | tf_op jit(solution)/shard_map/ppermute | solution.py:749
  559.6 14.9 %collective-permute-start.59 = (bf16[144,1728]{1,0:T(8,128)(2,1)S(1)}, bf16[144,1728]{1,0:T(8,128)(2,1)S(1)}, u32[]{:S(2)}, u32[]{:S(2)}) collective-permute-start(bf16[144,1728]{1,0:T(8,128)(2,1)S(1)} %copy-done.14), channel_id=1, source_target_pairs={{0,2},{1,3},{2,0},{3,1},{4,6},{5,7},{6,4},{7,5},{8,10},{9,11},{10,... | collective-permute-start | bytes 1493000 | tf_op jit(solution)/shard_map/ppermute | solution.py:749
  560.3 21.3 %collective-permute-start.58 = (bf16[144,1728]{1,0:T(8,128)(2,1)S(1)}, bf16[144,1728]{1,0:T(8,128)(2,1)S(1)}, u32[]{:S(2)}, u32[]{:S(2)}) collective-permute-start(bf16[144,1728]{1,0:T(8,128)(2,1)S(1)} %copy-done.14), channel_id=1, source_target_pairs={{0,1},{1,0},{2,3},{3,2},{4,5},{5,4},{6,7},{7,6},{8,9},{9,8},{10,11... | collective-permute-start | bytes 1493000 | tf_op jit(solution)/shard_map/ppermute | solution.py:749
  563.4 13.4 %collective-permute-start.57 = (bf16[208,640]{1,0:T(8,128)(2,1)S(1)}, bf16[208,640]{1,0:T(8,128)(2,1)S(1)}, u32[]{:S(2)}, u32[]{:S(2)}) collective-permute-start(bf16[208,640]{1,0:T(8,128)(2,1)S(1)} %collective-permute-done.56), channel_id=1, source_target_pairs={{0,1},{1,0},{2,3},{3,2},{4,5},{5,4},{6,7},{7,6},{8,9},{9,8},{10,11... | collective-permute-start | bytes 798728 | tf_op jit(solution)/shard_map/ppermute | solution.py:749
  (73 other events, 460.5 us)
Sparse Core Ops, SparseCore 0:
  44.3 44.9 all-gather.3
  90.9 43.9 all-gather.5
  137.1 75.1 all-gather.7
  372.6 40.9 reduce-scatter.9
  428.2 41.7 reduce-scatter.5
  477.7 40.3 reduce-scatter.7
